TPU v7x, 128 devices: a whole 4x4x4 slice. The times are simulated.
128 devices in a mesh: step: 32 (over y, x, core), seq: 4 (over z).
Axes of the slice: x: 4, y: 4, z: 4, core: 2. Of those that a mesh axis runs over, the one named last changes fastest.
Arguments:
- states: bfloat16 [32, 1024, 1536], P('step', 'seq'), may hold values from -6 to 6
- step_times: int32 [32, 2], P('step'), may hold values from 0 to 999, as said below
- positions: int32 [1024], P('seq'), may hold values from 0 to 1023, each once
- w_qkv: bfloat16 [1536, 4608], replicated, may hold values from -1 to 1
- qk_gain: float32 [2, 1536], replicated, may hold values from 0.2 to 6
- w_out: bfloat16 [1536, 1536], replicated, may hold values from -0.15625 to 0.15625
- time_weight: bfloat16 [256, 4608], replicated, may hold values from -0.375 to 0.375
Outputs:
- drift_sum: float32 [32, 1024, 1536], P('step', 'seq')
Inputs may be any that keep to these rules, and one draw needn't show every extreme that they name: `step_times`: column 0 of row k is the timestep index of step k and column 1 that of step k + 1, equal to column 0 of row k + 1; indices fall strictly along the steps and row 0 starts at 999.
All inputs are finite; a program needn't handle non-finite values.
Results may differ from a plain program's by a relative error of at most 0.004.
Values may be sent and summed in bfloat16 or wider, within the bound.
No kernel may reach another device: no remote copies, remote signals or barrier semaphores. Data moves between devices by JAX's collectives and lax.ppermute only.
A program may use at most 192 MiB of HBM per device.

v0:
```python
import math

import jax
import jax.numpy as jnp
from jax import lax
from jax.sharding import PartitionSpec as P

D = 1536
HEAD = 128


epsilon = 1e-06


def entering(shard, axis, combine, identity):
    size, mine = (lax.axis_size(axis), lax.axis_index(axis))
    everything = lax.all_gather(shard, axis)
    start = jnp.broadcast_to(jnp.asarray(identity, shard.dtype), shard.shape)

    def turn(k, before):
        reached = k < mine
        new = combine(before, everything[k])
        return jnp.where(reached, new, before)

    return lax.fori_loop(0, size, turn, start)


def rms_norm(entries):
    return entries * lax.rsqrt(jnp.mean(entries * entries, axis=-1, keepdims=True) + epsilon)


def modulation(step_times, time_weight):
    half_width = time_weight.shape[0] // 2
    steps_f = step_times[:, 0].astype(jnp.float32)
    frequency = jnp.exp(-math.log(10000.0) * jnp.arange(half_width, dtype=jnp.float32) / half_width)
    angles = steps_f[:, None] * frequency[None, :]
    embedded = jnp.concatenate([jnp.cos(angles), jnp.sin(angles)], axis=1)
    return jnp.dot(embedded, time_weight.astype(jnp.float32), precision=lax.Precision.HIGHEST)


def rotate(entries, positions):
    half_width = entries.shape[-1] // 2
    inverse = jnp.exp(-math.log(10000.0) * jnp.arange(half_width, dtype=jnp.float32) / half_width)
    angles = positions.astype(jnp.float32)[:, None] * inverse[None, :]
    cosine = jnp.cos(angles)[:, None, :]
    sine_part = jnp.sin(angles)[:, None, :]
    low_half = entries[..., :half_width]
    high_half = entries[..., half_width:]
    return jnp.concatenate(
        [low_half * cosine - high_half * sine_part, low_half * sine_part + high_half * cosine],
        axis=-1,
    )


def prepare(own_state, positions, shift_mod, scale_mod, w_qkv, qk_gain):
    model_width = own_state.shape[1]
    head_shape = (own_state.shape[0], model_width // HEAD, HEAD)
    normed = (rms_norm(own_state.astype(jnp.float32)) * (1.0 + scale_mod) + shift_mod).astype(
        jnp.bfloat16
    )
    projected_qkv = jnp.dot(normed, w_qkv, preferred_element_type=jnp.float32)
    queries = rms_norm(projected_qkv[:, :model_width]) * qk_gain[0]
    key_rows = rms_norm(projected_qkv[:, model_width : 2 * model_width]) * qk_gain[1]
    values = projected_qkv[:, 2 * model_width :].reshape(head_shape).astype(jnp.bfloat16)
    queries = rotate(queries.reshape(head_shape), positions).astype(jnp.bfloat16)
    key_rows = rotate(key_rows.reshape(head_shape), positions).astype(jnp.bfloat16)
    return (queries, key_rows, values)


def attend(queries, key_rows, values):
    score_scale = HEAD ** (-0.5)

    def one_head(operands):
        q_head, k_head, v_head = operands
        scores = jnp.dot(q_head, k_head.T, preferred_element_type=jnp.float32) * score_scale
        row_max = jnp.max(scores, axis=-1, keepdims=True)
        exp_scores = jnp.exp(scores - row_max)
        row_total = jnp.sum(exp_scores, axis=-1, keepdims=True)
        weighted = (
            jnp.dot(exp_scores.astype(jnp.bfloat16), v_head, preferred_element_type=jnp.float32)
            / row_total
        )
        return weighted.astype(jnp.bfloat16)

    stacked = lax.map(
        one_head,
        (queries.transpose(1, 0, 2), key_rows.transpose(1, 0, 2), values.transpose(1, 0, 2)),
    )
    return stacked.transpose(1, 0, 2)


def add_terms(first_term, second_term):
    return first_term + second_term


def on_device(states, step_times, positions, w_qkv, qk_gain, w_out, time_weight):
    modulated = modulation(step_times, time_weight)[0]
    shift_mod = modulated[:D]
    scale_mod = modulated[D : 2 * D]
    gate_mod = modulated[2 * D :]
    own_state = states[0]
    queries, key_rows, values = prepare(own_state, positions, shift_mod, scale_mod, w_qkv, qk_gain)
    all_keys, all_values = (
        lax.all_gather(key_rows, "seq", axis=0, tiled=True),
        lax.all_gather(values, "seq", axis=0, tiled=True),
    )
    attended = attend(queries, all_keys, all_values)
    attended = attended.reshape(own_state.shape[0], D)
    projected = jnp.dot(attended, w_out, preferred_element_type=jnp.float32)
    velocity = own_state.astype(jnp.float32) + gate_mod * projected
    step_size = (step_times[0, 1] - step_times[0, 0]).astype(jnp.float32) / 1000.0
    increment = step_size * velocity
    zero_term = jnp.zeros_like(increment)
    earlier = entering(increment, "step", add_terms, zero_term)
    result = earlier + increment
    return result[None]


def solution(mesh):
    placed = (P("step", "seq", None), P("step", None), P("seq"), P(), P(), P(), P())
    return jax.shard_map(
        on_device, mesh=mesh, in_specs=placed, out_specs=P("step", "seq", None), check_vma=False
    )
```

profile of v0, /device:TPU:1, one launch (start us, length us, event | category | flops | bytes accessed | tf_op | source)
XLA Modules:
  0.0 437.5 jit_solution(2464394026308449454)
XLA Ops:
  9.9 7.3 %fusion.20 = f32[256,4608]{1,0:T(8,128)S(1)} fusion(bf16[1536,4608]{1,0:T(8,128)(2,1)} %param.14, bf16[1,256,1536]{2,1,0:T(8,128)(2,1)S(1)} %copy-done.3, f32[1536]{0:T(1024)S(1)} %get-tuple-element.166, f32[1536]{0:T(1024)S(1)} %get-tuple-element.167, f32[256]{0:T(256)S(1)} %add_rsqrt_fusion.2), kind=kOutput, calls=%fused_computation.34 | convolution fusion | flops 3625844736 | bytes 19674112 | tf_op jit(solution)/shard_map/dot_general | solution.py:61
  33.4 41.0 %all-gather.5.cloned.1.call-done = bf16[1024,12,128]{0,2,1:T(8,128)(2,1)} async-done(((bf16[256,12,128]{0,2,1:T(8,128)(2,1)}), bf16[1024,12,128]{0,2,1:T(8,128)(2,1)}) %all-gather.5.cloned.1.call-update) | async-done | bytes 3145744 | tf_op jit(solution)/shard_map/all_gather | solution.py:104
  74.5 45.9 %all-gather.7.cloned.1.call-done = bf16[1024,12,128]{0,2,1:T(8,128)(2,1)} async-done(((bf16[256,12,128]{0,2,1:T(8,128)(2,1)}), bf16[1024,12,128]{0,2,1:T(8,128)(2,1)}) %all-gather.7.cloned.1.call-update) | async-done | bytes 3145744 | tf_op jit(solution)/shard_map/all_gather | solution.py:105
  120.4 37.9 %while.24 = (s32[]{:T(128)}, bf16[12,256,128]{1,2,0:T(8,128)(2,1)S(1)}, bf16[12,256,128]{1,2,0:T(8,128)(2,1)}, bf16[12,1024,128]{1,2,0:T(8,128)(2,1)}, bf16[12,1024,128]{1,2,0:T(8,128)(2,1)}, /*index=5*/s32[]{:T(128)}) while((s32[]{:T(128)}, bf16[12,256,128]{1,2,0:T(8,128)(2,1)S(1)}, bf16[12,256,128]{1,2,0:T(8,128)(2,1)}, ...), condition=%wide.region_6.7_spmd, body=%wide.region_3.6_spmd.sunk | while | flops 135855616 | bytes 4069961 | solution.py:85
  158.3 4.9 %fusion.15 = f32[256,1536]{1,0:T(8,128)} fusion(bf16[256,1536]{0,1:T(8,128)(2,1)S(1)} %bitcast.64, bf16[1536,1536]{1,0:T(8,128)(2,1)} %param.16, bf16[1,256,1536]{2,1,0:T(8,128)(2,1)S(1)} %copy-done.3, f32[1536]{0:T(1024)S(1)} %get-tuple-element.165, f32[]{:T(128)} %bitcast.4), kind=kOutput, calls=%fused_computation.20 | convolution fusion | flops 1209532416 | bytes 7870468 | tf_op jit(solution)/shard_map/dot_general | solution.py:109
  163.2 159.5 %all-gather.9.cloned.1.call-done = f32[8192,1536]{1,0:T(8,128)} async-done(((f32[256,1536]{1,0:T(8,128)}), f32[8192,1536]{1,0:T(8,128)}) %all-gather.9.cloned.1.call-update) | async-done | bytes 50331664 | tf_op jit(solution)/shard_map/all_gather | solution.py:17
  322.8 104.9 %while.25 = (s32[]{:T(128)}, f32[256,1536]{1,0:T(8,128)}, s32[]{:T(128)}, f32[32,256,1536]{2,1,0:T(8,128)}, s32[]{:T(128)}, /*index=5*/s32[]{:T(128)}) while((s32[]{:T(128)}, f32[256,1536]{1,0:T(8,128)}, s32[]{:T(128)}, f32[32,256,1536]{2,1,0:T(8,128)}, s32[]{:T(128)}, /*index=5*/s32[]{:T(128)}) %tuple.73), condition=%wide.region_8.9_spmd.clone, body=%wide.region_7.8_spmd.clone.sunk | while | flops 1179652 | bytes 4718685 | solution.py:25
  325.6 3.3 add_select_fusion.2
  328.9 3.3 add_select_fusion.2
  332.2 3.3 add_select_fusion.2
  335.5 3.3 add_select_fusion.2
  338.7 3.3 add_select_fusion.2
  342.0 3.3 add_select_fusion.2
  345.3 3.3 add_select_fusion.2
  348.6 3.3 add_select_fusion.2
  351.9 3.3 add_select_fusion.2
  355.2 3.3 add_select_fusion.2
  361.8 3.3 add_select_fusion.2
  365.1 3.3 add_select_fusion.2
  368.4 3.3 add_select_fusion.2
  371.7 3.3 add_select_fusion.2
  375.0 3.3 add_select_fusion.2
  378.3 3.3 add_select_fusion.2
  427.6 3.4 add_bitcast_fusion
  (117 shorter events, 107.3 us)
Async XLA Ops:
  6.5 2.1 copy-start
  6.5 3.2 copy-start.3
  6.5 67.9 %all-gather.5.cloned.1.call-start = ((), (), s32[]{:S(2)}) async-start(), calls=%async_computation | async-start | bytes 3932160 | tf_op jit(solution)/shard_map/all_gather | solution.py:104
  17.2 3.2 copy-start.2
  17.2 0.7 copy-start.4
  22.3 3.1 copy-start.5
  28.5 91.9 %all-gather.7.cloned.1.call-start = ((), (), s32[]{:S(2)}) async-start(), calls=%async_computation.1 | async-start | bytes 3932160 | tf_op jit(solution)/shard_map/all_gather | solution.py:105
  31.2 291.5 %all-gather.9.cloned.1.call-start = ((), (), s32[]{:S(2)}) async-start(), calls=%async_computation.2 | async-start | bytes 51904512 | tf_op jit(solution)/shard_map/all_gather | solution.py:17
  427.6 3.4 copy-start.1
Sparse Core Ops, SparseCore 0:
  28.7 45.7 all-gather.4
  76.1 44.2 all-gather.6
  163.3 159.3 all-gather.8
where the time goes:
time: 439 us; the launch traced here: 438 us
  waiting for transfers between devices  247 us (56%)
  other arithmetic  119 us (27%)
  matrix products  45.5 us (10%)
  between operations  15.1 us (3%)
  local copies, waits for them, and re-layouts  10.8 us (2%)
    all_gather x1, waiting for transfers between devices, entering(): everything = lax.all_gather(shard, axis)  160 us
    select_n x32, other arithmetic, turn(): return jnp.where(reached, new, before)  105 us
    all_gather x1, waiting for transfers between devices, on_device(): lax.all_gather(values, 'seq', axis=0, tiled=True)  45.9 us
    all_gather x1, waiting for transfers between devices, on_device(): lax.all_gather(key_rows, 'seq', axis=0, tiled=True)  41 us
    dot_general x12, matrix products, one_head(): jnp.dot(q_head, k_head.T, preferred_element_type=jnp.float32) * score_scale  16.7 us
    dot_general x12, matrix products, one_head(): jnp.dot(exp_scores.astype(jnp.bfloat16), v_head, preferred_element_type=j...  15.7 us
  transfers between devices with their start and end apart: 3, of which 3 were waited for; matrix products, arithmetic and copies ran while one was open for 1% of the time, Pallas kernels for 0%

commit v1 on v0

v1 whole, which is shorter than its diff:
```python
import functools
import math

import jax
import jax.numpy as jnp
from jax import lax
from jax.experimental import pallas as pl
from jax.experimental.pallas import tpu as pltpu
from jax.sharding import PartitionSpec as P

D = 1536
HEAD = 128
HEADS = D // HEAD
TILE = 512
TILES = D // TILE
epsilon = 1e-06
EXP_SCALE = HEAD ** (-0.5) * math.log2(math.e)
f32, bf16 = jnp.float32, jnp.bfloat16


def modulation(step_times, time_weight):
    half_width = time_weight.shape[0] // 2
    steps_f = step_times[:, 0].astype(f32)
    frequency = jnp.exp(-math.log(10000.0) * jnp.arange(half_width, dtype=f32) / half_width)
    angles = steps_f[:, None] * frequency[None, :]
    embedded = jnp.concatenate([jnp.cos(angles), jnp.sin(angles)], axis=1)
    return jnp.dot(embedded, time_weight.astype(f32), precision=lax.Precision.HIGHEST)


def rope_tables(positions):
    half_width = HEAD // 2
    inverse = jnp.exp(-math.log(10000.0) * jnp.arange(half_width, dtype=f32) / half_width)
    angles = positions.astype(f32)[:, None] * inverse[None, :]
    cosine, sine = jnp.cos(angles), jnp.sin(angles)
    return jnp.concatenate([cosine, cosine], axis=1), jnp.concatenate([-sine, sine], axis=1)


def norm_rope(proj, gain, cos, sin, out_ref):
    rows = proj.shape[0]
    total = jnp.zeros((rows, HEAD), f32)
    for h in range(HEADS):
        p = proj[:, h * HEAD : (h + 1) * HEAD]
        total = total + p * p
    inv = lax.rsqrt(jnp.sum(total, axis=1, keepdims=True) * (1.0 / D) + epsilon)
    cos, sin = cos[...], sin[...]
    for h in range(HEADS):
        at = slice(h * HEAD, (h + 1) * HEAD)
        y = proj[:, at] * inv * gain[:, at]
        out_ref[:, at] = (y * cos + pltpu.roll(y, HEAD // 2, 1) * sin).astype(bf16)


def project_kernel(n_x, with_q, *refs):
    x_refs, refs = refs[:n_x], refs[n_x:]
    shift, scale, gains, cos, sin, w = refs[:6]
    outs, (normed, proj) = refs[6:-2], refs[-2:]
    i = pl.program_id(0)

    @pl.when(i == 0)
    def _():
        at = 0
        for x_ref in x_refs:
            x = x_ref[...].astype(f32)
            inv = lax.rsqrt(jnp.sum(x * x, axis=1, keepdims=True) * (1.0 / D) + epsilon)
            normed[pl.ds(at, x.shape[0]), :] = (x * inv * (1.0 + scale[...]) + shift[...]).astype(bf16)
            at += x.shape[0]

    acc = jnp.dot(normed[...], w[...], preferred_element_type=f32)
    groups = ["q", "k", "v"] if with_q else ["k", "v"]
    for g, name in enumerate(groups):
        for t in range(TILES):

            @pl.when(i == g * TILES + t)
            def _(g=g, name=name, t=t):
                if name == "v":
                    outs[g][:, t * TILE : (t + 1) * TILE] = acc.astype(bf16)
                else:
                    proj[:, t * TILE : (t + 1) * TILE] = acc
                    if t == TILES - 1:
                        row = 0 if name == "q" else 1
                        norm_rope(proj, gains[row : row + 1, :], cos, sin, outs[g])


def project(xs, shift, scale, gains, cos, sin, w_qkv, with_q):
    rows = sum(x.shape[0] for x in xs)
    groups = 3 if with_q else 2
    first = 0 if with_q else TILES
    whole = lambda a: pl.BlockSpec(a.shape, lambda i: (0, 0))
    small = (shift, scale, gains, cos, sin)
    return pl.pallas_call(
        functools.partial(project_kernel, len(xs), with_q),
        grid=(groups * TILES,),
        in_specs=[whole(x) for x in xs]
        + [whole(a) for a in small]
        + [pl.BlockSpec((D, TILE), lambda i: (0, i + first))],
        out_specs=[pl.BlockSpec((rows, D), lambda i: (0, 0))] * groups,
        out_shape=[jax.ShapeDtypeStruct((rows, D), bf16)] * groups,
        scratch_shapes=[pltpu.VMEM((rows, D), bf16), pltpu.VMEM((rows, D), f32)],
        cost_estimate=pl.CostEstimate(
            flops=2 * rows * D * D * groups, bytes_accessed=2 * D * D * groups, transcendentals=0
        ),
        compiler_params=pltpu.CompilerParams(vmem_limit_bytes=28 << 20),
    )(*xs, *small, w_qkv)


def attend_kernel(n_kv, q_ref, *refs):
    kv, (m_ref, l_ref, acc_ref) = refs[: 2 * n_kv], refs[2 * n_kv :]
    rows = q_ref.shape[0]
    for h in range(HEADS):
        at = slice(h * HEAD, (h + 1) * HEAD)
        q = q_ref[:, at]
        scores = [
            lax.dot_general(q, kv[2 * j][:, at], (((1,), (1,)), ((), ())), preferred_element_type=f32)
            for j in range(n_kv)
        ]
        top = scores[0]
        for s in scores[1:]:
            top = jnp.maximum(top, s)
        m = jnp.max(top, axis=1, keepdims=True) * EXP_SCALE
        total = jnp.zeros((rows, 1), f32)
        acc = jnp.zeros((rows, HEAD), f32)
        for j in range(n_kv):
            p = jnp.exp2(scores[j] * EXP_SCALE - m)
            total = total + jnp.sum(p, axis=1, keepdims=True)
            acc = acc + jnp.dot(p.astype(bf16), kv[2 * j + 1][:, at], preferred_element_type=f32)
        m_ref[:, h : h + 1] = m
        l_ref[:, h : h + 1] = total
        acc_ref[:, at] = acc


def attend(q, kvs):
    rows = q.shape[0]
    keys = sum(k.shape[0] for k, _ in kvs)
    flat = [a for pair in kvs for a in pair]
    vm = pl.BlockSpec(memory_space=pltpu.VMEM)
    return pl.pallas_call(
        functools.partial(attend_kernel, len(kvs)),
        in_specs=[vm] * (1 + len(flat)),
        out_specs=[vm] * 3,
        out_shape=[
            jax.ShapeDtypeStruct((rows, HEAD), f32),
            jax.ShapeDtypeStruct((rows, HEAD), f32),
            jax.ShapeDtypeStruct((rows, D), f32),
        ],
        cost_estimate=pl.CostEstimate(
            flops=8 * rows * D * keys, bytes_accessed=4 * rows * D * 2, transcendentals=rows * keys * HEADS
        ),
        compiler_params=pltpu.CompilerParams(vmem_limit_bytes=28 << 20),
    )(q, *flat)


def finish_kernel(n_kv, h_ref, q_ref, *refs):
    kv, refs = refs[: 2 * n_kv], refs[2 * n_kv :]
    m_ref, l_ref, acc_ref, x_ref, gate_ref, w_hbm, out_ref, w_ref, attended, sem = refs
    load = pltpu.make_async_copy(w_hbm, w_ref, sem)
    load.start()
    for h in range(HEADS):
        at = slice(h * HEAD, (h + 1) * HEAD)
        q = q_ref[:, at]
        scores = [
            lax.dot_general(q, kv[2 * j][:, at], (((1,), (1,)), ((), ())), preferred_element_type=f32)
            for j in range(n_kv)
        ]
        top = scores[0]
        for s in scores[1:]:
            top = jnp.maximum(top, s)
        before = m_ref[:, h : h + 1]
        m = jnp.maximum(jnp.max(top, axis=1, keepdims=True) * EXP_SCALE, before)
        fade = jnp.exp2(before - m)
        total = l_ref[:, h : h + 1] * fade
        acc = acc_ref[:, at] * fade
        for j in range(n_kv):
            p = jnp.exp2(scores[j] * EXP_SCALE - m)
            total = total + jnp.sum(p, axis=1, keepdims=True)
            acc = acc + jnp.dot(p.astype(bf16), kv[2 * j + 1][:, at], preferred_element_type=f32)
        attended[:, at] = (acc / total).astype(bf16)
    load.wait()
    size = h_ref[0, 0]
    for t in range(TILES):
        at = slice(t * TILE, (t + 1) * TILE)
        proj = jnp.dot(attended[...], w_ref[:, at], preferred_element_type=f32)
        out_ref[:, at] = size * (x_ref[:, at].astype(f32) + gate_ref[:, at] * proj)


def finish(step_size, q, kvs, state, x, gate, w_out):
    rows = q.shape[0]
    keys = sum(k.shape[0] for k, _ in kvs)
    flat = [a for pair in kvs for a in pair]
    vm = pl.BlockSpec(memory_space=pltpu.VMEM)
    return pl.pallas_call(
        functools.partial(finish_kernel, len(kvs)),
        in_specs=[pl.BlockSpec(memory_space=pltpu.SMEM)]
        + [vm] * (1 + len(flat) + 3 + 2)
        + [pl.BlockSpec(memory_space=pl.ANY)],
        out_specs=vm,
        out_shape=jax.ShapeDtypeStruct((rows, D), f32),
        scratch_shapes=[pltpu.VMEM((D, D), bf16), pltpu.VMEM((rows, D), bf16), pltpu.SemaphoreType.DMA],
        cost_estimate=pl.CostEstimate(
            flops=8 * rows * D * keys + 2 * rows * D * D,
            bytes_accessed=2 * D * D,
            transcendentals=rows * keys * HEADS,
        ),
        compiler_params=pltpu.CompilerParams(vmem_limit_bytes=28 << 20),
    )(step_size, q, *flat, *state, x, gate, w_out)


def gather_states(x, n):
    half = x.shape[0] // 2
    right = [(i, (i + 1) % n) for i in range(n)]
    left = [(i, (i - 1) % n) for i in range(n)]
    first, second = x[:half], x[half:]
    to_right = lambda v: lax.ppermute(v, "seq", right)
    to_left = lambda v: lax.ppermute(v, "seq", left)
    r_first, l_second = to_right(first), to_left(second)
    r_second, l_first = to_right(second), to_left(first)
    return (r_first, l_second), (r_second, l_first), (to_right(r_first), to_left(l_second))


def scan_steps(inc):
    rows = inc.shape[0]
    half, part = rows // 2, rows // 8
    step = lax.axis_index("step")
    c, xx, yy = step % 2, (step // 2) % 4, step // 8
    pair = [(i, i ^ 1) for i in range(32)]

    def along_x(k):
        return [((y * 4 + x) * 2 + c, (y * 4 + (x + k) % 4) * 2 + c) for y in range(4) for x in range(4) for c in range(2)]

    def along_y(k):
        return [((y * 4 + x) * 2 + c, ((y + k) % 4 * 4 + x) * 2 + c) for y in range(4) for x in range(4) for c in range(2)]

    sent = lax.dynamic_slice_in_dim(inc, (1 - c) * half, half).astype(bf16)
    got = lax.ppermute(sent, "step", pair).astype(f32)
    mine = lax.dynamic_slice_in_dim(inc, c * half, half)
    both = (mine + got).reshape(4, part, D)
    narrow = both.astype(bf16)
    src = [lax.dynamic_index_in_dim(both, xx, 0, keepdims=False)]
    for k in (1, 2, 3):
        piece = lax.dynamic_index_in_dim(narrow, (xx + k) % 4, 0, keepdims=False)
        src.append(lax.ppermute(piece, "step", along_x(k)).astype(f32))
    row = src[0] + src[1] + src[2] + src[3]
    row_b = row.astype(bf16)
    rows_y = [lax.ppermute(row_b, "step", along_y(k)) for k in (1, 2, 3)]
    above = sum(jnp.where((yy - k) % 4 < yy, rows_y[k - 1].astype(f32), 0.0) for k in (1, 2, 3))
    before = []
    for k in range(4):
        target = (xx + k) % 4
        before.append(above + sum(jnp.where((xx - j) % 4 < target, src[j], 0.0) for j in range(4)))
    back = [before[0]] + [lax.ppermute(before[k].astype(bf16), "step", along_x(k)).astype(f32) for k in (1, 2, 3)]
    entering = jnp.zeros((4, part, D), f32)
    for k in range(4):
        entering = lax.dynamic_update_index_in_dim(entering, back[k], (xx - k) % 4, 0)
    entering = entering.reshape(half, D)
    given = jnp.where(c == 0, entering + mine, entering)
    other = lax.ppermute(given.astype(bf16), "step", pair).astype(f32)
    own = jnp.where(c == 0, given, entering + got + mine)
    rest = other + lax.dynamic_slice_in_dim(inc, (1 - c) * half, half)
    return jnp.concatenate([jnp.where(c == 0, own, rest), jnp.where(c == 0, rest, own)])


def on_device(states, step_times, positions, w_qkv, qk_gain, w_out, time_weight):
    n = lax.axis_size("seq")
    z = lax.axis_index("seq")
    x = states[0]
    half = x.shape[0] // 2
    chunks = gather_states(x, n)
    all_positions = lax.all_gather(positions, "seq", axis=0, tiled=True)

    modulated = modulation(step_times, time_weight)
    shift, scale, gate = modulated[:, :D], modulated[:, D : 2 * D], modulated[:, 2 * D :]

    q, k, v = project([x], shift, scale, qk_gain, *rope_tables(positions), w_qkv, True)
    kvs = [(k, v)]
    sources = [((z - 1) % n, (z + 1) % n), ((z - 1) % n, (z + 1) % n), ((z + 2) % n, (z + 2) % n)]
    halves = [(0, 1), (1, 0), (0, 1)]
    for chunk, source, which in zip(chunks, sources, halves):
        where = jnp.concatenate(
            [lax.dynamic_slice_in_dim(all_positions, (2 * s + w) * half, half) for s, w in zip(source, which)]
        )
        kvs.append(tuple(project(chunk, shift, scale, qk_gain, *rope_tables(where), w_qkv, False)))
    state = attend(q, kvs[:3])
    step_size = (step_times[:, 1:] - step_times[:, :1]).astype(f32) / 1000.0
    inc = finish(step_size, q, kvs[3:], state, x, gate, w_out)
    return scan_steps(inc)[None]


def solution(mesh):
    placed = (P("step", "seq", None), P("step", None), P("seq"), P(), P(), P(), P())
    return jax.shard_map(
        on_device, mesh=mesh, in_specs=placed, out_specs=P("step", "seq", None), check_vma=False
    )
```

time: 439 us -> 142 us (0.32)
  waiting for transfers between devices: 247 us -> 12.3 us
  other arithmetic: 119 us -> 12.8 us
  matrix products: 45.5 us -> 1.01 us
  Pallas kernels: 0 us -> 40 us
  starting transfers between devices: 0.09 us -> 30 us
  blocking collectives: 0 us -> 18.4 us
  local copies, waits for them, and re-layouts: 10.8 us -> 24.7 us
  between operations: 15.1 us -> 2.53 us
    all_gather x3 -> x0, waiting for transfers between devices: 247 us -> none  [the longest x1 160 us: entering(): everything = lax.all_gather(shard, axis)]
    select_n x32 -> x1, other arithmetic: 105 us -> 0.28 us  [scan_steps(): jnp.where(c == 0, own, rest)]
    dot_general x27 -> x1, matrix products: 45.5 us -> 1.01 us  [modulation(): jnp.dot(embedded, time_weight.astype(f32), precision=lax.Precision.HIGHEST)]
    pallas_call x0 -> x6, Pallas kernels: none -> 40 us  [the longest x4 26.9 us: project(): pl.pallas_call(functools.partial(project_kernel, len(xs), with_q), grid=(...]
    ppermute x0 -> x17, starting transfers between devices: none -> 30 us  [the longest x3 9.01 us: gather_states(): to_left = lambda v: lax.ppermute(v, 'seq', left)]
    unnamed x12 -> x70, local copies, waits for them, and re-layouts: 0.44 us -> 20.3 us
    all_gather x0 -> x1, blocking collectives: none -> 18.4 us  [on_device(): all_positions = lax.all_gather(positions, 'seq', axis=0, tiled=True)]
    ppermute x0 -> x17, waiting for transfers between devices: none -> 12.3 us  [the longest x3 3.88 us: scan_steps(): rows_y = [lax.ppermute(row_b, 'step', along_y(k)) for k in (1, 2, 3)]]
  transfers between devices with their start and end apart: 3 -> 17, of which waited for: 3 -> 7; matrix products, arithmetic and copies ran while one was open for 1% -> 7% of each run, Pallas kernels for 0% -> 19%
where the time goes in v1:
time: 142 us
  Pallas kernels  40 us (28%)
  starting transfers between devices  30 us (21%)
  local copies, waits for them, and re-layouts  24.7 us (17%)
  blocking collectives  18.4 us (13%)
  other arithmetic  12.8 us (9%)
  waiting for transfers between devices  12.3 us (9%)
  between operations  2.53 us (2%)
    pallas_call x4, Pallas kernels, project(): pl.pallas_call(functools.partial(project_kernel, len(xs), with_q), grid=(...  26.9 us
    unnamed x70, local copies, waits for them, and re-layouts  20.3 us
    all_gather x1, blocking collectives, on_device(): all_positions = lax.all_gather(positions, 'seq', axis=0, tiled=True)  18.4 us
    ppermute x3, starting transfers between devices, gather_states(): to_left = lambda v: lax.ppermute(v, 'seq', left)  9.01 us
    pallas_call x1, Pallas kernels, finish(): pl.pallas_call(functools.partial(finish_kernel, len(kvs)), in_specs=[pl.B...  7.94 us
    pallas_call x1, Pallas kernels, attend(): pl.pallas_call(functools.partial(attend_kernel, len(kvs)), in_specs=[vm]...  5.1 us
    ppermute x3, starting transfers between devices, scan_steps(): rows_y = [lax.ppermute(row_b, 'step', along_y(k)) for k in (1, 2, 3)]  4.98 us
    ppermute x3, starting transfers between devices, scan_steps(): src.append(lax.ppermute(piece, 'step', along_x(k)).astype(f32))  4.82 us
  transfers between devices with their start and end apart: 17, of which 7 were waited for; matrix products, arithmetic and copies ran while one was open for 7% of the time, Pallas kernels for 19%

profile of v1, /device:TPU:1, one launch (start us, length us, event | category | flops | bytes accessed | tf_op | source)
XLA Modules:
  0.0 141.6 jit_solution(2235465612548733291)
XLA Ops:
  0.0 2.3 %slice_bitcast_fusion = (bf16[128,1536]{1,0:T(8,128)(2,1)}, bf16[128,1536]{1,0:T(8,128)(2,1)}) fusion(bf16[1,256,1536]{2,1,0:T(8,128)(2,1)} %param.7), kind=kLoop, calls=%fused_computation.26 | loop fusion | bytes 1572864 | tf_op jit(solution)/shard_map/slice | solution.py:210
  2.3 4.6 %collective-permute-start.2 = (bf16[128,1536]{1,0:T(8,128)(2,1)}, bf16[128,1536]{1,0:T(8,128)(2,1)}, u32[]{:S(2)}, u32[]{:S(2)}) collective-permute-start(bf16[128,1536]{1,0:T(8,128)(2,1)} %get-tuple-element.33), channel_id=1, source_target_pairs={{0,3},{1,0},{2,1},{3,2},{4,7},{5,4},{6,5},{7,6},{8,11},{9,8},{10,9... | collective-permute-start | bytes 1179656 | tf_op jit(solution)/shard_map/ppermute | solution.py:212
  6.9 2.7 %collective-permute-start.5 = (bf16[128,1536]{1,0:T(8,128)(2,1)}, bf16[128,1536]{1,0:T(8,128)(2,1)}, u32[]{:S(2)}, u32[]{:S(2)}) collective-permute-start(bf16[128,1536]{1,0:T(8,128)(2,1)} %get-tuple-element.34), channel_id=1, source_target_pairs={{0,3},{1,0},{2,1},{3,2},{4,7},{5,4},{6,5},{7,6},{8,11},{9,8},{10,9... | collective-permute-start | bytes 1179656 | tf_op jit(solution)/shard_map/ppermute | solution.py:212
  9.6 18.4 %all-gather = s32[4,1,256]{2,1,0:T(1,128)S(1)} all-gather(s32[1,1,256]{2,1,0:T(1,128)S(1)} %bitcast.68), channel_id=1, replica_groups=mesh['step'=32,'seq'=4] {'seq'}, dimensions={0}, use_global_device_ids=true | all-gather | bytes 5120 | tf_op jit(solution)/shard_map/all_gather | solution.py:266
  28.1 2.5 %fusion.29 = (f32[256,64]{1,0:T(8,128)S(1)}, f32[256,64]{1,0:T(8,128)S(1)}, f32[256,64]{1,0:T(8,128)S(1)}, f32[256,64]{1,0:T(8,128)S(1)}, f32[256,64]{1,0:T(8,12...) fusion(f32[64]{0:T(128)S(1)} %multiply_exponential_fusion, ...), kind=kLoop, calls=%fused_computation.78 | loop fusion | flops 131072 | bytes 790784 | tf_op jit(solution)/shard_map/neg | solution.py:35
  35.4 5.0 %copy-done.1 = bf16[1536,4608]{1,0:T(8,128)(2,1)S(1)} copy-done((bf16[1536,4608]{1,0:T(8,128)(2,1)S(1)}, bf16[1536,4608]{1,0:T(8,128)(2,1)}, u32[]{:S(2)}) %copy-start.1) | copy-done | bytes 14155800
  40.4 8.3 %shard_map.73 = (bf16[256,1536]{1,0:T(8,128)(2,1)S(1)}, bf16[256,1536]{1,0:T(8,128)(2,1)S(1)}, bf16[256,1536]{1,0:T(8,128)(2,1)S(1)}) custom-call(bf16[256,1536]{1,0:T(8,128)(2,1)S(1)} %bitcast.59, f32[1,1536]{1,0:T(1,128)S(1)} %get-tuple-element.40.refs_1_.refs_2_, f32[1,1536]{1,0:T(1,128)S(1)} %get-tuple-element.39.refs_2_.refs_3_, ...), custom_call_target="tpu_custom_call" | custom-call | flops 3623878656 | bytes 14155776 | tf_op jit(solution)/shard_map/pallas_call | solution.py:89
  55.3 1.7 %collective-permute-start.3 = (bf16[128,1536]{1,0:T(8,128)(2,1)}, bf16[128,1536]{1,0:T(8,128)(2,1)S(1)}, u32[]{:S(2)}, u32[]{:S(2)}) collective-permute-start(bf16[128,1536]{1,0:T(8,128)(2,1)} %collective-permute-done.2.refs_1_), channel_id=1, source_target_pairs={{0,3},{1,0},{2,1},{3,2},{4,7},{5,4},{6,5},{7,6},{8,11},{9,8},{10,9... | collective-permute-start | bytes 1179656 | tf_op jit(solution)/shard_map/ppermute | solution.py:212
  57.0 5.0 %copy-done.2 = bf16[1536,4608]{1,0:T(8,128)(2,1)S(1)} copy-done((bf16[1536,4608]{1,0:T(8,128)(2,1)S(1)}, bf16[1536,4608]{1,0:T(8,128)(2,1)}, u32[]{:S(2)}) %copy-start.2) | copy-done | bytes 14155800
  64.3 6.6 %shard_map.75 = (bf16[256,1536]{1,0:T(8,128)(2,1)S(1)}, bf16[256,1536]{1,0:T(8,128)(2,1)S(1)}) custom-call(bf16[128,1536]{1,0:T(8,128)(2,1)} %collective-permute-done.refs_0_, bf16[128,1536]{1,0:T(8,128)(2,1)} %collective-permute-done.2.refs_1_, f32[1,1536]{1,0:T(1,128)S(1)} %copy-done.15, f32[1,1536]{1,0:T(1,128)S(1)} %copy-done.12, ...), custom_call_target="tpu_custom_call" | custom-call | flops 2415919104 | bytes 9437184 | tf_op jit(solution)/shard_map/pallas_call | solution.py:89
  72.7 6.6 %shard_map.76 = (bf16[256,1536]{1,0:T(8,128)(2,1)S(1)}, bf16[256,1536]{1,0:T(8,128)(2,1)S(1)}) custom-call(bf16[128,1536]{1,0:T(8,128)(2,1)} %collective-permute-done.4.refs_0_, bf16[128,1536]{1,0:T(8,128)(2,1)} %collective-permute-done.5.refs_1_, f32[1,1536]{1,0:T(1,128)S(1)} %copy-done.15, f32[1,1536]{1,0:T(1,128)S(1)} %copy-done.13, ...), custom_call_target="tpu_custom_call" | custom-call | flops 2415919104 | bytes 9437184 | tf_op jit(solution)/shard_map/pallas_call | solution.py:89
  81.6 5.1 %shard_map.77 = (f32[256,128]{1,0:T(8,128)S(1)}, f32[256,128]{1,0:T(8,128)S(1)}, f32[256,1536]{1,0:T(8,128)S(1)}) custom-call(bf16[256,1536]{1,0:T(8,128)(2,1)S(1)} %copy-done.7, bf16[256,1536]{1,0:T(8,128)(2,1)S(1)} %copy-done.18, bf16[256,1536]{1,0:T(8,128)(2,1)S(1)} %copy-done.20, bf16[256,1536]{1,0:T(8,128)(2,1)S(1)} %copy-done.22, ...), custom_call_target="tpu_custom_call" | custom-call | flops 2415919104 | bytes 3145728 | tf_op jit(solution)/shard_map/pallas_call | solution.py:135
  86.8 5.4 %shard_map.74 = (bf16[256,1536]{1,0:T(8,128)(2,1)S(1)}, bf16[256,1536]{1,0:T(8,128)(2,1)S(1)}) custom-call(bf16[128,1536]{1,0:T(8,128)(2,1)S(1)} %collective-permute-done.1.refs_0_, bf16[128,1536]{1,0:T(8,128)(2,1)S(1)} %collective-permute-done.3.refs_1_, f32[1,1536]{1,0:T(1,128)S(1)} %copy-done.15, f32[1,1536]{1,0:T(1,128)S(1)} %copy-done.13, ...), custom_call_target="tpu_custom_call" | custom-call | flops 2415919104 | bytes 9437184 | tf_op jit(solution)/shard_map/pallas_call | solution.py:89
  92.3 7.9 %shard_map.78 = f32[256,1536]{1,0:T(8,128)S(1)} custom-call(f32[1,1]{1,0:T(1,128)S(6)} %div.41.h_ref, bf16[256,1536]{1,0:T(8,128)(2,1)S(1)} %copy-done.7, bf16[256,1536]{1,0:T(8,128)(2,1)S(1)} %get-tuple-element.18.refs_0_, bf16[256,1536]{1,0:T(8,128)(2,1)S(1)} %get-tuple-element.19.refs_1_, f32[256,128]{1,0:T(8,128)S(1)} %get-tuple-element.26.refs_2_, ...), custom_call_target="tpu_custom_call" | custom-call | flops 2013265920 | bytes 4718592 | tf_op jit(solution)/shard_map/pallas_call | solution.py:189
  101.4 2.9 %collective-permute-start.6 = (bf16[128,1536]{1,0:T(8,128)(2,1)S(1)}, bf16[128,1536]{1,0:T(8,128)(2,1)S(1)}, u32[]{:S(2)}, u32[]{:S(2)}) collective-permute-start(bf16[128,1536]{1,0:T(8,128)(2,1)S(1)} %dynamic-slice_convert_fusion), channel_id=1, source_target_pairs={{0,4},{4,0},{8,12},{12,8},{16,20},{20,16},{24,28},{28,24},{32,36},... | collective-permute-start | bytes 1179656 | tf_op jit(solution)/shard_map/ppermute | solution.py:232
  104.3 1.3 collective-permute-done.6
  109.0 2.5 %collective-permute-start.8 = (bf16[32,1536]{1,0:T(8,128)(2,1)}, bf16[32,1536]{1,0:T(8,128)(2,1)S(1)}, u32[]{:S(2)}, u32[]{:S(2)}) collective-permute-start(bf16[32,1536]{1,0:T(8,128)(2,1)} %get-tuple-element.36), channel_id=1, source_target_pairs={{0,16},{4,20},{8,24},{12,28},{16,0},{20,4},{24,8},{28,12},{32,48},... | collective-permute-start | bytes 294920 | tf_op jit(solution)/shard_map/ppermute | solution.py:239
  113.2 3.1 %collective-permute-done.8 = bf16[32,1536]{1,0:T(8,128)(2,1)S(1)} collective-permute-done((bf16[32,1536]{1,0:T(8,128)(2,1)}, bf16[32,1536]{1,0:T(8,128)(2,1)S(1)}, u32[]{:S(2)}, u32[]{:S(2)}) %collective-permute-start.8) | collective-permute-done | bytes 98336 | tf_op jit(solution)/shard_map/ppermute | solution.py:239
  118.3 2.6 %collective-permute-start.11 = (bf16[32,1536]{1,0:T(8,128)(2,1)}, bf16[32,1536]{1,0:T(8,128)(2,1)}, u32[]{:S(2)}, u32[]{:S(2)}) collective-permute-start(bf16[32,1536]{1,0:T(8,128)(2,1)} %fusion.25), channel_id=1, source_target_pairs={{0,64},{4,68},{8,72},{12,76},{16,80},{20,84},{24,88},{28,92},{32,9... | collective-permute-start | bytes 294920 | tf_op jit(solution)/shard_map/ppermute | solution.py:242
  121.9 2.7 %collective-permute-done.11 = bf16[32,1536]{1,0:T(8,128)(2,1)} collective-permute-done((bf16[32,1536]{1,0:T(8,128)(2,1)}, bf16[32,1536]{1,0:T(8,128)(2,1)}, u32[]{:S(2)}, u32[]{:S(2)}) %collective-permute-start.11) | collective-permute-done | bytes 98336 | tf_op jit(solution)/shard_map/ppermute | solution.py:242
  126.9 1.5 %collective-permute-start.14 = (bf16[32,1536]{1,0:T(8,128)(2,1)S(1)}, bf16[32,1536]{1,0:T(8,128)(2,1)S(1)}, u32[]{:S(2)}, u32[]{:S(2)}) collective-permute-start(bf16[32,1536]{1,0:T(8,128)(2,1)S(1)} %fusion.19), channel_id=1, source_target_pairs={{0,16},{4,20},{8,24},{12,28},{16,0},{20,4},{24,8},{28,12},{32,48},... | collective-permute-start | bytes 294920 | tf_op jit(solution)/shard_map/ppermute | solution.py:248
  130.2 2.1 %collective-permute-start.15 = (bf16[32,1536]{1,0:T(8,128)(2,1)S(1)}, bf16[32,1536]{1,0:T(8,128)(2,1)S(1)}, u32[]{:S(2)}, u32[]{:S(2)}) collective-permute-start(bf16[32,1536]{1,0:T(8,128)(2,1)S(1)} %get-tuple-element.31), channel_id=1, source_target_pairs={{0,24},{4,28},{8,0},{12,4},{16,8},{20,12},{24,16},{28,20},{32,56},... | collective-permute-start | bytes 294920 | tf_op jit(solution)/shard_map/ppermute | solution.py:248
  133.4 2.0 %collective-permute-done.13 = bf16[32,1536]{1,0:T(8,128)(2,1)S(1)} collective-permute-done((bf16[32,1536]{1,0:T(8,128)(2,1)S(1)}, bf16[32,1536]{1,0:T(8,128)(2,1)S(1)}, u32[]{:S(2)}, u32[]{:S(2)}) %collective-permute-start.13) | collective-permute-done | bytes 98336 | tf_op jit(solution)/shard_map/ppermute | solution.py:248
  135.7 3.0 %collective-permute-start.16 = (bf16[128,1536]{1,0:T(8,128)(2,1)S(1)}, bf16[128,1536]{1,0:T(8,128)(2,1)S(1)}, u32[]{:S(2)}, u32[]{:S(2)}) collective-permute-start(bf16[128,1536]{1,0:T(8,128)(2,1)S(1)} %fusion.2), channel_id=1, source_target_pairs={{0,4},{4,0},{8,12},{12,8},{16,20},{20,16},{24,28},{28,24},{32,36},... | collective-permute-start | bytes 1179656 | tf_op jit(solution)/shard_map/ppermute | solution.py:254
  (123 shorter events, 33.2 us)
Async XLA Ops:
  0.0 32.7 %copy-start = (bf16[256,4608]{1,0:T(8,128)(2,1)S(1)}, bf16[256,4608]{1,0:T(8,128)(2,1)}, u32[]{:S(2)}) copy-start(bf16[256,4608]{1,0:T(8,128)(2,1)} %param.13) | copy-start | bytes 7077892
  0.0 31.4 %copy-start.28 = (s32[1,2]{1,0:T(1,128)S(1)}, s32[1,2]{1,0:T(1,128)}, u32[]{:S(2)}) copy-start(s32[1,2]{1,0:T(1,128)} %param.8) | copy-start | bytes 28
  2.3 53.0 %collective-permute-start.2 = (bf16[128,1536]{1,0:T(8,128)(2,1)}, bf16[128,1536]{1,0:T(8,128)(2,1)}, u32[]{:S(2)}, u32[]{:S(2)}) collective-permute-start(bf16[128,1536]{1,0:T(8,128)(2,1)} %get-tuple-element.33), channel_id=1, source_target_pairs={{0,3},{1,0},{2,1},{3,2},{4,7},{5,4},{6,5},{7,6},{8,11},{9,8},{10,9... | collective-permute-start | bytes 1179656 | tf_op jit(solution)/shard_map/ppermute | solution.py:212
  6.9 65.8 %collective-permute-start.4 = (bf16[128,1536]{1,0:T(8,128)(2,1)}, bf16[128,1536]{1,0:T(8,128)(2,1)}, u32[]{:S(2)}, u32[]{:S(2)}) collective-permute-start(bf16[128,1536]{1,0:T(8,128)(2,1)} %get-tuple-element.33), channel_id=1, source_target_pairs={{0,1},{1,2},{2,3},{3,0},{4,5},{5,6},{6,7},{7,4},{8,9},{9,10},{10,1... | collective-permute-start | bytes 1179656 | tf_op jit(solution)/shard_map/ppermute | solution.py:211
  6.9 47.4 %collective-permute-start = (bf16[128,1536]{1,0:T(8,128)(2,1)}, bf16[128,1536]{1,0:T(8,128)(2,1)}, u32[]{:S(2)}, u32[]{:S(2)}) collective-permute-start(bf16[128,1536]{1,0:T(8,128)(2,1)} %get-tuple-element.34), channel_id=1, source_target_pairs={{0,1},{1,2},{2,3},{3,0},{4,5},{5,6},{6,7},{7,4},{8,9},{9,10},{10,1... | collective-permute-start | bytes 1179656 | tf_op jit(solution)/shard_map/ppermute | solution.py:211
  6.9 65.8 %collective-permute-start.5 = (bf16[128,1536]{1,0:T(8,128)(2,1)}, bf16[128,1536]{1,0:T(8,128)(2,1)}, u32[]{:S(2)}, u32[]{:S(2)}) collective-permute-start(bf16[128,1536]{1,0:T(8,128)(2,1)} %get-tuple-element.34), channel_id=1, source_target_pairs={{0,3},{1,0},{2,1},{3,2},{4,7},{5,4},{6,5},{7,6},{8,11},{9,8},{10,9... | collective-permute-start | bytes 1179656 | tf_op jit(solution)/shard_map/ppermute | solution.py:212
  34.4 14.4 %copy-start.14 = (f32[1,1536]{1,0:T(1,128)}, f32[1,1536]{1,0:T(1,128)S(1)}, u32[]{:S(2)}) copy-start(f32[1,1536]{1,0:T(1,128)S(1)} %get-tuple-element.40.refs_1_.refs_2_) | copy-start | bytes 18436
  53.1 19.6 %copy-start.9 = (f32[256,128]{1,0:T(8,128)S(1)}, f32[256,128]{1,0:T(8,128)}, u32[]{:S(2)}) copy-start(f32[256,128]{1,0:T(8,128)} %pad_maximum_fusion.6.refs_5_) | copy-start | bytes 393220
  53.1 19.6 %copy-start.13 = (f32[1,1536]{1,0:T(1,128)S(1)}, f32[1,1536]{1,0:T(1,128)}, u32[]{:S(2)}) copy-start(f32[1,1536]{1,0:T(1,128)} %copy-done.11) | copy-start | bytes 18436
  54.2 32.5 %collective-permute-start.1 = (bf16[128,1536]{1,0:T(8,128)(2,1)}, bf16[128,1536]{1,0:T(8,128)(2,1)S(1)}, u32[]{:S(2)}, u32[]{:S(2)}) collective-permute-start(bf16[128,1536]{1,0:T(8,128)(2,1)} %collective-permute-done.refs_0_), channel_id=1, source_target_pairs={{0,1},{1,2},{2,3},{3,0},{4,5},{5,6},{6,7},{7,4},{8,9},{9,10},{10,1... | collective-permute-start | bytes 1179656 | tf_op jit(solution)/shard_map/ppermute | solution.py:211
  55.3 31.5 %collective-permute-start.3 = (bf16[128,1536]{1,0:T(8,128)(2,1)}, bf16[128,1536]{1,0:T(8,128)(2,1)S(1)}, u32[]{:S(2)}, u32[]{:S(2)}) collective-permute-start(bf16[128,1536]{1,0:T(8,128)(2,1)} %collective-permute-done.2.refs_1_), channel_id=1, source_target_pairs={{0,3},{1,0},{2,1},{3,2},{4,7},{5,4},{6,5},{7,6},{8,11},{9,8},{10,9... | collective-permute-start | bytes 1179656 | tf_op jit(solution)/shard_map/ppermute | solution.py:212
  64.3 22.5 %slice-start = ((s8[14155776]{0:T(1024)(128)(4,1)}), s8[4194304]{0:T(1024)(128)(4,1)S(1)}, s32[]{:S(2)}) async-start(s8[14155776]{0:T(1024)(128)(4,1)} %bitcast.57), calls=%async_computation | async-start | bytes 8388608
  64.3 22.5 %slice-start.1 = ((s8[14155776]{0:T(1024)(128)(4,1)}), s8[4194304]{0:T(1024)(128)(4,1)S(1)}, s32[]{:S(2)}) async-start(s8[14155776]{0:T(1024)(128)(4,1)} %bitcast.57), calls=%async_computation.1 | async-start | bytes 8388608
  101.4 4.2 %collective-permute-start.6 = (bf16[128,1536]{1,0:T(8,128)(2,1)S(1)}, bf16[128,1536]{1,0:T(8,128)(2,1)S(1)}, u32[]{:S(2)}, u32[]{:S(2)}) collective-permute-start(bf16[128,1536]{1,0:T(8,128)(2,1)S(1)} %dynamic-slice_convert_fusion), channel_id=1, source_target_pairs={{0,4},{4,0},{8,12},{12,8},{16,20},{20,16},{24,28},{28,24},{32,36},... | collective-permute-start | bytes 1179656 | tf_op jit(solution)/shard_map/ppermute | solution.py:232
  107.8 5.4 %collective-permute-start.7 = (bf16[32,1536]{1,0:T(8,128)(2,1)}, bf16[32,1536]{1,0:T(8,128)(2,1)S(1)}, u32[]{:S(2)}, u32[]{:S(2)}) collective-permute-start(bf16[32,1536]{1,0:T(8,128)(2,1)} %get-tuple-element.37), channel_id=1, source_target_pairs={{0,8},{4,12},{8,16},{12,20},{16,24},{20,28},{24,0},{28,4},{32,40},... | collective-permute-start | bytes 294920 | tf_op jit(solution)/shard_map/ppermute | solution.py:239
  109.0 7.3 %collective-permute-start.8 = (bf16[32,1536]{1,0:T(8,128)(2,1)}, bf16[32,1536]{1,0:T(8,128)(2,1)S(1)}, u32[]{:S(2)}, u32[]{:S(2)}) collective-permute-start(bf16[32,1536]{1,0:T(8,128)(2,1)} %get-tuple-element.36), channel_id=1, source_target_pairs={{0,16},{4,20},{8,24},{12,28},{16,0},{20,4},{24,8},{28,12},{32,48},... | collective-permute-start | bytes 294920 | tf_op jit(solution)/shard_map/ppermute | solution.py:239
  111.4 4.9 %collective-permute-start.9 = (bf16[32,1536]{1,0:T(8,128)(2,1)}, bf16[32,1536]{1,0:T(8,128)(2,1)S(1)}, u32[]{:S(2)}, u32[]{:S(2)}) collective-permute-start(bf16[32,1536]{1,0:T(8,128)(2,1)} %get-tuple-element.35), channel_id=1, source_target_pairs={{0,24},{4,28},{8,0},{12,4},{16,8},{20,12},{24,16},{28,20},{32,56},... | collective-permute-start | bytes 294920 | tf_op jit(solution)/shard_map/ppermute | solution.py:239
  117.0 5.0 %collective-permute-start.10 = (bf16[32,1536]{1,0:T(8,128)(2,1)}, bf16[32,1536]{1,0:T(8,128)(2,1)S(1)}, u32[]{:S(2)}, u32[]{:S(2)}) collective-permute-start(bf16[32,1536]{1,0:T(8,128)(2,1)} %fusion.25), channel_id=1, source_target_pairs={{0,32},{4,36},{8,40},{12,44},{16,48},{20,52},{24,56},{28,60},{32,6... | collective-permute-start | bytes 294920 | tf_op jit(solution)/shard_map/ppermute | solution.py:242
  118.3 6.4 %collective-permute-start.11 = (bf16[32,1536]{1,0:T(8,128)(2,1)}, bf16[32,1536]{1,0:T(8,128)(2,1)}, u32[]{:S(2)}, u32[]{:S(2)}) collective-permute-start(bf16[32,1536]{1,0:T(8,128)(2,1)} %fusion.25), channel_id=1, source_target_pairs={{0,64},{4,68},{8,72},{12,76},{16,80},{20,84},{24,88},{28,92},{32,9... | collective-permute-start | bytes 294920 | tf_op jit(solution)/shard_map/ppermute | solution.py:242
  120.9 4.9 %collective-permute-start.12 = (bf16[32,1536]{1,0:T(8,128)(2,1)}, bf16[32,1536]{1,0:T(8,128)(2,1)}, u32[]{:S(2)}, u32[]{:S(2)}) collective-permute-start(bf16[32,1536]{1,0:T(8,128)(2,1)} %fusion.25), channel_id=1, source_target_pairs={{0,96},{4,100},{8,104},{12,108},{16,112},{20,116},{24,120},{28,124... | collective-permute-start | bytes 294920 | tf_op jit(solution)/shard_map/ppermute | solution.py:242
  126.9 8.6 %collective-permute-start.14 = (bf16[32,1536]{1,0:T(8,128)(2,1)S(1)}, bf16[32,1536]{1,0:T(8,128)(2,1)S(1)}, u32[]{:S(2)}, u32[]{:S(2)}) collective-permute-start(bf16[32,1536]{1,0:T(8,128)(2,1)S(1)} %fusion.19), channel_id=1, source_target_pairs={{0,16},{4,20},{8,24},{12,28},{16,0},{20,4},{24,8},{28,12},{32,48},... | collective-permute-start | bytes 294920 | tf_op jit(solution)/shard_map/ppermute | solution.py:248
  129.5 5.9 %collective-permute-start.13 = (bf16[32,1536]{1,0:T(8,128)(2,1)S(1)}, bf16[32,1536]{1,0:T(8,128)(2,1)S(1)}, u32[]{:S(2)}, u32[]{:S(2)}) collective-permute-start(bf16[32,1536]{1,0:T(8,128)(2,1)S(1)} %get-tuple-element.32), channel_id=1, source_target_pairs={{0,8},{4,12},{8,16},{12,20},{16,24},{20,28},{24,0},{28,4},{32,40},... | collective-permute-start | bytes 294920 | tf_op jit(solution)/shard_map/ppermute | solution.py:248
  130.2 5.4 %collective-permute-start.15 = (bf16[32,1536]{1,0:T(8,128)(2,1)S(1)}, bf16[32,1536]{1,0:T(8,128)(2,1)S(1)}, u32[]{:S(2)}, u32[]{:S(2)}) collective-permute-start(bf16[32,1536]{1,0:T(8,128)(2,1)S(1)} %get-tuple-element.31), channel_id=1, source_target_pairs={{0,24},{4,28},{8,0},{12,4},{16,8},{20,12},{24,16},{28,20},{32,56},... | collective-permute-start | bytes 294920 | tf_op jit(solution)/shard_map/ppermute | solution.py:248
  135.7 4.4 %collective-permute-start.16 = (bf16[128,1536]{1,0:T(8,128)(2,1)S(1)}, bf16[128,1536]{1,0:T(8,128)(2,1)S(1)}, u32[]{:S(2)}, u32[]{:S(2)}) collective-permute-start(bf16[128,1536]{1,0:T(8,128)(2,1)S(1)} %fusion.2), channel_id=1, source_target_pairs={{0,4},{4,0},{8,12},{12,8},{16,20},{20,16},{24,28},{28,24},{32,36},... | collective-permute-start | bytes 1179656 | tf_op jit(solution)/shard_map/ppermute | solution.py:254
  (28 other events, 136.1 us)

commit v2 on v1

--- a/solution.py
+++ b/solution.py
@@ -13,6 +13,8 @@
 HEADS = D // HEAD
 TILE = 512
 TILES = D // TILE
+WIDE = D + HEAD
+VMEM = 16 << 20
 epsilon = 1e-06
 EXP_SCALE = HEAD ** (-0.5) * math.log2(math.e)
 f32, bf16 = jnp.float32, jnp.bfloat16
@@ -27,12 +29,18 @@
     return jnp.dot(embedded, time_weight.astype(f32), precision=lax.Precision.HIGHEST)
 
 
-def rope_tables(positions):
+def with_positions(x, positions):
+    lane = jnp.arange(HEAD, dtype=jnp.int32)[None, :]
+    high, low = (positions // 32)[:, None], (positions % 32)[:, None]
+    digits = jnp.where(lane == 0, high, jnp.where(lane == 1, low, 0))
+    return jnp.concatenate([x, digits.astype(bf16)], axis=1)
+
+
+def rope_rates():
     half_width = HEAD // 2
-    inverse = jnp.exp(-math.log(10000.0) * jnp.arange(half_width, dtype=f32) / half_width)
-    angles = positions.astype(f32)[:, None] * inverse[None, :]
-    cosine, sine = jnp.cos(angles), jnp.sin(angles)
-    return jnp.concatenate([cosine, cosine], axis=1), jnp.concatenate([-sine, sine], axis=1)
+    lane = jnp.arange(HEAD, dtype=jnp.int32)
+    inverse = jnp.exp(-math.log(10000.0) * (lane % half_width).astype(f32) / half_width)
+    return jnp.stack([inverse, jnp.where(lane < half_width, -1.0, 1.0)])
 
 
 def norm_rope(proj, gain, cos, sin, out_ref):
@@ -42,64 +50,58 @@
         p = proj[:, h * HEAD : (h + 1) * HEAD]
         total = total + p * p
     inv = lax.rsqrt(jnp.sum(total, axis=1, keepdims=True) * (1.0 / D) + epsilon)
-    cos, sin = cos[...], sin[...]
     for h in range(HEADS):
         at = slice(h * HEAD, (h + 1) * HEAD)
         y = proj[:, at] * inv * gain[:, at]
         out_ref[:, at] = (y * cos + pltpu.roll(y, HEAD // 2, 1) * sin).astype(bf16)
 
 
-def project_kernel(n_x, with_q, *refs):
-    x_refs, refs = refs[:n_x], refs[n_x:]
-    shift, scale, gains, cos, sin, w = refs[:6]
-    outs, (normed, proj) = refs[6:-2], refs[-2:]
-    i = pl.program_id(0)
-
-    @pl.when(i == 0)
-    def _():
-        at = 0
-        for x_ref in x_refs:
-            x = x_ref[...].astype(f32)
-            inv = lax.rsqrt(jnp.sum(x * x, axis=1, keepdims=True) * (1.0 / D) + epsilon)
-            normed[pl.ds(at, x.shape[0]), :] = (x * inv * (1.0 + scale[...]) + shift[...]).astype(bf16)
-            at += x.shape[0]
-
-    acc = jnp.dot(normed[...], w[...], preferred_element_type=f32)
-    groups = ["q", "k", "v"] if with_q else ["k", "v"]
-    for g, name in enumerate(groups):
+def project_kernel(with_q, *refs):
+    x_refs, (shift, scale, gains, rates, w) = refs[:2], refs[2:7]
+    outs, (normed, proj) = refs[7:-2], refs[-2:]
+    at, angles = 0, []
+    for x_ref in x_refs:
+        rows = x_ref.shape[0]
+        x = x_ref[:, :D].astype(f32)
+        inv = lax.rsqrt(jnp.sum(x * x, axis=1, keepdims=True) * (1.0 / D) + epsilon)
+        normed[pl.ds(at, rows), :] = (x * inv * (1.0 + scale[...]) + shift[...]).astype(bf16)
+        digits = x_ref[:, D:].astype(f32)
+        angles.append((digits[:, 0:1] * 32.0 + digits[:, 1:2]) * rates[0:1, :])
+        at += rows
+    angles = jnp.concatenate(angles, axis=0)
+    cos, sin = jnp.cos(angles), jnp.sin(angles) * rates[1:2, :]
+    names = ["q", "k", "v"] if with_q else ["k", "v"]
+    out_of = dict(zip(names, outs))
+    first = {"q": 0, "k": TILES, "v": 2 * TILES}
+    for g, name in enumerate(["k", "q", "v"] if with_q else ["k", "v"]):
         for t in range(TILES):
-
-            @pl.when(i == g * TILES + t)
-            def _(g=g, name=name, t=t):
-                if name == "v":
-                    outs[g][:, t * TILE : (t + 1) * TILE] = acc.astype(bf16)
-                else:
-                    proj[:, t * TILE : (t + 1) * TILE] = acc
-                    if t == TILES - 1:
-                        row = 0 if name == "q" else 1
-                        norm_rope(proj, gains[row : row + 1, :], cos, sin, outs[g])
-
-
-def project(xs, shift, scale, gains, cos, sin, w_qkv, with_q):
+            at = slice(t * TILE, (t + 1) * TILE)
+            col = (first[name] + t) * TILE
+            acc = jnp.dot(normed[...], w[:, col : col + TILE], preferred_element_type=f32)
+            if name == "v":
+                out_of[name][:, at] = acc.astype(bf16)
+            else:
+                proj[g, :, at] = acc
+        if name != "v":
+            row = 1 if name == "k" else 0
+            norm_rope(proj.at[g], gains[row : row + 1, :], cos, sin, out_of[name])
+
+
+def project(xs, shift, scale, gains, rates, w_qkv, with_q):
     rows = sum(x.shape[0] for x in xs)
     groups = 3 if with_q else 2
-    first = 0 if with_q else TILES
-    whole = lambda a: pl.BlockSpec(a.shape, lambda i: (0, 0))
-    small = (shift, scale, gains, cos, sin)
+    vm = pl.BlockSpec(memory_space=pltpu.VMEM)
     return pl.pallas_call(
-        functools.partial(project_kernel, len(xs), with_q),
-        grid=(groups * TILES,),
-        in_specs=[whole(x) for x in xs]
-        + [whole(a) for a in small]
-        + [pl.BlockSpec((D, TILE), lambda i: (0, i + first))],
-        out_specs=[pl.BlockSpec((rows, D), lambda i: (0, 0))] * groups,
-        out_shape=[jax.ShapeDtypeStruct((rows, D), bf16)] * groups,
-        scratch_shapes=[pltpu.VMEM((rows, D), bf16), pltpu.VMEM((rows, D), f32)],
+        functools.partial(project_kernel, with_q),
+        in_specs=[vm] * 7,
+        out_specs=[vm] * groups,
+        out_shape=[pltpu.VMEM((rows, D), bf16)] * groups,
+        scratch_shapes=[pltpu.VMEM((rows, D), bf16), pltpu.VMEM((groups - 1, rows, D), f32)],
         cost_estimate=pl.CostEstimate(
             flops=2 * rows * D * D * groups, bytes_accessed=2 * D * D * groups, transcendentals=0
         ),
-        compiler_params=pltpu.CompilerParams(vmem_limit_bytes=28 << 20),
-    )(*xs, *small, w_qkv)
+        compiler_params=pltpu.CompilerParams(vmem_limit_bytes=VMEM),
+    )(*xs, shift, scale, gains, rates, w_qkv)
 
 
 def attend_kernel(n_kv, q_ref, *refs):
@@ -137,22 +139,20 @@
         in_specs=[vm] * (1 + len(flat)),
         out_specs=[vm] * 3,
         out_shape=[
-            jax.ShapeDtypeStruct((rows, HEAD), f32),
-            jax.ShapeDtypeStruct((rows, HEAD), f32),
-            jax.ShapeDtypeStruct((rows, D), f32),
+            pltpu.VMEM((rows, HEAD), f32),
+            pltpu.VMEM((rows, HEAD), f32),
+            pltpu.VMEM((rows, D), f32),
         ],
         cost_estimate=pl.CostEstimate(
             flops=8 * rows * D * keys, bytes_accessed=4 * rows * D * 2, transcendentals=rows * keys * HEADS
         ),
-        compiler_params=pltpu.CompilerParams(vmem_limit_bytes=28 << 20),
+        compiler_params=pltpu.CompilerParams(vmem_limit_bytes=VMEM),
     )(q, *flat)
 
 
 def finish_kernel(n_kv, h_ref, q_ref, *refs):
     kv, refs = refs[: 2 * n_kv], refs[2 * n_kv :]
-    m_ref, l_ref, acc_ref, x_ref, gate_ref, w_hbm, out_ref, w_ref, attended, sem = refs
-    load = pltpu.make_async_copy(w_hbm, w_ref, sem)
-    load.start()
+    m_ref, l_ref, acc_ref, x_ref, gate_ref, w_ref, out_ref, attended = refs
     for h in range(HEADS):
         at = slice(h * HEAD, (h + 1) * HEAD)
         q = q_ref[:, at]
@@ -173,7 +173,6 @@
             total = total + jnp.sum(p, axis=1, keepdims=True)
             acc = acc + jnp.dot(p.astype(bf16), kv[2 * j + 1][:, at], preferred_element_type=f32)
         attended[:, at] = (acc / total).astype(bf16)
-    load.wait()
     size = h_ref[0, 0]
     for t in range(TILES):
         at = slice(t * TILE, (t + 1) * TILE)
@@ -189,25 +188,22 @@
     return pl.pallas_call(
         functools.partial(finish_kernel, len(kvs)),
         in_specs=[pl.BlockSpec(memory_space=pltpu.SMEM)]
-        + [vm] * (1 + len(flat) + 3 + 2)
-        + [pl.BlockSpec(memory_space=pl.ANY)],
+        + [vm] * (1 + len(flat) + 3 + 3),
         out_specs=vm,
-        out_shape=jax.ShapeDtypeStruct((rows, D), f32),
-        scratch_shapes=[pltpu.VMEM((D, D), bf16), pltpu.VMEM((rows, D), bf16), pltpu.SemaphoreType.DMA],
+        out_shape=pltpu.VMEM((rows, D), f32),
+        scratch_shapes=[pltpu.VMEM((rows, D), bf16)],
         cost_estimate=pl.CostEstimate(
             flops=8 * rows * D * keys + 2 * rows * D * D,
             bytes_accessed=2 * D * D,
             transcendentals=rows * keys * HEADS,
         ),
-        compiler_params=pltpu.CompilerParams(vmem_limit_bytes=28 << 20),
+        compiler_params=pltpu.CompilerParams(vmem_limit_bytes=VMEM),
     )(step_size, q, *flat, *state, x, gate, w_out)
 
 
-def gather_states(x, n):
-    half = x.shape[0] // 2
+def gather_states(first, second, n):
     right = [(i, (i + 1) % n) for i in range(n)]
     left = [(i, (i - 1) % n) for i in range(n)]
-    first, second = x[:half], x[half:]
     to_right = lambda v: lax.ppermute(v, "seq", right)
     to_left = lambda v: lax.ppermute(v, "seq", left)
     r_first, l_second = to_right(first), to_left(second)
@@ -259,24 +255,20 @@
 
 def on_device(states, step_times, positions, w_qkv, qk_gain, w_out, time_weight):
     n = lax.axis_size("seq")
-    z = lax.axis_index("seq")
     x = states[0]
     half = x.shape[0] // 2
-    chunks = gather_states(x, n)
-    all_positions = lax.all_gather(positions, "seq", axis=0, tiled=True)
+    message = with_positions(x, positions)
+    own = (message[:half], message[half:])
+    chunks = gather_states(*own, n)
 
     modulated = modulation(step_times, time_weight)
     shift, scale, gate = modulated[:, :D], modulated[:, D : 2 * D], modulated[:, 2 * D :]
-
-    q, k, v = project([x], shift, scale, qk_gain, *rope_tables(positions), w_qkv, True)
+    rates = rope_rates()
+
+    q, k, v = project(own, shift, scale, qk_gain, rates, w_qkv, True)
     kvs = [(k, v)]
-    sources = [((z - 1) % n, (z + 1) % n), ((z - 1) % n, (z + 1) % n), ((z + 2) % n, (z + 2) % n)]
-    halves = [(0, 1), (1, 0), (0, 1)]
-    for chunk, source, which in zip(chunks, sources, halves):
-        where = jnp.concatenate(
-            [lax.dynamic_slice_in_dim(all_positions, (2 * s + w) * half, half) for s, w in zip(source, which)]
-        )
-        kvs.append(tuple(project(chunk, shift, scale, qk_gain, *rope_tables(where), w_qkv, False)))
+    for chunk in chunks:
+        kvs.append(tuple(project(chunk, shift, scale, qk_gain, rates, w_qkv, False)))
     state = attend(q, kvs[:3])
     step_size = (step_times[:, 1:] - step_times[:, :1]).astype(f32) / 1000.0
     inc = finish(step_size, q, kvs[3:], state, x, gate, w_out)

time: 142 us -> 95.2 us (0.67)
  blocking collectives: 18.4 us -> 0 us
  local copies, waits for them, and re-layouts: 24.7 us -> 7.72 us
  Pallas kernels: 40 us -> 27.7 us
  waiting for transfers between devices: 12.3 us -> 17.3 us
  other arithmetic: 12.8 us -> 9.25 us
    all_gather x1 -> x0, blocking collectives: 18.4 us -> none  [on_device(): all_positions = lax.all_gather(positions, 'seq', axis=0, tiled=True)]
    unnamed x70 -> x24, local copies, waits for them, and re-layouts: 20.3 us -> 6.21 us
    pallas_call x4, Pallas kernels: 26.9 us -> 16.3 us  [project(): pl.pallas_call(functools.partial(project_kernel, with_q), in_specs=[vm] *...]
    ppermute x3, waiting for transfers between devices: 0.01 us -> 4.98 us  [gather_states(): to_right = lambda v: lax.ppermute(v, 'seq', right)]
    neg x1 -> x0, other arithmetic: 2.53 us -> none  [rope_tables(): -sine]
    slice x1 -> x0, local copies, waits for them, and re-layouts: 2.26 us -> none  [gather_states(): first, second = (x[:half], x[half:])]
    concatenate x8 -> x1, other arithmetic: 3.14 us -> 1.18 us  [with_positions(): return jnp.concatenate([x, digits.astype(bf16)], axis=1)]
    pallas_call x1, Pallas kernels: 7.94 us -> 6.34 us  [finish(): pl.pallas_call(functools.partial(finish_kernel, len(kvs)), in_specs=[pl.B...]
  transfers between devices with their start and end apart: 17 -> 17, of which waited for: 7 -> 8; matrix products, arithmetic and copies ran while one was open for 7% -> 4% of each run, Pallas kernels for 19% -> 19%
where the time goes in v2:
time: 95.2 us; the launch traced here: 94.9 us
  starting transfers between devices  29.6 us (31%)
  Pallas kernels  27.7 us (29%)
  waiting for transfers between devices  17.3 us (18%)
  other arithmetic  9.25 us (10%)
  local copies, waits for them, and re-layouts  7.72 us (8%)
  between operations  2.29 us (2%)
  matrix products  1.01 us (1%)
    pallas_call x4, Pallas kernels, project(): pl.pallas_call(functools.partial(project_kernel, with_q), in_specs=[vm] *...  16.3 us
    ppermute x3, starting transfers between devices, gather_states(): to_left = lambda v: lax.ppermute(v, 'seq', left)  10 us
    pallas_call x1, Pallas kernels, finish(): pl.pallas_call(functools.partial(finish_kernel, len(kvs)), in_specs=[pl.B...  6.34 us
    unnamed x24, local copies, waits for them, and re-layouts  6.21 us
    pallas_call x1, Pallas kernels, attend(): pl.pallas_call(functools.partial(attend_kernel, len(kvs)), in_specs=[vm]...  5.06 us
    ppermute x3, starting transfers between devices, scan_steps(): rows_y = [lax.ppermute(row_b, 'step', along_y(k)) for k in (1, 2, 3)]  4.99 us
    ppermute x3, waiting for transfers between devices, gather_states(): to_right = lambda v: lax.ppermute(v, 'seq', right)  4.98 us
    ppermute x3, starting transfers between devices, scan_steps(): src.append(lax.ppermute(piece, 'step', along_x(k)).astype(f32))  4.82 us
  transfers between devices with their start and end apart: 17, of which 8 were waited for; matrix products, arithmetic and copies ran while one was open for 4% of the time, Pallas kernels for 19%

profile of v2, /device:TPU:1, one launch (start us, length us, event | category | flops | bytes accessed | tf_op | source)
XLA Modules:
  0.0 94.9 jit_solution(16457463728083187906)
XLA Ops:
  2.2 4.7 %collective-permute-start.2 = (bf16[128,1664]{1,0:T(8,128)(2,1)S(1)}, bf16[128,1664]{1,0:T(8,128)(2,1)}, u32[]{:S(2)}, u32[]{:S(2)}) collective-permute-start(bf16[128,1664]{1,0:T(8,128)(2,1)S(1)} %get-tuple-element.33.refs_1_), channel_id=1, source_target_pairs={{0,3},{1,0},{2,1},{3,2},{4,7},{5,4},{6,5},{7,6},{8,11},{9,8},{10,9... | collective-permute-start | bytes 1277960 | tf_op jit(solution)/shard_map/ppermute | solution.py:208
  6.9 2.7 %collective-permute-start.5 = (bf16[128,1664]{1,0:T(8,128)(2,1)S(1)}, bf16[128,1664]{1,0:T(8,128)(2,1)}, u32[]{:S(2)}, u32[]{:S(2)}) collective-permute-start(bf16[128,1664]{1,0:T(8,128)(2,1)S(1)} %get-tuple-element.34.refs_0_), channel_id=1, source_target_pairs={{0,3},{1,0},{2,1},{3,2},{4,7},{5,4},{6,5},{7,6},{8,11},{9,8},{10,9... | collective-permute-start | bytes 1277960 | tf_op jit(solution)/shard_map/ppermute | solution.py:208
  13.3 5.0 %copy-done.1 = bf16[1536,4608]{1,0:T(8,128)(2,1)S(1)} copy-done((bf16[1536,4608]{1,0:T(8,128)(2,1)S(1)}, bf16[1536,4608]{1,0:T(8,128)(2,1)}, u32[]{:S(2)}) %copy-start.1) | copy-done | bytes 14155800
  18.3 4.4 %shard_map.73 = (bf16[256,1536]{1,0:T(8,128)(2,1)S(1)}, bf16[256,1536]{1,0:T(8,128)(2,1)S(1)}, bf16[256,1536]{1,0:T(8,128)(2,1)S(1)}) custom-call(bf16[128,1664]{1,0:T(8,128)(2,1)S(1)} %get-tuple-element.34.refs_0_, bf16[128,1664]{1,0:T(8,128)(2,1)S(1)} %get-tuple-element.33.refs_1_, f32[1,1536]{1,0:T(1,128)S(1)} %get-tuple-element.40.refs_2_, ...), custom_call_target="tpu_custom_call" | custom-call | flops 3623878656 | bytes 14155776 | tf_op jit(solution)/shard_map/pallas_call | solution.py:94
  22.7 5.0 %collective-permute-done.refs_0_ = bf16[128,1664]{1,0:T(8,128)(2,1)} collective-permute-done((bf16[128,1664]{1,0:T(8,128)(2,1)S(1)}, bf16[128,1664]{1,0:T(8,128)(2,1)}, u32[]{:S(2)}, u32[]{:S(2)}) %collective-permute-start) | collective-permute-done | bytes 426016 | tf_op jit(solution)/shard_map/ppermute | solution.py:207
  27.7 2.7 %collective-permute-start.3 = (bf16[128,1664]{1,0:T(8,128)(2,1)}, bf16[128,1664]{1,0:T(8,128)(2,1)S(1)}, u32[]{:S(2)}, u32[]{:S(2)}) collective-permute-start(bf16[128,1664]{1,0:T(8,128)(2,1)} %collective-permute-done.2.refs_1_), channel_id=1, source_target_pairs={{0,3},{1,0},{2,1},{3,2},{4,7},{5,4},{6,5},{7,6},{8,11},{9,8},{10,9... | collective-permute-start | bytes 1277960 | tf_op jit(solution)/shard_map/ppermute | solution.py:208
  30.3 4.3 %shard_map.75 = (bf16[256,1536]{1,0:T(8,128)(2,1)S(1)}, bf16[256,1536]{1,0:T(8,128)(2,1)S(1)}) custom-call(bf16[128,1664]{1,0:T(8,128)(2,1)} %collective-permute-done.refs_0_, bf16[128,1664]{1,0:T(8,128)(2,1)} %collective-permute-done.2.refs_1_, f32[1,1536]{1,0:T(1,128)S(1)} %get-tuple-element.40.refs_2_, f32[1,1536]{1,0:T(1,128)S(1)} %get-tuple-element.39.refs_3_, ...), custom_call_target="tpu_custom_call" | custom-call | flops 2415919104 | bytes 9437184 | tf_op jit(solution)/shard_map/pallas_call | solution.py:94
  34.6 4.3 %shard_map.76 = (bf16[256,1536]{1,0:T(8,128)(2,1)S(1)}, bf16[256,1536]{1,0:T(8,128)(2,1)S(1)}) custom-call(bf16[128,1664]{1,0:T(8,128)(2,1)} %collective-permute-done.4.refs_0_, bf16[128,1664]{1,0:T(8,128)(2,1)} %collective-permute-done.5.refs_1_, f32[1,1536]{1,0:T(1,128)S(1)} %get-tuple-element.40.refs_2_, f32[1,1536]{1,0:T(1,128)S(1)} %get-tuple-element.39.refs_3_, ...), custom_call_target="tpu_custom_call" | custom-call | flops 2415919104 | bytes 9437184 | tf_op jit(solution)/shard_map/pallas_call | solution.py:94
  38.9 5.1 %shard_map.77 = (f32[256,128]{1,0:T(8,128)S(1)}, f32[256,128]{1,0:T(8,128)S(1)}, f32[256,1536]{1,0:T(8,128)S(1)}) custom-call(bf16[256,1536]{1,0:T(8,128)(2,1)S(1)} %get-tuple-element.17.q_ref, bf16[256,1536]{1,0:T(8,128)(2,1)S(1)} %get-tuple-element.20.refs_0_, bf16[256,1536]{1,0:T(8,128)(2,1)S(1)} %get-tuple-element.21.refs_1_, ...), custom_call_target="tpu_custom_call" | custom-call | flops 2415919104 | bytes 3145728 | tf_op jit(solution)/shard_map/pallas_call | solution.py:137
  44.0 3.4 %shard_map.74 = (bf16[256,1536]{1,0:T(8,128)(2,1)S(1)}, bf16[256,1536]{1,0:T(8,128)(2,1)S(1)}) custom-call(bf16[128,1664]{1,0:T(8,128)(2,1)S(1)} %collective-permute-done.1.refs_0_, bf16[128,1664]{1,0:T(8,128)(2,1)S(1)} %collective-permute-done.3.refs_1_, f32[1,1536]{1,0:T(1,128)S(1)} %get-tuple-element.40.refs_2_, f32[1,1536]{1,0:T(1,128)S(1)} %get-tuple-element.39.refs_3_, ...), custom_call_target="tpu_custom_call" | custom-call | flops 2415919104 | bytes 9437184 | tf_op jit(solution)/shard_map/pallas_call | solution.py:94
  47.5 6.3 %shard_map.78 = f32[256,1536]{1,0:T(8,128)S(1)} custom-call(f32[1,1]{1,0:T(1,128)S(6)} %div.45.h_ref, bf16[256,1536]{1,0:T(8,128)(2,1)S(1)} %get-tuple-element.17.q_ref, bf16[256,1536]{1,0:T(8,128)(2,1)S(1)} %get-tuple-element.18.refs_0_, bf16[256,1536]{1,0:T(8,128)(2,1)S(1)} %get-tuple-element.19.refs_1_, f32[256,128]{1,0:T(8,128)S(1)} %get-tuple-element.26.refs_2_, ...), custom_call_target="tpu_custom_call" | custom-call | flops 2013265920 | bytes 4718592 | tf_op jit(solution)/shard_map/pallas_call | solution.py:188
  55.0 2.5 %collective-permute-start.6 = (bf16[128,1536]{1,0:T(8,128)(2,1)S(1)}, bf16[128,1536]{1,0:T(8,128)(2,1)S(1)}, u32[]{:S(2)}, u32[]{:S(2)}) collective-permute-start(bf16[128,1536]{1,0:T(8,128)(2,1)S(1)} %dynamic-slice_convert_fusion), channel_id=1, source_target_pairs={{0,4},{4,0},{8,12},{12,8},{16,20},{20,16},{24,28},{28,24},{32,36},... | collective-permute-start | bytes 1179656 | tf_op jit(solution)/shard_map/ppermute | solution.py:228
  57.5 1.3 %collective-permute-done.6 = bf16[128,1536]{1,0:T(8,128)(2,1)S(1)} collective-permute-done((bf16[128,1536]{1,0:T(8,128)(2,1)S(1)}, bf16[128,1536]{1,0:T(8,128)(2,1)S(1)}, u32[]{:S(2)}, u32[]{:S(2)}) %collective-permute-start.6) | collective-permute-done | bytes 393248 | tf_op jit(solution)/shard_map/ppermute | solution.py:228
  58.9 1.3 %convert_add_fusion.1 = f32[128,1536]{1,0:T(8,128)S(1)} fusion(bf16[128,1536]{1,0:T(8,128)(2,1)S(1)} %collective-permute-done.6, f32[256,1536]{1,0:T(8,128)} %copy-done.3, s32[]{:T(128)S(6)} %select_n.318), kind=kLoop, calls=%fused_computation.3 | loop fusion | flops 393216 | bytes 1966084 | tf_op jit(solution)/shard_map/add | solution.py:230
  62.2 2.4 %collective-permute-start.8 = (bf16[32,1536]{1,0:T(8,128)(2,1)}, bf16[32,1536]{1,0:T(8,128)(2,1)S(1)}, u32[]{:S(2)}, u32[]{:S(2)}) collective-permute-start(bf16[32,1536]{1,0:T(8,128)(2,1)} %get-tuple-element.36), channel_id=1, source_target_pairs={{0,16},{4,20},{8,24},{12,28},{16,0},{20,4},{24,8},{28,12},{32,48},... | collective-permute-start | bytes 294920 | tf_op jit(solution)/shard_map/ppermute | solution.py:235
  66.5 3.1 %collective-permute-done.8 = bf16[32,1536]{1,0:T(8,128)(2,1)S(1)} collective-permute-done((bf16[32,1536]{1,0:T(8,128)(2,1)}, bf16[32,1536]{1,0:T(8,128)(2,1)S(1)}, u32[]{:S(2)}, u32[]{:S(2)}) %collective-permute-start.8) | collective-permute-done | bytes 98336 | tf_op jit(solution)/shard_map/ppermute | solution.py:235
  70.2 1.3 %collective-permute-start.10 = (bf16[32,1536]{1,0:T(8,128)(2,1)}, bf16[32,1536]{1,0:T(8,128)(2,1)S(1)}, u32[]{:S(2)}, u32[]{:S(2)}) collective-permute-start(bf16[32,1536]{1,0:T(8,128)(2,1)} %fusion.26), channel_id=1, source_target_pairs={{0,32},{4,36},{8,40},{12,44},{16,48},{20,52},{24,56},{28,60},{32,6... | collective-permute-start | bytes 294920 | tf_op jit(solution)/shard_map/ppermute | solution.py:238
  71.5 2.6 %collective-permute-start.11 = (bf16[32,1536]{1,0:T(8,128)(2,1)}, bf16[32,1536]{1,0:T(8,128)(2,1)}, u32[]{:S(2)}, u32[]{:S(2)}) collective-permute-start(bf16[32,1536]{1,0:T(8,128)(2,1)} %fusion.26), channel_id=1, source_target_pairs={{0,64},{4,68},{8,72},{12,76},{16,80},{20,84},{24,88},{28,92},{32,9... | collective-permute-start | bytes 294920 | tf_op jit(solution)/shard_map/ppermute | solution.py:238
  75.2 2.7 %collective-permute-done.11 = bf16[32,1536]{1,0:T(8,128)(2,1)} collective-permute-done((bf16[32,1536]{1,0:T(8,128)(2,1)}, bf16[32,1536]{1,0:T(8,128)(2,1)}, u32[]{:S(2)}, u32[]{:S(2)}) %collective-permute-start.11) | collective-permute-done | bytes 98336 | tf_op jit(solution)/shard_map/ppermute | solution.py:238
  80.2 1.5 %collective-permute-start.14 = (bf16[32,1536]{1,0:T(8,128)(2,1)S(1)}, bf16[32,1536]{1,0:T(8,128)(2,1)S(1)}, u32[]{:S(2)}, u32[]{:S(2)}) collective-permute-start(bf16[32,1536]{1,0:T(8,128)(2,1)S(1)} %fusion.20), channel_id=1, source_target_pairs={{0,16},{4,20},{8,24},{12,28},{16,0},{20,4},{24,8},{28,12},{32,48},... | collective-permute-start | bytes 294920 | tf_op jit(solution)/shard_map/ppermute | solution.py:244
  83.1 2.4 %collective-permute-start.15 = (bf16[32,1536]{1,0:T(8,128)(2,1)S(1)}, bf16[32,1536]{1,0:T(8,128)(2,1)S(1)}, u32[]{:S(2)}, u32[]{:S(2)}) collective-permute-start(bf16[32,1536]{1,0:T(8,128)(2,1)S(1)} %get-tuple-element.31), channel_id=1, source_target_pairs={{0,24},{4,28},{8,0},{12,4},{16,8},{20,12},{24,16},{28,20},{32,56},... | collective-permute-start | bytes 294920 | tf_op jit(solution)/shard_map/ppermute | solution.py:244
  86.7 2.1 %collective-permute-done.13 = bf16[32,1536]{1,0:T(8,128)(2,1)S(1)} collective-permute-done((bf16[32,1536]{1,0:T(8,128)(2,1)S(1)}, bf16[32,1536]{1,0:T(8,128)(2,1)S(1)}, u32[]{:S(2)}, u32[]{:S(2)}) %collective-permute-start.13) | collective-permute-done | bytes 98336 | tf_op jit(solution)/shard_map/ppermute | solution.py:244
  89.0 3.0 %collective-permute-start.16 = (bf16[128,1536]{1,0:T(8,128)(2,1)S(1)}, bf16[128,1536]{1,0:T(8,128)(2,1)S(1)}, u32[]{:S(2)}, u32[]{:S(2)}) collective-permute-start(bf16[128,1536]{1,0:T(8,128)(2,1)S(1)} %fusion.2), channel_id=1, source_target_pairs={{0,4},{4,0},{8,12},{12,8},{16,20},{20,16},{24,28},{28,24},{32,36},... | collective-permute-start | bytes 1179656 | tf_op jit(solution)/shard_map/ppermute | solution.py:250
  92.0 1.3 %collective-permute-done.16 = bf16[128,1536]{1,0:T(8,128)(2,1)S(1)} collective-permute-done((bf16[128,1536]{1,0:T(8,128)(2,1)S(1)}, bf16[128,1536]{1,0:T(8,128)(2,1)S(1)}, u32[]{:S(2)}, u32[]{:S(2)}) %collective-permute-start.16) | collective-permute-done | bytes 393248 | tf_op jit(solution)/shard_map/ppermute | solution.py:250
  (66 shorter events, 17.2 us)
Async XLA Ops:
  0.0 10.9 %copy-start = (bf16[256,4608]{1,0:T(8,128)(2,1)S(1)}, bf16[256,4608]{1,0:T(8,128)(2,1)}, u32[]{:S(2)}) copy-start(bf16[256,4608]{1,0:T(8,128)(2,1)} %param.13) | copy-start | bytes 7077892
  0.0 9.6 %copy-start.9 = (s32[1,2]{1,0:T(1,128)S(1)}, s32[1,2]{1,0:T(1,128)}, u32[]{:S(2)}) copy-start(s32[1,2]{1,0:T(1,128)} %param.8) | copy-start | bytes 28
  2.2 11.1 %copy-start.6 = (f32[2,1536]{1,0:T(2,128)S(1)}, f32[2,1536]{1,0:T(2,128)}, u32[]{:S(2)}) copy-start(f32[2,1536]{1,0:T(2,128)} %refs_4_.7) | copy-start | bytes 36868
  2.2 25.5 %collective-permute-start.2 = (bf16[128,1664]{1,0:T(8,128)(2,1)S(1)}, bf16[128,1664]{1,0:T(8,128)(2,1)}, u32[]{:S(2)}, u32[]{:S(2)}) collective-permute-start(bf16[128,1664]{1,0:T(8,128)(2,1)S(1)} %get-tuple-element.33.refs_1_), channel_id=1, source_target_pairs={{0,3},{1,0},{2,1},{3,2},{4,7},{5,4},{6,5},{7,6},{8,11},{9,8},{10,9... | collective-permute-start | bytes 1277960 | tf_op jit(solution)/shard_map/ppermute | solution.py:208
  6.8 27.8 %collective-permute-start.4 = (bf16[128,1664]{1,0:T(8,128)(2,1)S(1)}, bf16[128,1664]{1,0:T(8,128)(2,1)}, u32[]{:S(2)}, u32[]{:S(2)}) collective-permute-start(bf16[128,1664]{1,0:T(8,128)(2,1)S(1)} %get-tuple-element.33.refs_1_), channel_id=1, source_target_pairs={{0,1},{1,2},{2,3},{3,0},{4,5},{5,6},{6,7},{7,4},{8,9},{9,10},{10,1... | collective-permute-start | bytes 1277960 | tf_op jit(solution)/shard_map/ppermute | solution.py:207
  6.9 20.8 %collective-permute-start = (bf16[128,1664]{1,0:T(8,128)(2,1)S(1)}, bf16[128,1664]{1,0:T(8,128)(2,1)}, u32[]{:S(2)}, u32[]{:S(2)}) collective-permute-start(bf16[128,1664]{1,0:T(8,128)(2,1)S(1)} %get-tuple-element.34.refs_0_), channel_id=1, source_target_pairs={{0,1},{1,2},{2,3},{3,0},{4,5},{5,6},{6,7},{7,4},{8,9},{9,10},{10,1... | collective-permute-start | bytes 1277960 | tf_op jit(solution)/shard_map/ppermute | solution.py:207
  6.9 27.8 %collective-permute-start.5 = (bf16[128,1664]{1,0:T(8,128)(2,1)S(1)}, bf16[128,1664]{1,0:T(8,128)(2,1)}, u32[]{:S(2)}, u32[]{:S(2)}) collective-permute-start(bf16[128,1664]{1,0:T(8,128)(2,1)S(1)} %get-tuple-element.34.refs_0_), channel_id=1, source_target_pairs={{0,3},{1,0},{2,1},{3,2},{4,7},{5,4},{6,5},{7,6},{8,11},{9,8},{10,9... | collective-permute-start | bytes 1277960 | tf_op jit(solution)/shard_map/ppermute | solution.py:208
  18.3 12.0 %copy-start.2 = (bf16[1536,4608]{1,0:T(8,128)(2,1)S(1)}, bf16[1536,4608]{1,0:T(8,128)(2,1)}, u32[]{:S(2)}) copy-start(bf16[1536,4608]{1,0:T(8,128)(2,1)} %refs_6_.7) | copy-start | bytes 42467332
  27.7 16.4 %collective-permute-start.1 = (bf16[128,1664]{1,0:T(8,128)(2,1)}, bf16[128,1664]{1,0:T(8,128)(2,1)S(1)}, u32[]{:S(2)}, u32[]{:S(2)}) collective-permute-start(bf16[128,1664]{1,0:T(8,128)(2,1)} %collective-permute-done.refs_0_), channel_id=1, source_target_pairs={{0,1},{1,2},{2,3},{3,0},{4,5},{5,6},{6,7},{7,4},{8,9},{9,10},{10,1... | collective-permute-start | bytes 1277960 | tf_op jit(solution)/shard_map/ppermute | solution.py:207
  27.7 16.4 %collective-permute-start.3 = (bf16[128,1664]{1,0:T(8,128)(2,1)}, bf16[128,1664]{1,0:T(8,128)(2,1)S(1)}, u32[]{:S(2)}, u32[]{:S(2)}) collective-permute-start(bf16[128,1664]{1,0:T(8,128)(2,1)} %collective-permute-done.2.refs_1_), channel_id=1, source_target_pairs={{0,3},{1,0},{2,1},{3,2},{4,7},{5,4},{6,5},{7,6},{8,11},{9,8},{10,9... | collective-permute-start | bytes 1277960 | tf_op jit(solution)/shard_map/ppermute | solution.py:208
  38.9 8.5 %slice-start = ((s8[4718592]{0:T(1024)(128)(4,1)}), s8[524288]{0:T(1024)(128)(4,1)S(1)}, s32[]{:S(2)}) async-start(s8[4718592]{0:T(1024)(128)(4,1)} %bitcast.51), calls=%async_computation | async-start | bytes 1048576
  55.0 3.9 %collective-permute-start.6 = (bf16[128,1536]{1,0:T(8,128)(2,1)S(1)}, bf16[128,1536]{1,0:T(8,128)(2,1)S(1)}, u32[]{:S(2)}, u32[]{:S(2)}) collective-permute-start(bf16[128,1536]{1,0:T(8,128)(2,1)S(1)} %dynamic-slice_convert_fusion), channel_id=1, source_target_pairs={{0,4},{4,0},{8,12},{12,8},{16,20},{20,16},{24,28},{28,24},{32,36},... | collective-permute-start | bytes 1179656 | tf_op jit(solution)/shard_map/ppermute | solution.py:228
  61.0 5.4 %collective-permute-start.7 = (bf16[32,1536]{1,0:T(8,128)(2,1)}, bf16[32,1536]{1,0:T(8,128)(2,1)S(1)}, u32[]{:S(2)}, u32[]{:S(2)}) collective-permute-start(bf16[32,1536]{1,0:T(8,128)(2,1)} %get-tuple-element.37), channel_id=1, source_target_pairs={{0,8},{4,12},{8,16},{12,20},{16,24},{20,28},{24,0},{28,4},{32,40},... | collective-permute-start | bytes 294920 | tf_op jit(solution)/shard_map/ppermute | solution.py:235
  62.2 7.3 %collective-permute-start.8 = (bf16[32,1536]{1,0:T(8,128)(2,1)}, bf16[32,1536]{1,0:T(8,128)(2,1)S(1)}, u32[]{:S(2)}, u32[]{:S(2)}) collective-permute-start(bf16[32,1536]{1,0:T(8,128)(2,1)} %get-tuple-element.36), channel_id=1, source_target_pairs={{0,16},{4,20},{8,24},{12,28},{16,0},{20,4},{24,8},{28,12},{32,48},... | collective-permute-start | bytes 294920 | tf_op jit(solution)/shard_map/ppermute | solution.py:235
  64.7 4.9 %collective-permute-start.9 = (bf16[32,1536]{1,0:T(8,128)(2,1)}, bf16[32,1536]{1,0:T(8,128)(2,1)S(1)}, u32[]{:S(2)}, u32[]{:S(2)}) collective-permute-start(bf16[32,1536]{1,0:T(8,128)(2,1)} %get-tuple-element.35), channel_id=1, source_target_pairs={{0,24},{4,28},{8,0},{12,4},{16,8},{20,12},{24,16},{28,20},{32,56},... | collective-permute-start | bytes 294920 | tf_op jit(solution)/shard_map/ppermute | solution.py:235
  70.2 5.0 %collective-permute-start.10 = (bf16[32,1536]{1,0:T(8,128)(2,1)}, bf16[32,1536]{1,0:T(8,128)(2,1)S(1)}, u32[]{:S(2)}, u32[]{:S(2)}) collective-permute-start(bf16[32,1536]{1,0:T(8,128)(2,1)} %fusion.26), channel_id=1, source_target_pairs={{0,32},{4,36},{8,40},{12,44},{16,48},{20,52},{24,56},{28,60},{32,6... | collective-permute-start | bytes 294920 | tf_op jit(solution)/shard_map/ppermute | solution.py:238
  71.5 6.4 %collective-permute-start.11 = (bf16[32,1536]{1,0:T(8,128)(2,1)}, bf16[32,1536]{1,0:T(8,128)(2,1)}, u32[]{:S(2)}, u32[]{:S(2)}) collective-permute-start(bf16[32,1536]{1,0:T(8,128)(2,1)} %fusion.26), channel_id=1, source_target_pairs={{0,64},{4,68},{8,72},{12,76},{16,80},{20,84},{24,88},{28,92},{32,9... | collective-permute-start | bytes 294920 | tf_op jit(solution)/shard_map/ppermute | solution.py:238
  74.1 4.9 %collective-permute-start.12 = (bf16[32,1536]{1,0:T(8,128)(2,1)}, bf16[32,1536]{1,0:T(8,128)(2,1)}, u32[]{:S(2)}, u32[]{:S(2)}) collective-permute-start(bf16[32,1536]{1,0:T(8,128)(2,1)} %fusion.26), channel_id=1, source_target_pairs={{0,96},{4,100},{8,104},{12,108},{16,112},{20,116},{24,120},{28,124... | collective-permute-start | bytes 294920 | tf_op jit(solution)/shard_map/ppermute | solution.py:238
  80.2 8.7 %copy-start.4 = (f32[256,1536]{1,0:T(8,128)S(1)}, f32[256,1536]{1,0:T(8,128)}, u32[]{:S(2)}) copy-start(f32[256,1536]{1,0:T(8,128)} %copy-done.3) | copy-start | bytes 4718596
  80.2 8.6 %collective-permute-start.14 = (bf16[32,1536]{1,0:T(8,128)(2,1)S(1)}, bf16[32,1536]{1,0:T(8,128)(2,1)S(1)}, u32[]{:S(2)}, u32[]{:S(2)}) collective-permute-start(bf16[32,1536]{1,0:T(8,128)(2,1)S(1)} %fusion.20), channel_id=1, source_target_pairs={{0,16},{4,20},{8,24},{12,28},{16,0},{20,4},{24,8},{28,12},{32,48},... | collective-permute-start | bytes 294920 | tf_op jit(solution)/shard_map/ppermute | solution.py:244
  82.8 6.0 %collective-permute-start.13 = (bf16[32,1536]{1,0:T(8,128)(2,1)S(1)}, bf16[32,1536]{1,0:T(8,128)(2,1)S(1)}, u32[]{:S(2)}, u32[]{:S(2)}) collective-permute-start(bf16[32,1536]{1,0:T(8,128)(2,1)S(1)} %get-tuple-element.32), channel_id=1, source_target_pairs={{0,8},{4,12},{8,16},{12,20},{16,24},{20,28},{24,0},{28,4},{32,40},... | collective-permute-start | bytes 294920 | tf_op jit(solution)/shard_map/ppermute | solution.py:244
  83.1 5.7 %collective-permute-start.15 = (bf16[32,1536]{1,0:T(8,128)(2,1)S(1)}, bf16[32,1536]{1,0:T(8,128)(2,1)S(1)}, u32[]{:S(2)}, u32[]{:S(2)}) collective-permute-start(bf16[32,1536]{1,0:T(8,128)(2,1)S(1)} %get-tuple-element.31), channel_id=1, source_target_pairs={{0,24},{4,28},{8,0},{12,4},{16,8},{20,12},{24,16},{28,20},{32,56},... | collective-permute-start | bytes 294920 | tf_op jit(solution)/shard_map/ppermute | solution.py:244
  86.7 6.7 %copy-start.8 = (bf16[128,1536]{1,0:T(8,128)(2,1)S(1)}, bf16[128,1536]{1,0:T(8,128)(2,1)}, u32[]{:S(2)}) copy-start(bf16[128,1536]{1,0:T(8,128)(2,1)} %copy-done.7) | copy-start | bytes 1179652
  89.0 4.4 %collective-permute-start.16 = (bf16[128,1536]{1,0:T(8,128)(2,1)S(1)}, bf16[128,1536]{1,0:T(8,128)(2,1)S(1)}, u32[]{:S(2)}, u32[]{:S(2)}) collective-permute-start(bf16[128,1536]{1,0:T(8,128)(2,1)S(1)} %fusion.2), channel_id=1, source_target_pairs={{0,4},{4,0},{8,12},{12,8},{16,20},{20,16},{24,28},{28,24},{32,36},... | collective-permute-start | bytes 1179656 | tf_op jit(solution)/shard_map/ppermute | solution.py:250
  (5 other events, 14.5 us)

commit v3 on v2

--- a/solution.py
+++ b/solution.py
@@ -29,11 +29,25 @@
     return jnp.dot(embedded, time_weight.astype(f32), precision=lax.Precision.HIGHEST)
 
 
+def message_kernel(x_ref, positions_ref, first_ref, second_ref):
+    rows = first_ref.shape[0]
+    lane = lax.broadcasted_iota(jnp.int32, (rows, HEAD), 1)
+    for at, out in ((0, first_ref), (rows, second_ref)):
+        ids = positions_ref[at : at + rows, :]
+        out[:, :D] = x_ref[at : at + rows, :]
+        out[:, D:] = jnp.where(lane == 0, ids >> 5, jnp.where(lane == 1, ids & 31, 0)).astype(f32).astype(bf16)
+
+
 def with_positions(x, positions):
-    lane = jnp.arange(HEAD, dtype=jnp.int32)[None, :]
-    high, low = (positions // 32)[:, None], (positions % 32)[:, None]
-    digits = jnp.where(lane == 0, high, jnp.where(lane == 1, low, 0))
-    return jnp.concatenate([x, digits.astype(bf16)], axis=1)
+    half = x.shape[0] // 2
+    vm = pl.BlockSpec(memory_space=pltpu.VMEM)
+    return pl.pallas_call(
+        message_kernel,
+        in_specs=[vm] * 2,
+        out_specs=[vm] * 2,
+        out_shape=[pltpu.VMEM((half, WIDE), bf16)] * 2,
+        compiler_params=pltpu.CompilerParams(vmem_limit_bytes=4 << 20),
+    )(x, positions[:, None])
 
 
 def rope_rates():
@@ -100,7 +114,7 @@
         cost_estimate=pl.CostEstimate(
             flops=2 * rows * D * D * groups, bytes_accessed=2 * D * D * groups, transcendentals=0
         ),
-        compiler_params=pltpu.CompilerParams(vmem_limit_bytes=VMEM),
+        compiler_params=pltpu.CompilerParams(vmem_limit_bytes=8 << 20),
     )(*xs, shift, scale, gains, rates, w_qkv)
 
 
@@ -146,13 +160,13 @@
         cost_estimate=pl.CostEstimate(
             flops=8 * rows * D * keys, bytes_accessed=4 * rows * D * 2, transcendentals=rows * keys * HEADS
         ),
-        compiler_params=pltpu.CompilerParams(vmem_limit_bytes=VMEM),
+        compiler_params=pltpu.CompilerParams(vmem_limit_bytes=10 << 20),
     )(q, *flat)
 
 
-def finish_kernel(n_kv, h_ref, q_ref, *refs):
+def finish_kernel(n_kv, h_ref, place_ref, q_ref, *refs):
     kv, refs = refs[: 2 * n_kv], refs[2 * n_kv :]
-    m_ref, l_ref, acc_ref, x_ref, gate_ref, w_ref, out_ref, attended = refs
+    m_ref, l_ref, acc_ref, x_ref, gate_ref, w_ref, out_ref, sent_ref, attended = refs
     for h in range(HEADS):
         at = slice(h * HEAD, (h + 1) * HEAD)
         q = q_ref[:, at]
@@ -178,101 +192,146 @@
         at = slice(t * TILE, (t + 1) * TILE)
         proj = jnp.dot(attended[...], w_ref[:, at], preferred_element_type=f32)
         out_ref[:, at] = size * (x_ref[:, at].astype(f32) + gate_ref[:, at] * proj)
-
-
-def finish(step_size, q, kvs, state, x, gate, w_out):
+    half = sent_ref.shape[0]
+    theirs = pl.ds(pl.multiple_of((1 - place_ref[0]) * half, half), half)
+    sent_ref[...] = out_ref[theirs, :].astype(bf16)
+
+
+def finish(step_size, place, q, kvs, state, x, gate, w_out):
     rows = q.shape[0]
     keys = sum(k.shape[0] for k, _ in kvs)
     flat = [a for pair in kvs for a in pair]
     vm = pl.BlockSpec(memory_space=pltpu.VMEM)
     return pl.pallas_call(
         functools.partial(finish_kernel, len(kvs)),
-        in_specs=[pl.BlockSpec(memory_space=pltpu.SMEM)]
+        in_specs=[pl.BlockSpec(memory_space=pltpu.SMEM)] * 2
         + [vm] * (1 + len(flat) + 3 + 3),
-        out_specs=vm,
-        out_shape=pltpu.VMEM((rows, D), f32),
+        out_specs=[vm] * 2,
+        out_shape=[pltpu.VMEM((rows, D), f32), pltpu.VMEM((rows // 2, D), bf16)],
         scratch_shapes=[pltpu.VMEM((rows, D), bf16)],
         cost_estimate=pl.CostEstimate(
             flops=8 * rows * D * keys + 2 * rows * D * D,
             bytes_accessed=2 * D * D,
             transcendentals=rows * keys * HEADS,
         ),
-        compiler_params=pltpu.CompilerParams(vmem_limit_bytes=VMEM),
-    )(step_size, q, *flat, *state, x, gate, w_out)
-
-
-def gather_states(first, second, n):
+        compiler_params=pltpu.CompilerParams(vmem_limit_bytes=6 << 20),
+    )(step_size, place, q, *flat, *state, x, gate, w_out)
+
+
+def split_kernel(place, inc, got, own, *pieces):
+    c, xx = place[0], place[1]
+    part = own.shape[0]
+    for k, out in enumerate((own,) + pieces):
+        at = pl.multiple_of(((xx + k) & 3) * part, part)
+        both = inc[pl.ds(pl.multiple_of(c * 4 * part, part) + at, part), :] + got[pl.ds(at, part), :].astype(f32)
+        out[...] = both.astype(out.dtype)
+
+
+def row_kernel(own, one, two, three, out):
+    out[...] = (own[...] + one[...].astype(f32) + two[...].astype(f32) + three[...].astype(f32)).astype(bf16)
+
+
+def before_kernel(place, own, *refs):
+    xs, ys, outs = refs[:3], refs[3:6], refs[6:]
+    xx, yy = place[1], place[2]
+    above = jnp.zeros(own.shape, f32)
+    for k in (1, 2, 3):
+        above = above + jnp.where(((yy - k) & 3) < yy, ys[k - 1][...].astype(f32), 0.0)
+    src = [own[...]] + [r[...].astype(f32) for r in xs]
+    for k, out in enumerate(outs):
+        total = above
+        for j in range(4):
+            total = total + jnp.where(((xx - j) & 3) < ((xx + k) & 3), src[j], 0.0)
+        out[...] = total.astype(out.dtype)
+
+
+def join_kernel(place, inc, got, *refs):
+    pieces, (own, given) = refs[:4], refs[4:]
+    c, xx = place[0], place[1]
+    part = pieces[0].shape[0]
+    for k in range(4):
+        at = pl.multiple_of(((xx - k) & 3) * part, part)
+        mine = inc[pl.ds(pl.multiple_of(c * 4 * part, part) + at, part), :]
+        theirs = got[pl.ds(at, part), :].astype(f32)
+        entering = pieces[k][...].astype(f32)
+        even = entering + jnp.where(c == 0, mine, theirs)
+        own[pl.ds(at, part), :] = jnp.where(c == 0, even, even + mine)
+        given[pl.ds(at, part), :] = jnp.where(c == 0, even, entering).astype(bf16)
+
+
+def last_kernel(place, inc, own, other, out):
+    c, half = place[0], own.shape[0]
+    at = pl.multiple_of(c * half, half)
+    rest = pl.multiple_of((1 - c) * half, half)
+    out[pl.ds(at, half), :] = own[...]
+    out[pl.ds(rest, half), :] = other[...].astype(f32) + inc[pl.ds(rest, half), :]
+
+
+def small_call(kernel, place, args, outs):
+    vm = pl.BlockSpec(memory_space=pltpu.VMEM)
+    head = [] if place is None else [place]
+    return pl.pallas_call(
+        kernel,
+        in_specs=[pl.BlockSpec(memory_space=pltpu.SMEM)] * len(head) + [vm] * len(args),
+        out_specs=[vm] * len(outs),
+        out_shape=outs,
+        compiler_params=pltpu.CompilerParams(vmem_limit_bytes=3 << 20),
+    )(*head, *args)
+
+
+def scan_steps(place, inc, sent):
+    rows = inc.shape[0]
+    half, part = rows // 2, rows // 8
+    pair = [(i, i ^ 1) for i in range(32)]
+    ring = range(4)
+
+    def along_x(k):
+        return [((y * 4 + x) * 2 + c, (y * 4 + (x + k) % 4) * 2 + c) for y in ring for x in ring for c in (0, 1)]
+
+    def along_y(k):
+        return [((y * 4 + x) * 2 + c, ((y + k) % 4 * 4 + x) * 2 + c) for y in ring for x in ring for c in (0, 1)]
+
+    narrow, wide = pltpu.VMEM((part, D), bf16), pltpu.VMEM((part, D), f32)
+    got = lax.ppermute(sent, "step", pair)
+    own, *pieces = small_call(split_kernel, place, (inc, got), [wide] + [narrow] * 3)
+    xs = [lax.ppermute(piece, "step", along_x(k)) for k, piece in zip((1, 2, 3), pieces)]
+    (row,) = small_call(row_kernel, None, (own, *xs), [narrow])
+    ys = [lax.ppermute(row, "step", along_y(k)) for k in (1, 2, 3)]
+    home, *away = small_call(before_kernel, place, (own, *xs, *ys), [wide] + [narrow] * 3)
+    back = [lax.ppermute(piece, "step", along_x(k)) for k, piece in zip((1, 2, 3), away)]
+    done, given = small_call(
+        join_kernel, place, (inc, got, home, *back), [pltpu.VMEM((half, D), f32), pltpu.VMEM((half, D), bf16)]
+    )
+    other = lax.ppermute(given, "step", pair)
+    return small_call(last_kernel, place, (inc, done, other), [jax.ShapeDtypeStruct((rows, D), f32)])[0]
+
+
+def on_device(states, step_times, positions, w_qkv, qk_gain, w_out, time_weight):
+    n = lax.axis_size("seq")
     right = [(i, (i + 1) % n) for i in range(n)]
     left = [(i, (i - 1) % n) for i in range(n)]
     to_right = lambda v: lax.ppermute(v, "seq", right)
     to_left = lambda v: lax.ppermute(v, "seq", left)
+    step = lax.axis_index("step")
+    place = jnp.stack([step % 2, (step // 2) % 4, step // 8])
+
+    x = states[0]
+    first, second = with_positions(x, positions)
     r_first, l_second = to_right(first), to_left(second)
-    r_second, l_first = to_right(second), to_left(first)
-    return (r_first, l_second), (r_second, l_first), (to_right(r_first), to_left(l_second))
-
-
-def scan_steps(inc):
-    rows = inc.shape[0]
-    half, part = rows // 2, rows // 8
-    step = lax.axis_index("step")
-    c, xx, yy = step % 2, (step // 2) % 4, step // 8
-    pair = [(i, i ^ 1) for i in range(32)]
-
-    def along_x(k):
-        return [((y * 4 + x) * 2 + c, (y * 4 + (x + k) % 4) * 2 + c) for y in range(4) for x in range(4) for c in range(2)]
-
-    def along_y(k):
-        return [((y * 4 + x) * 2 + c, ((y + k) % 4 * 4 + x) * 2 + c) for y in range(4) for x in range(4) for c in range(2)]
-
-    sent = lax.dynamic_slice_in_dim(inc, (1 - c) * half, half).astype(bf16)
-    got = lax.ppermute(sent, "step", pair).astype(f32)
-    mine = lax.dynamic_slice_in_dim(inc, c * half, half)
-    both = (mine + got).reshape(4, part, D)
-    narrow = both.astype(bf16)
-    src = [lax.dynamic_index_in_dim(both, xx, 0, keepdims=False)]
-    for k in (1, 2, 3):
-        piece = lax.dynamic_index_in_dim(narrow, (xx + k) % 4, 0, keepdims=False)
-        src.append(lax.ppermute(piece, "step", along_x(k)).astype(f32))
-    row = src[0] + src[1] + src[2] + src[3]
-    row_b = row.astype(bf16)
-    rows_y = [lax.ppermute(row_b, "step", along_y(k)) for k in (1, 2, 3)]
-    above = sum(jnp.where((yy - k) % 4 < yy, rows_y[k - 1].astype(f32), 0.0) for k in (1, 2, 3))
-    before = []
-    for k in range(4):
-        target = (xx + k) % 4
-        before.append(above + sum(jnp.where((xx - j) % 4 < target, src[j], 0.0) for j in range(4)))
-    back = [before[0]] + [lax.ppermute(before[k].astype(bf16), "step", along_x(k)).astype(f32) for k in (1, 2, 3)]
-    entering = jnp.zeros((4, part, D), f32)
-    for k in range(4):
-        entering = lax.dynamic_update_index_in_dim(entering, back[k], (xx - k) % 4, 0)
-    entering = entering.reshape(half, D)
-    given = jnp.where(c == 0, entering + mine, entering)
-    other = lax.ppermute(given.astype(bf16), "step", pair).astype(f32)
-    own = jnp.where(c == 0, given, entering + got + mine)
-    rest = other + lax.dynamic_slice_in_dim(inc, (1 - c) * half, half)
-    return jnp.concatenate([jnp.where(c == 0, own, rest), jnp.where(c == 0, rest, own)])
-
-
-def on_device(states, step_times, positions, w_qkv, qk_gain, w_out, time_weight):
-    n = lax.axis_size("seq")
-    x = states[0]
-    half = x.shape[0] // 2
-    message = with_positions(x, positions)
-    own = (message[:half], message[half:])
-    chunks = gather_states(*own, n)
-
-    modulated = modulation(step_times, time_weight)
+    step_size = (step_times[:, 1:] - step_times[:, :1]).astype(f32) / 1000.0
+    ready = (modulation(step_times, time_weight), rope_rates(), step_size, place, second, first)
+    modulated, rates, step_size, place, second_later, first_later = lax.optimization_barrier(ready)
+    r_second, l_first = to_right(second_later), to_left(first_later)
+    forward = to_right(r_first), to_left(l_second)
     shift, scale, gate = modulated[:, :D], modulated[:, D : 2 * D], modulated[:, 2 * D :]
-    rates = rope_rates()
-
-    q, k, v = project(own, shift, scale, qk_gain, rates, w_qkv, True)
+
+    q, k, v = project((first_later, second_later), shift, scale, qk_gain, rates, w_qkv, True)
     kvs = [(k, v)]
-    for chunk in chunks:
+    for chunk in ((r_first, l_second), (r_second, l_first), forward):
         kvs.append(tuple(project(chunk, shift, scale, qk_gain, rates, w_qkv, False)))
     state = attend(q, kvs[:3])
-    step_size = (step_times[:, 1:] - step_times[:, :1]).astype(f32) / 1000.0
-    inc = finish(step_size, q, kvs[3:], state, x, gate, w_out)
-    return scan_steps(inc)[None]
+    inc, sent = finish(step_size, place, q, kvs[3:], state, x, gate, w_out)
+    return scan_steps(place, inc, sent)[None]
 
 
 def solution(mesh):

time: 95.2 us -> 86.5 us (0.909)
  other arithmetic: 9.25 us -> 0.15 us
  Pallas kernels: 27.7 us -> 32.4 us
  waiting for transfers between devices: 17.3 us -> 12.8 us
    pallas_call x0 -> x6, Pallas kernels: none -> 5.12 us  [the longest x5 4.11 us: small_call(): pl.pallas_call(kernel, in_specs=[pl.BlockSpec(memory_space=pltpu.SMEM)] *...]
    ppermute x17, waiting for transfers between devices: 17.3 us -> 12.8 us  [the longest x6 6.5 us: scan_steps(): lax.ppermute(piece, 'step', along_x(k))]
    convert_element_type x6 -> x0, other arithmetic: 3.16 us -> none  [the longest x2 2.2 us: scan_steps(): before[k].astype(bf16)]
    add x1 -> x0, other arithmetic: 1.34 us -> none  [scan_steps(): both = (mine + got).reshape(4, part, D)]
    broadcast_in_dim x1 -> x0, other arithmetic: 1.25 us -> none  [on_device(): return scan_steps(inc)[None]]
    concatenate x1 -> x0, other arithmetic: 1.18 us -> none  [with_positions(): return jnp.concatenate([x, digits.astype(bf16)], axis=1)]
    select_n x2 -> x0, other arithmetic: 1.13 us -> none  [the longest x1 0.84 us: with_positions(): high, low = ((positions // 32)[:, None], (positions % 32)[:, None])]
    dynamic_update_slice x4 -> x0, other arithmetic: 1.12 us -> none  [scan_steps(): lax.dynamic_update_index_in_dim(entering, back[k], (xx - k) % 4, 0)]
  transfers between devices with their start and end apart: 17 -> 17, of which waited for: 8 -> 8; matrix products, arithmetic and copies ran while one was open for 4% -> 3% of each run, Pallas kernels for 19% -> 20%
where the time goes in v3:
time: 86.5 us; the launch traced here: 86.3 us
  Pallas kernels  32.4 us (37%)
  starting transfers between devices  29.4 us (34%)
  waiting for transfers between devices  12.8 us (15%)
  local copies, waits for them, and re-layouts  8.53 us (10%)
  between operations  2.03 us (2%)
  matrix products  1.02 us (1%)
    pallas_call x4, Pallas kernels, project(): pl.pallas_call(functools.partial(project_kernel, with_q), in_specs=[vm] *...  15.3 us
    ppermute x6, starting transfers between devices, scan_steps(): lax.ppermute(piece, 'step', along_x(k))  8.56 us
    ppermute x3, starting transfers between devices, on_device(): to_left = lambda v: lax.ppermute(v, 'seq', left)  7.46 us
    pallas_call x1, Pallas kernels, finish(): pl.pallas_call(functools.partial(finish_kernel, len(kvs)), in_specs=[pl.B...  6.92 us
    ppermute x6, waiting for transfers between devices, scan_steps(): lax.ppermute(piece, 'step', along_x(k))  6.5 us
    unnamed x16, local copies, waits for them, and re-layouts  6.19 us
    pallas_call x1, Pallas kernels, attend(): pl.pallas_call(functools.partial(attend_kernel, len(kvs)), in_specs=[vm]...  5.06 us
    ppermute x3, starting transfers between devices, scan_steps(): ys = [lax.ppermute(row, 'step', along_y(k)) for k in (1, 2, 3)]  5.05 us
  transfers between devices with their start and end apart: 17, of which 8 were waited for; matrix products, arithmetic and copies ran while one was open for 3% of the time, Pallas kernels for 20%

profile of v3, /device:TPU:1, one launch (start us, length us, event | category | flops | bytes accessed | tf_op | source)
XLA Modules:
  0.0 86.3 jit_solution(5487782651346206157)
XLA Ops:
  3.1 2.5 %collective-permute-start = (bf16[128,1664]{1,0:T(8,128)(2,1)}, bf16[128,1664]{1,0:T(8,128)(2,1)S(1)}, u32[]{:S(2)}, u32[]{:S(2)}) collective-permute-start(bf16[128,1664]{1,0:T(8,128)(2,1)} %get-tuple-element.41.refs_0_), channel_id=1, source_target_pairs={{0,1},{1,2},{2,3},{3,0},{4,5},{5,6},{6,7},{7,4},{8,9},{9,10},{10,1... | collective-permute-start | bytes 1277960 | tf_op jit(solution)/shard_map/ppermute | solution.py:313
  5.6 2.1 %collective-permute-start.2 = (bf16[128,1664]{1,0:T(8,128)(2,1)}, bf16[128,1664]{1,0:T(8,128)(2,1)S(1)}, u32[]{:S(2)}, u32[]{:S(2)}) collective-permute-start(bf16[128,1664]{1,0:T(8,128)(2,1)} %get-tuple-element.42.refs_1_), channel_id=1, source_target_pairs={{0,3},{1,0},{2,1},{3,2},{4,7},{5,4},{6,5},{7,6},{8,11},{9,8},{10,9... | collective-permute-start | bytes 1277960 | tf_op jit(solution)/shard_map/ppermute | solution.py:314
  7.7 1.4 %fusion.10 = (s32[1,1]{1,0:T(1,128)}, s32[1,1]{1,0:T(1,128)}) fusion(s32[1,2]{1,0:T(1,128)} %param.8), kind=kLoop, calls=%fused_computation.16 | loop fusion | bytes 16 | tf_op jit(solution)/shard_map/slice | solution.py:321
  12.1 2.7 %collective-permute-start.5 = (bf16[128,1664]{1,0:T(8,128)(2,1)}, bf16[128,1664]{1,0:T(8,128)(2,1)S(1)}, u32[]{:S(2)}, u32[]{:S(2)}) collective-permute-start(bf16[128,1664]{1,0:T(8,128)(2,1)} %get-tuple-element.41.refs_0_), channel_id=1, source_target_pairs={{0,3},{1,0},{2,1},{3,2},{4,7},{5,4},{6,5},{7,6},{8,11},{9,8},{10,9... | collective-permute-start | bytes 1277960 | tf_op jit(solution)/shard_map/ppermute | solution.py:314
  14.8 5.0 %copy-done.1 = bf16[1536,4608]{1,0:T(8,128)(2,1)S(1)} copy-done((bf16[1536,4608]{1,0:T(8,128)(2,1)S(1)}, bf16[1536,4608]{1,0:T(8,128)(2,1)}, u32[]{:S(2)}) %copy-start.1) | copy-done | bytes 14155800
  19.8 5.7 %shard_map.74 = (bf16[256,1536]{1,0:T(8,128)(2,1)S(1)}, bf16[256,1536]{1,0:T(8,128)(2,1)S(1)}, bf16[256,1536]{1,0:T(8,128)(2,1)S(1)}) custom-call(bf16[128,1664]{1,0:T(8,128)(2,1)} %get-tuple-element.41.refs_0_, bf16[128,1664]{1,0:T(8,128)(2,1)} %get-tuple-element.42.refs_1_, f32[1,1536]{1,0:T(1,128)S(1)} %get-tuple-element.71.refs_2_, ...), custom_call_target="tpu_custom_call" | custom-call | flops 3623878656 | bytes 14155776 | tf_op jit(solution)/shard_map/pallas_call | solution.py:108
  25.6 2.7 %collective-permute-start.3 = (bf16[128,1664]{1,0:T(8,128)(2,1)S(1)}, bf16[128,1664]{1,0:T(8,128)(2,1)S(1)}, u32[]{:S(2)}, u32[]{:S(2)}) collective-permute-start(bf16[128,1664]{1,0:T(8,128)(2,1)S(1)} %collective-permute-done.2.refs_1_), channel_id=1, source_target_pairs={{0,3},{1,0},{2,1},{3,2},{4,7},{5,4},{6,5},{7,6},{8,11},{9,8},{10,9... | collective-permute-start | bytes 1277960 | tf_op jit(solution)/shard_map/ppermute | solution.py:314
  28.2 3.1 %shard_map.76 = (bf16[256,1536]{1,0:T(8,128)(2,1)S(1)}, bf16[256,1536]{1,0:T(8,128)(2,1)S(1)}) custom-call(bf16[128,1664]{1,0:T(8,128)(2,1)S(1)} %collective-permute-done.refs_0_, bf16[128,1664]{1,0:T(8,128)(2,1)S(1)} %collective-permute-done.2.refs_1_, f32[1,1536]{1,0:T(1,128)S(1)} %get-tuple-element.71.refs_2_, f32[1,1536]{1,0:T(1,128)S(1)} %get-tuple-element.70.refs_3_, ...), custom_call_target="tpu_custom_call" | custom-call | flops 2415919104 | bytes 9437184 | tf_op jit(solution)/shard_map/pallas_call | solution.py:108
  31.4 3.1 %shard_map.77 = (bf16[256,1536]{1,0:T(8,128)(2,1)S(1)}, bf16[256,1536]{1,0:T(8,128)(2,1)S(1)}) custom-call(bf16[128,1664]{1,0:T(8,128)(2,1)S(1)} %collective-permute-done.4.refs_0_, bf16[128,1664]{1,0:T(8,128)(2,1)S(1)} %collective-permute-done.5.refs_1_, f32[1,1536]{1,0:T(1,128)S(1)} %get-tuple-element.71.refs_2_, f32[1,1536]{1,0:T(1,128)S(1)} %get-tuple-element.70.refs_3_, ...), custom_call_target="tpu_custom_call" | custom-call | flops 2415919104 | bytes 9437184 | tf_op jit(solution)/shard_map/pallas_call | solution.py:108
  34.6 5.1 %shard_map.78 = (f32[256,128]{1,0:T(8,128)S(1)}, f32[256,128]{1,0:T(8,128)S(1)}, f32[256,1536]{1,0:T(8,128)S(1)}) custom-call(bf16[256,1536]{1,0:T(8,128)(2,1)S(1)} %get-tuple-element.45.q_ref, bf16[256,1536]{1,0:T(8,128)(2,1)S(1)} %get-tuple-element.48.refs_0_, bf16[256,1536]{1,0:T(8,128)(2,1)S(1)} %get-tuple-element.49.refs_1_, ...), custom_call_target="tpu_custom_call" | custom-call | flops 2415919104 | bytes 3145728 | tf_op jit(solution)/shard_map/pallas_call | solution.py:151
  39.7 3.4 %shard_map.75 = (bf16[256,1536]{1,0:T(8,128)(2,1)S(1)}, bf16[256,1536]{1,0:T(8,128)(2,1)S(1)}) custom-call(bf16[128,1664]{1,0:T(8,128)(2,1)S(1)} %collective-permute-done.1.refs_0_, bf16[128,1664]{1,0:T(8,128)(2,1)S(1)} %collective-permute-done.3.refs_1_, f32[1,1536]{1,0:T(1,128)S(1)} %get-tuple-element.71.refs_2_, f32[1,1536]{1,0:T(1,128)S(1)} %get-tuple-element.70.refs_3_, ...), custom_call_target="tpu_custom_call" | custom-call | flops 2415919104 | bytes 9437184 | tf_op jit(solution)/shard_map/pallas_call | solution.py:108
  43.1 6.9 %shard_map.79 = (f32[256,1536]{1,0:T(8,128)S(1)}, bf16[128,1536]{1,0:T(8,128)(2,1)S(1)}) custom-call(f32[1,1]{1,0:T(1,128)S(6)} %div.34.h_ref, s32[3]{0:T(128)S(1)} %pad_add_fusion.place_ref.place, bf16[256,1536]{1,0:T(8,128)(2,1)S(1)} %get-tuple-element.45.q_ref, bf16[256,1536]{1,0:T(8,128)(2,1)S(1)} %get-tuple-element.46.refs_0_, ...), custom_call_target="tpu_custom_call" | custom-call | flops 2013265920 | bytes 4718592 | tf_op jit(solution)/shard_map/pallas_call | solution.py:205
  50.0 2.2 %collective-permute-start.6 = (bf16[128,1536]{1,0:T(8,128)(2,1)S(1)}, bf16[128,1536]{1,0:T(8,128)(2,1)S(1)}, u32[]{:S(2)}, u32[]{:S(2)}) collective-permute-start(bf16[128,1536]{1,0:T(8,128)(2,1)S(1)} %get-tuple-element.58), channel_id=1, source_target_pairs={{0,4},{4,0},{8,12},{12,8},{16,20},{20,16},{24,28},{28,24},{32,36},... | collective-permute-start | bytes 1179656 | tf_op jit(solution)/shard_map/ppermute | solution.py:295
  52.2 1.3 %collective-permute-done.6.got = bf16[128,1536]{1,0:T(8,128)(2,1)S(1)} collective-permute-done((bf16[128,1536]{1,0:T(8,128)(2,1)S(1)}, bf16[128,1536]{1,0:T(8,128)(2,1)S(1)}, u32[]{:S(2)}, u32[]{:S(2)}) %collective-permute-start.6) | collective-permute-done | bytes 393248 | tf_op jit(solution)/shard_map/ppermute | solution.py:295
  55.4 2.5 %collective-permute-start.8 = (bf16[32,1536]{1,0:T(8,128)(2,1)S(1)}, bf16[32,1536]{1,0:T(8,128)(2,1)S(1)}, u32[]{:S(2)}, u32[]{:S(2)}) collective-permute-start(bf16[32,1536]{1,0:T(8,128)(2,1)S(1)} %get-tuple-element.61), channel_id=1, source_target_pairs={{0,16},{4,20},{8,24},{12,28},{16,0},{20,4},{24,8},{28,12},{32,48},... | collective-permute-start | bytes 294920 | tf_op jit(solution)/shard_map/ppermute | solution.py:297
  59.4 3.1 %collective-permute-done.8.two.refs_1_ = bf16[32,1536]{1,0:T(8,128)(2,1)S(1)} collective-permute-done((bf16[32,1536]{1,0:T(8,128)(2,1)S(1)}, bf16[32,1536]{1,0:T(8,128)(2,1)S(1)}, u32[]{:S(2)}, u32[]{:S(2)}) %collective-permute-start.8) | collective-permute-done | bytes 98336 | tf_op jit(solution)/shard_map/ppermute | solution.py:297
  62.6 1.4 %collective-permute-start.10 = (bf16[32,1536]{1,0:T(8,128)(2,1)S(1)}, bf16[32,1536]{1,0:T(8,128)(2,1)S(1)}, u32[]{:S(2)}, u32[]{:S(2)}) collective-permute-start(bf16[32,1536]{1,0:T(8,128)(2,1)S(1)} %shard_map.81), channel_id=1, source_target_pairs={{0,32},{4,36},{8,40},{12,44},{16,48},{20,52},{24,56},{28,60},{32,6... | collective-permute-start | bytes 294920 | tf_op jit(solution)/shard_map/ppermute | solution.py:299
  64.0 2.6 %collective-permute-start.11 = (bf16[32,1536]{1,0:T(8,128)(2,1)S(1)}, bf16[32,1536]{1,0:T(8,128)(2,1)S(1)}, u32[]{:S(2)}, u32[]{:S(2)}) collective-permute-start(bf16[32,1536]{1,0:T(8,128)(2,1)S(1)} %shard_map.81), channel_id=1, source_target_pairs={{0,64},{4,68},{8,72},{12,76},{16,80},{20,84},{24,88},{28,92},{32,9... | collective-permute-start | bytes 294920 | tf_op jit(solution)/shard_map/ppermute | solution.py:299
  67.7 2.4 %collective-permute-done.11.refs_4_ = bf16[32,1536]{1,0:T(8,128)(2,1)S(1)} collective-permute-done((bf16[32,1536]{1,0:T(8,128)(2,1)S(1)}, bf16[32,1536]{1,0:T(8,128)(2,1)S(1)}, u32[]{:S(2)}, u32[]{:S(2)}) %collective-permute-start.11) | collective-permute-done | bytes 98336 | tf_op jit(solution)/shard_map/ppermute | solution.py:299
  72.5 2.2 %collective-permute-start.14 = (bf16[32,1536]{1,0:T(8,128)(2,1)S(1)}, bf16[32,1536]{1,0:T(8,128)(2,1)S(1)}, u32[]{:S(2)}, u32[]{:S(2)}) collective-permute-start(bf16[32,1536]{1,0:T(8,128)(2,1)S(1)} %get-tuple-element.65), channel_id=1, source_target_pairs={{0,16},{4,20},{8,24},{12,28},{16,0},{20,4},{24,8},{28,12},{32,48},... | collective-permute-start | bytes 294920 | tf_op jit(solution)/shard_map/ppermute | solution.py:301
  75.7 2.1 %collective-permute-done.13.refs_1_ = bf16[32,1536]{1,0:T(8,128)(2,1)S(1)} collective-permute-done((bf16[32,1536]{1,0:T(8,128)(2,1)S(1)}, bf16[32,1536]{1,0:T(8,128)(2,1)S(1)}, u32[]{:S(2)}, u32[]{:S(2)}) %collective-permute-start.13) | collective-permute-done | bytes 98336 | tf_op jit(solution)/shard_map/ppermute | solution.py:301
  79.5 3.6 %collective-permute-start.16 = (bf16[128,1536]{1,0:T(8,128)(2,1)S(1)}, bf16[128,1536]{1,0:T(8,128)(2,1)S(1)}, u32[]{:S(2)}, u32[]{:S(2)}) collective-permute-start(bf16[128,1536]{1,0:T(8,128)(2,1)S(1)} %get-tuple-element.68), channel_id=1, source_target_pairs={{0,4},{4,0},{8,12},{12,8},{16,20},{20,16},{24,28},{28,24},{32,36},... | collective-permute-start | bytes 1179656 | tf_op jit(solution)/shard_map/ppermute | solution.py:305
  83.1 1.3 %collective-permute-done.16.other = bf16[128,1536]{1,0:T(8,128)(2,1)S(1)} collective-permute-done((bf16[128,1536]{1,0:T(8,128)(2,1)S(1)}, bf16[128,1536]{1,0:T(8,128)(2,1)S(1)}, u32[]{:S(2)}, u32[]{:S(2)}) %collective-permute-start.16) | collective-permute-done | bytes 393248 | tf_op jit(solution)/shard_map/ppermute | solution.py:305
  84.5 1.8 %shard_map.84 = f32[256,1536]{1,0:T(8,128)} custom-call(s32[3]{0:T(128)S(1)} %pad_add_fusion.place_ref.place, f32[256,1536]{1,0:T(8,128)S(1)} %get-tuple-element.57.inc, f32[128,1536]{1,0:T(8,128)S(1)} %get-tuple-element.67.own, bf16[128,1536]{1,0:T(8,128)(2,1)S(1)} %collective-permute-done.16.other), custom_call_target="tpu_custom_call" | custom-call | tf_op jit(solution)/shard_map/pallas_call | solution.py:273
  (47 shorter events, 14.1 us)
Async XLA Ops:
  0.0 11.1 %copy-start = (bf16[256,4608]{1,0:T(8,128)(2,1)S(1)}, bf16[256,4608]{1,0:T(8,128)(2,1)}, u32[]{:S(2)}) copy-start(bf16[256,4608]{1,0:T(8,128)(2,1)} %param.13) | copy-start | bytes 7077892
  0.0 14.8 %copy-start.5 = (f32[2,1536]{1,0:T(2,128)S(1)}, f32[2,1536]{1,0:T(2,128)}, u32[]{:S(2)}) copy-start(f32[2,1536]{1,0:T(2,128)} %refs_4_.7) | copy-start | bytes 36868
  3.1 22.4 %collective-permute-start = (bf16[128,1664]{1,0:T(8,128)(2,1)}, bf16[128,1664]{1,0:T(8,128)(2,1)S(1)}, u32[]{:S(2)}, u32[]{:S(2)}) collective-permute-start(bf16[128,1664]{1,0:T(8,128)(2,1)} %get-tuple-element.41.refs_0_), channel_id=1, source_target_pairs={{0,1},{1,2},{2,3},{3,0},{4,5},{5,6},{6,7},{7,4},{8,9},{9,10},{10,1... | collective-permute-start | bytes 1277960 | tf_op jit(solution)/shard_map/ppermute | solution.py:313
  5.6 20.0 %collective-permute-start.2 = (bf16[128,1664]{1,0:T(8,128)(2,1)}, bf16[128,1664]{1,0:T(8,128)(2,1)S(1)}, u32[]{:S(2)}, u32[]{:S(2)}) collective-permute-start(bf16[128,1664]{1,0:T(8,128)(2,1)} %get-tuple-element.42.refs_1_), channel_id=1, source_target_pairs={{0,3},{1,0},{2,1},{3,2},{4,7},{5,4},{6,5},{7,6},{8,11},{9,8},{10,9... | collective-permute-start | bytes 1277960 | tf_op jit(solution)/shard_map/ppermute | solution.py:314
  12.1 19.3 %collective-permute-start.4 = (bf16[128,1664]{1,0:T(8,128)(2,1)}, bf16[128,1664]{1,0:T(8,128)(2,1)S(1)}, u32[]{:S(2)}, u32[]{:S(2)}) collective-permute-start(bf16[128,1664]{1,0:T(8,128)(2,1)} %get-tuple-element.42.refs_1_), channel_id=1, source_target_pairs={{0,1},{1,2},{2,3},{3,0},{4,5},{5,6},{6,7},{7,4},{8,9},{9,10},{10,1... | collective-permute-start | bytes 1277960 | tf_op jit(solution)/shard_map/ppermute | solution.py:313
  12.1 19.3 %collective-permute-start.5 = (bf16[128,1664]{1,0:T(8,128)(2,1)}, bf16[128,1664]{1,0:T(8,128)(2,1)S(1)}, u32[]{:S(2)}, u32[]{:S(2)}) collective-permute-start(bf16[128,1664]{1,0:T(8,128)(2,1)} %get-tuple-element.41.refs_0_), channel_id=1, source_target_pairs={{0,3},{1,0},{2,1},{3,2},{4,7},{5,4},{6,5},{7,6},{8,11},{9,8},{10,9... | collective-permute-start | bytes 1277960 | tf_op jit(solution)/shard_map/ppermute | solution.py:314
  14.8 5.0 %copy-start.1 = (bf16[1536,4608]{1,0:T(8,128)(2,1)S(1)}, bf16[1536,4608]{1,0:T(8,128)(2,1)}, u32[]{:S(2)}) copy-start(bf16[1536,4608]{1,0:T(8,128)(2,1)} %refs_6_.7) | copy-start | bytes 42467332
  19.8 8.4 %copy-start.2 = (bf16[1536,4608]{1,0:T(8,128)(2,1)S(1)}, bf16[1536,4608]{1,0:T(8,128)(2,1)}, u32[]{:S(2)}) copy-start(bf16[1536,4608]{1,0:T(8,128)(2,1)} %refs_6_.7) | copy-start | bytes 42467332
  25.5 14.2 %collective-permute-start.1 = (bf16[128,1664]{1,0:T(8,128)(2,1)S(1)}, bf16[128,1664]{1,0:T(8,128)(2,1)S(1)}, u32[]{:S(2)}, u32[]{:S(2)}) collective-permute-start(bf16[128,1664]{1,0:T(8,128)(2,1)S(1)} %collective-permute-done.refs_0_), channel_id=1, source_target_pairs={{0,1},{1,2},{2,3},{3,0},{4,5},{5,6},{6,7},{7,4},{8,9},{9,10},{10,1... | collective-permute-start | bytes 1277960 | tf_op jit(solution)/shard_map/ppermute | solution.py:313
  25.6 14.1 %collective-permute-start.3 = (bf16[128,1664]{1,0:T(8,128)(2,1)S(1)}, bf16[128,1664]{1,0:T(8,128)(2,1)S(1)}, u32[]{:S(2)}, u32[]{:S(2)}) collective-permute-start(bf16[128,1664]{1,0:T(8,128)(2,1)S(1)} %collective-permute-done.2.refs_1_), channel_id=1, source_target_pairs={{0,3},{1,0},{2,1},{3,2},{4,7},{5,4},{6,5},{7,6},{8,11},{9,8},{10,9... | collective-permute-start | bytes 1277960 | tf_op jit(solution)/shard_map/ppermute | solution.py:314
  34.5 8.5 %slice-start = ((s8[4718592]{0:T(1024)(128)(4,1)}), s8[4194304]{0:T(1024)(128)(4,1)S(1)}, s32[]{:S(2)}) async-start(s8[4718592]{0:T(1024)(128)(4,1)} %bitcast.12), calls=%async_computation | async-start | bytes 8388608
  39.6 3.4 %slice-start.1 = ((s8[4718592]{0:T(1024)(128)(4,1)}), s8[524288]{0:T(1024)(128)(4,1)S(1)}, s32[]{:S(2)}) async-start(s8[4718592]{0:T(1024)(128)(4,1)} %bitcast.12), calls=%async_computation.1 | async-start | bytes 1048576
  39.6 3.4 %copy-start.4 = (bf16[1,256,1536]{2,1,0:T(8,128)(2,1)S(1)}, bf16[1,256,1536]{2,1,0:T(8,128)(2,1)}, u32[]{:S(2)}) copy-start(bf16[1,256,1536]{2,1,0:T(8,128)(2,1)} %param.7) | copy-start | bytes 2359300
  50.0 3.5 %collective-permute-start.6 = (bf16[128,1536]{1,0:T(8,128)(2,1)S(1)}, bf16[128,1536]{1,0:T(8,128)(2,1)S(1)}, u32[]{:S(2)}, u32[]{:S(2)}) collective-permute-start(bf16[128,1536]{1,0:T(8,128)(2,1)S(1)} %get-tuple-element.58), channel_id=1, source_target_pairs={{0,4},{4,0},{8,12},{12,8},{16,20},{20,16},{24,28},{28,24},{32,36},... | collective-permute-start | bytes 1179656 | tf_op jit(solution)/shard_map/ppermute | solution.py:295
  54.2 5.3 %collective-permute-start.7 = (bf16[32,1536]{1,0:T(8,128)(2,1)S(1)}, bf16[32,1536]{1,0:T(8,128)(2,1)S(1)}, u32[]{:S(2)}, u32[]{:S(2)}) collective-permute-start(bf16[32,1536]{1,0:T(8,128)(2,1)S(1)} %get-tuple-element.60), channel_id=1, source_target_pairs={{0,8},{4,12},{8,16},{12,20},{16,24},{20,28},{24,0},{28,4},{32,40},... | collective-permute-start | bytes 294920 | tf_op jit(solution)/shard_map/ppermute | solution.py:297
  55.4 7.1 %collective-permute-start.8 = (bf16[32,1536]{1,0:T(8,128)(2,1)S(1)}, bf16[32,1536]{1,0:T(8,128)(2,1)S(1)}, u32[]{:S(2)}, u32[]{:S(2)}) collective-permute-start(bf16[32,1536]{1,0:T(8,128)(2,1)S(1)} %get-tuple-element.61), channel_id=1, source_target_pairs={{0,16},{4,20},{8,24},{12,28},{16,0},{20,4},{24,8},{28,12},{32,48},... | collective-permute-start | bytes 294920 | tf_op jit(solution)/shard_map/ppermute | solution.py:297
  57.9 4.7 %collective-permute-start.9 = (bf16[32,1536]{1,0:T(8,128)(2,1)S(1)}, bf16[32,1536]{1,0:T(8,128)(2,1)S(1)}, u32[]{:S(2)}, u32[]{:S(2)}) collective-permute-start(bf16[32,1536]{1,0:T(8,128)(2,1)S(1)} %get-tuple-element.62), channel_id=1, source_target_pairs={{0,24},{4,28},{8,0},{12,4},{16,8},{20,12},{24,16},{28,20},{32,56},... | collective-permute-start | bytes 294920 | tf_op jit(solution)/shard_map/ppermute | solution.py:297
  62.6 5.1 %collective-permute-start.10 = (bf16[32,1536]{1,0:T(8,128)(2,1)S(1)}, bf16[32,1536]{1,0:T(8,128)(2,1)S(1)}, u32[]{:S(2)}, u32[]{:S(2)}) collective-permute-start(bf16[32,1536]{1,0:T(8,128)(2,1)S(1)} %shard_map.81), channel_id=1, source_target_pairs={{0,32},{4,36},{8,40},{12,44},{16,48},{20,52},{24,56},{28,60},{32,6... | collective-permute-start | bytes 294920 | tf_op jit(solution)/shard_map/ppermute | solution.py:299
  64.0 6.1 %collective-permute-start.11 = (bf16[32,1536]{1,0:T(8,128)(2,1)S(1)}, bf16[32,1536]{1,0:T(8,128)(2,1)S(1)}, u32[]{:S(2)}, u32[]{:S(2)}) collective-permute-start(bf16[32,1536]{1,0:T(8,128)(2,1)S(1)} %shard_map.81), channel_id=1, source_target_pairs={{0,64},{4,68},{8,72},{12,76},{16,80},{20,84},{24,88},{28,92},{32,9... | collective-permute-start | bytes 294920 | tf_op jit(solution)/shard_map/ppermute | solution.py:299
  66.6 4.6 %collective-permute-start.12 = (bf16[32,1536]{1,0:T(8,128)(2,1)S(1)}, bf16[32,1536]{1,0:T(8,128)(2,1)S(1)}, u32[]{:S(2)}, u32[]{:S(2)}) collective-permute-start(bf16[32,1536]{1,0:T(8,128)(2,1)S(1)} %shard_map.81), channel_id=1, source_target_pairs={{0,96},{4,100},{8,104},{12,108},{16,112},{20,116},{24,120},{28,124... | collective-permute-start | bytes 294920 | tf_op jit(solution)/shard_map/ppermute | solution.py:299
  72.0 5.8 %collective-permute-start.13 = (bf16[32,1536]{1,0:T(8,128)(2,1)S(1)}, bf16[32,1536]{1,0:T(8,128)(2,1)S(1)}, u32[]{:S(2)}, u32[]{:S(2)}) collective-permute-start(bf16[32,1536]{1,0:T(8,128)(2,1)S(1)} %get-tuple-element.64), channel_id=1, source_target_pairs={{0,8},{4,12},{8,16},{12,20},{16,24},{20,28},{24,0},{28,4},{32,40},... | collective-permute-start | bytes 294920 | tf_op jit(solution)/shard_map/ppermute | solution.py:301
  72.5 5.3 %collective-permute-start.14 = (bf16[32,1536]{1,0:T(8,128)(2,1)S(1)}, bf16[32,1536]{1,0:T(8,128)(2,1)S(1)}, u32[]{:S(2)}, u32[]{:S(2)}) collective-permute-start(bf16[32,1536]{1,0:T(8,128)(2,1)S(1)} %get-tuple-element.65), channel_id=1, source_target_pairs={{0,16},{4,20},{8,24},{12,28},{16,0},{20,4},{24,8},{28,12},{32,48},... | collective-permute-start | bytes 294920 | tf_op jit(solution)/shard_map/ppermute | solution.py:301
  74.7 4.0 %collective-permute-start.15 = (bf16[32,1536]{1,0:T(8,128)(2,1)S(1)}, bf16[32,1536]{1,0:T(8,128)(2,1)S(1)}, u32[]{:S(2)}, u32[]{:S(2)}) collective-permute-start(bf16[32,1536]{1,0:T(8,128)(2,1)S(1)} %get-tuple-element.66), channel_id=1, source_target_pairs={{0,24},{4,28},{8,0},{12,4},{16,8},{20,12},{24,16},{28,20},{32,56},... | collective-permute-start | bytes 294920 | tf_op jit(solution)/shard_map/ppermute | solution.py:301
  79.5 5.0 %collective-permute-start.16 = (bf16[128,1536]{1,0:T(8,128)(2,1)S(1)}, bf16[128,1536]{1,0:T(8,128)(2,1)S(1)}, u32[]{:S(2)}, u32[]{:S(2)}) collective-permute-start(bf16[128,1536]{1,0:T(8,128)(2,1)S(1)} %get-tuple-element.68), channel_id=1, source_target_pairs={{0,4},{4,0},{8,12},{12,8},{16,20},{20,16},{24,28},{28,24},{32,36},... | collective-permute-start | bytes 1179656 | tf_op jit(solution)/shard_map/ppermute | solution.py:305
  (1 other events, 1.1 us)

commit v4 on v3

--- a/solution.py
+++ b/solution.py
@@ -13,6 +13,7 @@
 HEADS = D // HEAD
 TILE = 512
 TILES = D // TILE
+HINT = 1 << 33
 WIDE = D + HEAD
 VMEM = 16 << 20
 epsilon = 1e-06
@@ -20,22 +21,54 @@
 f32, bf16 = jnp.float32, jnp.bfloat16
 
 
+def modulation_kernel(times, weight, shift, scale, gate, rates):
+    rows, freq = 16, HEAD
+    lane = lax.broadcasted_iota(jnp.int32, (rows, freq), 1)
+    row = lax.broadcasted_iota(jnp.int32, (rows, 2 * freq), 0)
+    t = jnp.full((rows, freq), times[0, 0], jnp.int32).astype(f32)
+    angles = t * jnp.exp(-math.log(10000.0) * lane.astype(f32) / freq)
+    embedded = jnp.concatenate([jnp.cos(angles), jnp.sin(angles)], axis=1)
+    high = embedded.astype(bf16).astype(f32)
+    middle = (embedded - high).astype(bf16).astype(f32)
+    low = embedded - high - middle
+    terms = jnp.where(row == 0, high, jnp.where(row == 1, middle, jnp.where(row == 2, low, 0.0))).astype(bf16)
+    for g, out in enumerate((shift, scale, gate)):
+        product = jnp.dot(terms, weight[:, g * D : (g + 1) * D], preferred_element_type=f32)
+        out[...] = jnp.sum(product, axis=0, keepdims=True)
+    half_width = HEAD // 2
+    lane = lax.broadcasted_iota(jnp.int32, (1, HEAD), 1)
+    rates[0:1, :] = jnp.exp(-math.log(10000.0) * (lane & (half_width - 1)).astype(f32) / half_width)
+    rates[1:2, :] = jnp.where(lane < half_width, -1.0, 1.0)
+
+
 def modulation(step_times, time_weight):
-    half_width = time_weight.shape[0] // 2
-    steps_f = step_times[:, 0].astype(f32)
-    frequency = jnp.exp(-math.log(10000.0) * jnp.arange(half_width, dtype=f32) / half_width)
-    angles = steps_f[:, None] * frequency[None, :]
-    embedded = jnp.concatenate([jnp.cos(angles), jnp.sin(angles)], axis=1)
-    return jnp.dot(embedded, time_weight.astype(f32), precision=lax.Precision.HIGHEST)
-
-
-def message_kernel(x_ref, positions_ref, first_ref, second_ref):
-    rows = first_ref.shape[0]
+    vm = pl.BlockSpec(memory_space=pltpu.VMEM)
+    return pl.pallas_call(
+        modulation_kernel,
+        in_specs=[pl.BlockSpec(memory_space=pltpu.SMEM), vm],
+        out_specs=[vm] * 4,
+        out_shape=[pltpu.VMEM((1, D), f32)] * 3 + [pltpu.VMEM((2, HEAD), f32)],
+        cost_estimate=pl.CostEstimate(flops=HINT, bytes_accessed=0, transcendentals=0),
+        compiler_params=pltpu.CompilerParams(vmem_limit_bytes=3 << 20),
+    )(step_times, time_weight)
+
+
+def message_kernel(x, positions, first, second, sems):
+    rows = first.shape[0]
+    loads = [
+        pltpu.make_async_copy(x.at[pl.ds(j * rows, rows), :], out.at[:, pl.ds(0, D)], sems.at[j])
+        for j, out in enumerate((first, second))
+    ]
+    for load in loads:
+        load.start()
     lane = lax.broadcasted_iota(jnp.int32, (rows, HEAD), 1)
-    for at, out in ((0, first_ref), (rows, second_ref)):
-        ids = positions_ref[at : at + rows, :]
-        out[:, :D] = x_ref[at : at + rows, :]
+    row = lax.broadcasted_iota(jnp.int32, (rows, HEAD), 0)
+    for j, out in enumerate((first, second)):
+        spread = jnp.where(row == lane, positions[j : j + 1, :], 0).astype(f32)
+        ids = jnp.sum(spread, axis=1, keepdims=True).astype(jnp.int32)
         out[:, D:] = jnp.where(lane == 0, ids >> 5, jnp.where(lane == 1, ids & 31, 0)).astype(f32).astype(bf16)
+    for load in loads:
+        load.wait()
 
 
 def with_positions(x, positions):
@@ -43,18 +76,13 @@
     vm = pl.BlockSpec(memory_space=pltpu.VMEM)
     return pl.pallas_call(
         message_kernel,
-        in_specs=[vm] * 2,
+        in_specs=[pl.BlockSpec(memory_space=pl.ANY), vm],
         out_specs=[vm] * 2,
         out_shape=[pltpu.VMEM((half, WIDE), bf16)] * 2,
+        scratch_shapes=[pltpu.SemaphoreType.DMA((2,))],
+        cost_estimate=pl.CostEstimate(flops=HINT, bytes_accessed=0, transcendentals=0),
         compiler_params=pltpu.CompilerParams(vmem_limit_bytes=4 << 20),
-    )(x, positions[:, None])
-
-
-def rope_rates():
-    half_width = HEAD // 2
-    lane = jnp.arange(HEAD, dtype=jnp.int32)
-    inverse = jnp.exp(-math.log(10000.0) * (lane % half_width).astype(f32) / half_width)
-    return jnp.stack([inverse, jnp.where(lane < half_width, -1.0, 1.0)])
+    )(x, positions.reshape(2, half))
 
 
 def norm_rope(proj, gain, cos, sin, out_ref):
@@ -138,8 +166,8 @@
             p = jnp.exp2(scores[j] * EXP_SCALE - m)
             total = total + jnp.sum(p, axis=1, keepdims=True)
             acc = acc + jnp.dot(p.astype(bf16), kv[2 * j + 1][:, at], preferred_element_type=f32)
-        m_ref[:, h : h + 1] = m
-        l_ref[:, h : h + 1] = total
+        m_ref[h] = jnp.broadcast_to(m, (rows, HEAD))
+        l_ref[h] = jnp.broadcast_to(total, (rows, HEAD))
         acc_ref[:, at] = acc
 
 
@@ -153,20 +181,21 @@
         in_specs=[vm] * (1 + len(flat)),
         out_specs=[vm] * 3,
         out_shape=[
-            pltpu.VMEM((rows, HEAD), f32),
-            pltpu.VMEM((rows, HEAD), f32),
+            pltpu.VMEM((HEADS, rows, HEAD), f32),
+            pltpu.VMEM((HEADS, rows, HEAD), f32),
             pltpu.VMEM((rows, D), f32),
         ],
         cost_estimate=pl.CostEstimate(
             flops=8 * rows * D * keys, bytes_accessed=4 * rows * D * 2, transcendentals=rows * keys * HEADS
         ),
-        compiler_params=pltpu.CompilerParams(vmem_limit_bytes=10 << 20),
+        compiler_params=pltpu.CompilerParams(vmem_limit_bytes=12 << 20),
     )(q, *flat)
 
 
 def finish_kernel(n_kv, h_ref, place_ref, q_ref, *refs):
     kv, refs = refs[: 2 * n_kv], refs[2 * n_kv :]
     m_ref, l_ref, acc_ref, x_ref, gate_ref, w_ref, out_ref, sent_ref, attended = refs
+    rows = q_ref.shape[0]
     for h in range(HEADS):
         at = slice(h * HEAD, (h + 1) * HEAD)
         q = q_ref[:, at]
@@ -177,17 +206,21 @@
         top = scores[0]
         for s in scores[1:]:
             top = jnp.maximum(top, s)
-        before = m_ref[:, h : h + 1]
-        m = jnp.maximum(jnp.max(top, axis=1, keepdims=True) * EXP_SCALE, before)
-        fade = jnp.exp2(before - m)
-        total = l_ref[:, h : h + 1] * fade
-        acc = acc_ref[:, at] * fade
+        new = jnp.max(top, axis=1, keepdims=True) * EXP_SCALE
+        total = jnp.zeros((rows, 1), f32)
+        acc = jnp.zeros((rows, HEAD), f32)
         for j in range(n_kv):
-            p = jnp.exp2(scores[j] * EXP_SCALE - m)
+            p = jnp.exp2(scores[j] * EXP_SCALE - new)
             total = total + jnp.sum(p, axis=1, keepdims=True)
             acc = acc + jnp.dot(p.astype(bf16), kv[2 * j + 1][:, at], preferred_element_type=f32)
+        old = m_ref[h]
+        new = jnp.broadcast_to(new, (rows, HEAD))
+        m = jnp.maximum(new, old)
+        fade_old, fade_new = jnp.exp2(old - m), jnp.exp2(new - m)
+        total = l_ref[h] * fade_old + jnp.broadcast_to(total, (rows, HEAD)) * fade_new
+        acc = acc_ref[:, at] * fade_old + acc * fade_new
         attended[:, at] = (acc / total).astype(bf16)
-    size = h_ref[0, 0]
+    size = jnp.full((1, TILE), h_ref[0, 1] - h_ref[0, 0], jnp.int32).astype(f32) / 1000.0
     for t in range(TILES):
         at = slice(t * TILE, (t + 1) * TILE)
         proj = jnp.dot(attended[...], w_ref[:, at], preferred_element_type=f32)
@@ -197,7 +230,7 @@
     sent_ref[...] = out_ref[theirs, :].astype(bf16)
 
 
-def finish(step_size, place, q, kvs, state, x, gate, w_out):
+def finish(step_times, place, q, kvs, state, x, gate, w_out):
     rows = q.shape[0]
     keys = sum(k.shape[0] for k, _ in kvs)
     flat = [a for pair in kvs for a in pair]
@@ -214,8 +247,8 @@
             bytes_accessed=2 * D * D,
             transcendentals=rows * keys * HEADS,
         ),
-        compiler_params=pltpu.CompilerParams(vmem_limit_bytes=6 << 20),
-    )(step_size, place, q, *flat, *state, x, gate, w_out)
+        compiler_params=pltpu.CompilerParams(vmem_limit_bytes=12 << 20),
+    )(step_times, place, q, *flat, *state, x, gate, w_out)
 
 
 def split_kernel(place, inc, got, own, *pieces):
@@ -318,19 +351,17 @@
     x = states[0]
     first, second = with_positions(x, positions)
     r_first, l_second = to_right(first), to_left(second)
-    step_size = (step_times[:, 1:] - step_times[:, :1]).astype(f32) / 1000.0
-    ready = (modulation(step_times, time_weight), rope_rates(), step_size, place, second, first)
-    modulated, rates, step_size, place, second_later, first_later = lax.optimization_barrier(ready)
+    ready = (modulation(step_times, time_weight), place, second, first)
+    (shift, scale, gate, rates), place, second_later, first_later = lax.optimization_barrier(ready)
     r_second, l_first = to_right(second_later), to_left(first_later)
     forward = to_right(r_first), to_left(l_second)
-    shift, scale, gate = modulated[:, :D], modulated[:, D : 2 * D], modulated[:, 2 * D :]
 
     q, k, v = project((first_later, second_later), shift, scale, qk_gain, rates, w_qkv, True)
     kvs = [(k, v)]
     for chunk in ((r_first, l_second), (r_second, l_first), forward):
         kvs.append(tuple(project(chunk, shift, scale, qk_gain, rates, w_qkv, False)))
     state = attend(q, kvs[:3])
-    inc, sent = finish(step_size, place, q, kvs[3:], state, x, gate, w_out)
+    inc, sent = finish(step_times, place, q, kvs[3:], state, x, gate, w_out)
     return scan_steps(place, inc, sent)[None]
 
 

time: 86.5 us -> 77.1 us (0.89)
  Pallas kernels: 32.4 us -> 27.9 us
  local copies, waits for them, and re-layouts: 8.53 us -> 4.53 us
  waiting for transfers between devices: 12.8 us -> 15.5 us
  between operations: 2.03 us -> 0.19 us
  matrix products: 1.02 us -> 0 us
    pallas_call x1, Pallas kernels: 6.92 us -> 3.54 us  [finish(): pl.pallas_call(functools.partial(finish_kernel, len(kvs)), in_specs=[pl.B...]
    ppermute x3, waiting for transfers between devices: 0.01 us -> 2.71 us  [on_device(): to_right = lambda v: lax.ppermute(v, 'seq', right)]
    unnamed x16 -> x24, local copies, waits for them, and re-layouts: 6.19 us -> 4.53 us
    slice x2 -> x0, local copies, waits for them, and re-layouts: 1.38 us -> none  [the longest x1 1.38 us: on_device(): step_size = (step_times[:, 1:] - step_times[:, :1]).astype(f32) / 1000.0]
    pallas_call x4, Pallas kernels: 15.3 us -> 14 us  [project(): pl.pallas_call(functools.partial(project_kernel, with_q), in_specs=[vm] *...]
    dot_general x1 -> x0, matrix products: 1.02 us -> none  [modulation(): jnp.dot(embedded, time_weight.astype(f32), precision=lax.Precision.HIGHEST)]
    broadcast_in_dim x1 -> x0, local copies, waits for them, and re-layouts: 0.95 us -> none  [with_positions(): positions[:, None]]
  transfers between devices with their start and end apart: 17 -> 17, of which waited for: 8 -> 10; matrix products, arithmetic and copies ran while one was open for 3% -> 0% of each run, Pallas kernels for 20% -> 22%
where the time goes in v4:
time: 77.1 us; the launch traced here: 76.9 us
  starting transfers between devices  28.7 us (37%)
  Pallas kernels  27.9 us (36%)
  waiting for transfers between devices  15.5 us (20%)
  local copies, waits for them, and re-layouts  4.53 us (6%)
    pallas_call x4, Pallas kernels, project(): pl.pallas_call(functools.partial(project_kernel, with_q), in_specs=[vm] *...  14 us
    ppermute x6, starting transfers between devices, scan_steps(): lax.ppermute(piece, 'step', along_x(k))  8.57 us
    ppermute x3, starting transfers between devices, on_device(): to_left = lambda v: lax.ppermute(v, 'seq', left)  7.52 us
    ppermute x6, waiting for transfers between devices, scan_steps(): lax.ppermute(piece, 'step', along_x(k))  6.48 us
    pallas_call x1, Pallas kernels, attend(): pl.pallas_call(functools.partial(attend_kernel, len(kvs)), in_specs=[vm]...  5.08 us
    ppermute x3, starting transfers between devices, scan_steps(): ys = [lax.ppermute(row, 'step', along_y(k)) for k in (1, 2, 3)]  5.06 us
    unnamed x24, local copies, waits for them, and re-layouts  4.53 us
    pallas_call x5, Pallas kernels, small_call(): pl.pallas_call(kernel, in_specs=[pl.BlockSpec(memory_space=pltpu.SMEM)] *...  4.11 us
  transfers between devices with their start and end apart: 17, of which 10 were waited for; matrix products, arithmetic and copies ran while one was open for 0% of the time, Pallas kernels for 22%

profile of v4, /device:TPU:1, one launch (start us, length us, event | category | flops | bytes accessed | tf_op | source)
XLA Modules:
  0.0 76.9 jit_solution(6372409271247272629)
XLA Ops:
  2.0 2.5 %collective-permute-start = (bf16[128,1664]{1,0:T(8,128)(2,1)S(1)}, bf16[128,1664]{1,0:T(8,128)(2,1)S(1)}, u32[]{:S(2)}, u32[]{:S(2)}) collective-permute-start(bf16[128,1664]{1,0:T(8,128)(2,1)S(1)} %get-tuple-element.49.refs_0_), channel_id=1, source_target_pairs={{0,1},{1,2},{2,3},{3,0},{4,5},{5,6},{6,7},{7,4},{8,9},{9,10},{10,1... | collective-permute-start | bytes 1277960 | tf_op jit(solution)/shard_map/ppermute | solution.py:346
  4.6 2.2 %collective-permute-start.2 = (bf16[128,1664]{1,0:T(8,128)(2,1)S(1)}, bf16[128,1664]{1,0:T(8,128)(2,1)S(1)}, u32[]{:S(2)}, u32[]{:S(2)}) collective-permute-start(bf16[128,1664]{1,0:T(8,128)(2,1)S(1)} %get-tuple-element.50.refs_1_), channel_id=1, source_target_pairs={{0,3},{1,0},{2,1},{3,2},{4,7},{5,4},{6,5},{7,6},{8,11},{9,8},{10,9... | collective-permute-start | bytes 1277960 | tf_op jit(solution)/shard_map/ppermute | solution.py:347
  6.8 1.8 %copy-done.4 = bf16[256,4608]{1,0:T(8,128)(2,1)S(1)} copy-done((bf16[256,4608]{1,0:T(8,128)(2,1)S(1)}, bf16[256,4608]{1,0:T(8,128)(2,1)}, u32[]{:S(2)}) %copy-start.4) | copy-done | bytes 2359320
  9.7 2.7 %collective-permute-start.5 = (bf16[128,1664]{1,0:T(8,128)(2,1)S(1)}, bf16[128,1664]{1,0:T(8,128)(2,1)S(1)}, u32[]{:S(2)}, u32[]{:S(2)}) collective-permute-start(bf16[128,1664]{1,0:T(8,128)(2,1)S(1)} %get-tuple-element.49.refs_0_), channel_id=1, source_target_pairs={{0,3},{1,0},{2,1},{3,2},{4,7},{5,4},{6,5},{7,6},{8,11},{9,8},{10,9... | collective-permute-start | bytes 1277960 | tf_op jit(solution)/shard_map/ppermute | solution.py:347
  13.2 4.4 %shard_map.75 = (bf16[256,1536]{1,0:T(8,128)(2,1)S(1)}, bf16[256,1536]{1,0:T(8,128)(2,1)S(1)}, bf16[256,1536]{1,0:T(8,128)(2,1)S(1)}) custom-call(bf16[128,1664]{1,0:T(8,128)(2,1)S(1)} %get-tuple-element.49.refs_0_, bf16[128,1664]{1,0:T(8,128)(2,1)S(1)} %get-tuple-element.50.refs_1_, f32[1,1536]{1,0:T(1,128)S(1)} %get-tuple-element.51.refs_2_, ...), custom_call_target="tpu_custom_call" | custom-call | flops 3623878656 | bytes 14155776 | tf_op jit(solution)/shard_map/pallas_call | solution.py:136
  17.7 2.7 %collective-permute-start.3 = (bf16[128,1664]{1,0:T(8,128)(2,1)S(1)}, bf16[128,1664]{1,0:T(8,128)(2,1)S(1)}, u32[]{:S(2)}, u32[]{:S(2)}) collective-permute-start(bf16[128,1664]{1,0:T(8,128)(2,1)S(1)} %collective-permute-done.2.refs_1_), channel_id=1, source_target_pairs={{0,3},{1,0},{2,1},{3,2},{4,7},{5,4},{6,5},{7,6},{8,11},{9,8},{10,9... | collective-permute-start | bytes 1277960 | tf_op jit(solution)/shard_map/ppermute | solution.py:347
  20.4 3.1 %shard_map.77 = (bf16[256,1536]{1,0:T(8,128)(2,1)S(1)}, bf16[256,1536]{1,0:T(8,128)(2,1)S(1)}) custom-call(bf16[128,1664]{1,0:T(8,128)(2,1)S(1)} %collective-permute-done.refs_0_, bf16[128,1664]{1,0:T(8,128)(2,1)S(1)} %collective-permute-done.2.refs_1_, f32[1,1536]{1,0:T(1,128)S(1)} %get-tuple-element.51.refs_2_, f32[1,1536]{1,0:T(1,128)S(1)} %get-tuple-element.52.refs_3_, ...), custom_call_target="tpu_custom_call" | custom-call | flops 2415919104 | bytes 9437184 | tf_op jit(solution)/shard_map/pallas_call | solution.py:136
  23.5 1.8 %collective-permute-done.4.refs_0_ = bf16[128,1664]{1,0:T(8,128)(2,1)S(1)} collective-permute-done((bf16[128,1664]{1,0:T(8,128)(2,1)S(1)}, bf16[128,1664]{1,0:T(8,128)(2,1)S(1)}, u32[]{:S(2)}, u32[]{:S(2)}) %collective-permute-start.4) | collective-permute-done | bytes 426016 | tf_op jit(solution)/shard_map/ppermute | solution.py:346
  25.3 3.1 %shard_map.78 = (bf16[256,1536]{1,0:T(8,128)(2,1)S(1)}, bf16[256,1536]{1,0:T(8,128)(2,1)S(1)}) custom-call(bf16[128,1664]{1,0:T(8,128)(2,1)S(1)} %collective-permute-done.4.refs_0_, bf16[128,1664]{1,0:T(8,128)(2,1)S(1)} %collective-permute-done.5.refs_1_, f32[1,1536]{1,0:T(1,128)S(1)} %get-tuple-element.51.refs_2_, f32[1,1536]{1,0:T(1,128)S(1)} %get-tuple-element.52.refs_3_, ...), custom_call_target="tpu_custom_call" | custom-call | flops 2415919104 | bytes 9437184 | tf_op jit(solution)/shard_map/pallas_call | solution.py:136
  28.5 5.1 %shard_map.79 = (f32[12,256,128]{2,1,0:T(8,128)S(1)}, f32[12,256,128]{2,1,0:T(8,128)S(1)}, f32[256,1536]{1,0:T(8,128)S(1)}) custom-call(bf16[256,1536]{1,0:T(8,128)(2,1)S(1)} %get-tuple-element.54.q_ref, bf16[256,1536]{1,0:T(8,128)(2,1)S(1)} %get-tuple-element.57.refs_0_, bf16[256,1536]{1,0:T(8,128)(2,1)S(1)} %get-tuple-element.58.refs_1_, ...), custom_call_target="tpu_custom_call" | custom-call | flops 2415919104 | bytes 3145728 | tf_op jit(solution)/shard_map/pallas_call | solution.py:179
  34.5 3.4 %shard_map.76 = (bf16[256,1536]{1,0:T(8,128)(2,1)S(1)}, bf16[256,1536]{1,0:T(8,128)(2,1)S(1)}) custom-call(bf16[128,1664]{1,0:T(8,128)(2,1)S(1)} %collective-permute-done.1.refs_0_, bf16[128,1664]{1,0:T(8,128)(2,1)S(1)} %collective-permute-done.3.refs_1_, f32[1,1536]{1,0:T(1,128)S(1)} %get-tuple-element.51.refs_2_, f32[1,1536]{1,0:T(1,128)S(1)} %get-tuple-element.52.refs_3_, ...), custom_call_target="tpu_custom_call" | custom-call | flops 2415919104 | bytes 9437184 | tf_op jit(solution)/shard_map/pallas_call | solution.py:136
  37.9 3.5 %shard_map.80 = (f32[256,1536]{1,0:T(8,128)S(1)}, bf16[128,1536]{1,0:T(8,128)(2,1)S(1)}) custom-call(s32[1,2]{1,0:T(1,128)S(1)} %copy-done.3, s32[3]{0:T(128)S(1)} %pad_add_fusion.place_ref.place, bf16[256,1536]{1,0:T(8,128)(2,1)S(1)} %get-tuple-element.54.q_ref, bf16[256,1536]{1,0:T(8,128)(2,1)S(1)} %get-tuple-element.55.refs_0_, ...), custom_call_target="tpu_custom_call" | custom-call | flops 2013265920 | bytes 4718592 | tf_op jit(solution)/shard_map/pallas_call | solution.py:238
  41.5 1.3 %collective-permute-start.6 = (bf16[128,1536]{1,0:T(8,128)(2,1)S(1)}, bf16[128,1536]{1,0:T(8,128)(2,1)S(1)}, u32[]{:S(2)}, u32[]{:S(2)}) collective-permute-start(bf16[128,1536]{1,0:T(8,128)(2,1)S(1)} %get-tuple-element.68), channel_id=1, source_target_pairs={{0,4},{4,0},{8,12},{12,8},{16,20},{20,16},{24,28},{28,24},{32,36},... | collective-permute-start | bytes 1179656 | tf_op jit(solution)/shard_map/ppermute | solution.py:328
  42.8 1.3 %collective-permute-done.6.got = bf16[128,1536]{1,0:T(8,128)(2,1)S(1)} collective-permute-done((bf16[128,1536]{1,0:T(8,128)(2,1)S(1)}, bf16[128,1536]{1,0:T(8,128)(2,1)S(1)}, u32[]{:S(2)}, u32[]{:S(2)}) %collective-permute-start.6) | collective-permute-done | bytes 393248 | tf_op jit(solution)/shard_map/ppermute | solution.py:328
  46.0 2.4 %collective-permute-start.8 = (bf16[32,1536]{1,0:T(8,128)(2,1)S(1)}, bf16[32,1536]{1,0:T(8,128)(2,1)S(1)}, u32[]{:S(2)}, u32[]{:S(2)}) collective-permute-start(bf16[32,1536]{1,0:T(8,128)(2,1)S(1)} %get-tuple-element.71), channel_id=1, source_target_pairs={{0,16},{4,20},{8,24},{12,28},{16,0},{20,4},{24,8},{28,12},{32,48},... | collective-permute-start | bytes 294920 | tf_op jit(solution)/shard_map/ppermute | solution.py:330
  50.0 3.1 %collective-permute-done.8.two.refs_1_ = bf16[32,1536]{1,0:T(8,128)(2,1)S(1)} collective-permute-done((bf16[32,1536]{1,0:T(8,128)(2,1)S(1)}, bf16[32,1536]{1,0:T(8,128)(2,1)S(1)}, u32[]{:S(2)}, u32[]{:S(2)}) %collective-permute-start.8) | collective-permute-done | bytes 98336 | tf_op jit(solution)/shard_map/ppermute | solution.py:330
  53.2 1.4 %collective-permute-start.10 = (bf16[32,1536]{1,0:T(8,128)(2,1)S(1)}, bf16[32,1536]{1,0:T(8,128)(2,1)S(1)}, u32[]{:S(2)}, u32[]{:S(2)}) collective-permute-start(bf16[32,1536]{1,0:T(8,128)(2,1)S(1)} %shard_map.82), channel_id=1, source_target_pairs={{0,32},{4,36},{8,40},{12,44},{16,48},{20,52},{24,56},{28,60},{32,6... | collective-permute-start | bytes 294920 | tf_op jit(solution)/shard_map/ppermute | solution.py:332
  54.5 2.6 %collective-permute-start.11 = (bf16[32,1536]{1,0:T(8,128)(2,1)S(1)}, bf16[32,1536]{1,0:T(8,128)(2,1)S(1)}, u32[]{:S(2)}, u32[]{:S(2)}) collective-permute-start(bf16[32,1536]{1,0:T(8,128)(2,1)S(1)} %shard_map.82), channel_id=1, source_target_pairs={{0,64},{4,68},{8,72},{12,76},{16,80},{20,84},{24,88},{28,92},{32,9... | collective-permute-start | bytes 294920 | tf_op jit(solution)/shard_map/ppermute | solution.py:332
  58.2 2.4 %collective-permute-done.11.refs_4_ = bf16[32,1536]{1,0:T(8,128)(2,1)S(1)} collective-permute-done((bf16[32,1536]{1,0:T(8,128)(2,1)S(1)}, bf16[32,1536]{1,0:T(8,128)(2,1)S(1)}, u32[]{:S(2)}, u32[]{:S(2)}) %collective-permute-start.11) | collective-permute-done | bytes 98336 | tf_op jit(solution)/shard_map/ppermute | solution.py:332
  63.1 2.0 %collective-permute-start.14 = (bf16[32,1536]{1,0:T(8,128)(2,1)S(1)}, bf16[32,1536]{1,0:T(8,128)(2,1)S(1)}, u32[]{:S(2)}, u32[]{:S(2)}) collective-permute-start(bf16[32,1536]{1,0:T(8,128)(2,1)S(1)} %get-tuple-element.75), channel_id=1, source_target_pairs={{0,16},{4,20},{8,24},{12,28},{16,0},{20,4},{24,8},{28,12},{32,48},... | collective-permute-start | bytes 294920 | tf_op jit(solution)/shard_map/ppermute | solution.py:334
  66.3 2.1 %collective-permute-done.13.refs_1_ = bf16[32,1536]{1,0:T(8,128)(2,1)S(1)} collective-permute-done((bf16[32,1536]{1,0:T(8,128)(2,1)S(1)}, bf16[32,1536]{1,0:T(8,128)(2,1)S(1)}, u32[]{:S(2)}, u32[]{:S(2)}) %collective-permute-start.13) | collective-permute-done | bytes 98336 | tf_op jit(solution)/shard_map/ppermute | solution.py:334
  70.1 3.7 %collective-permute-start.16 = (bf16[128,1536]{1,0:T(8,128)(2,1)S(1)}, bf16[128,1536]{1,0:T(8,128)(2,1)S(1)}, u32[]{:S(2)}, u32[]{:S(2)}) collective-permute-start(bf16[128,1536]{1,0:T(8,128)(2,1)S(1)} %get-tuple-element.78), channel_id=1, source_target_pairs={{0,4},{4,0},{8,12},{12,8},{16,20},{20,16},{24,28},{28,24},{32,36},... | collective-permute-start | bytes 1179656 | tf_op jit(solution)/shard_map/ppermute | solution.py:338
  73.7 1.3 %collective-permute-done.16.other = bf16[128,1536]{1,0:T(8,128)(2,1)S(1)} collective-permute-done((bf16[128,1536]{1,0:T(8,128)(2,1)S(1)}, bf16[128,1536]{1,0:T(8,128)(2,1)S(1)}, u32[]{:S(2)}, u32[]{:S(2)}) %collective-permute-start.16) | collective-permute-done | bytes 393248 | tf_op jit(solution)/shard_map/ppermute | solution.py:338
  75.1 1.8 %shard_map.85 = f32[256,1536]{1,0:T(8,128)} custom-call(s32[3]{0:T(128)S(1)} %pad_add_fusion.place_ref.place, f32[256,1536]{1,0:T(8,128)S(1)} %get-tuple-element.67.inc, f32[128,1536]{1,0:T(8,128)S(1)} %get-tuple-element.77.own, bf16[128,1536]{1,0:T(8,128)(2,1)S(1)} %collective-permute-done.16.other), custom_call_target="tpu_custom_call" | custom-call | tf_op jit(solution)/shard_map/pallas_call | solution.py:306
  (50 shorter events, 14.9 us)
Async XLA Ops:
  1.8 4.9 %copy-start.3 = (s32[1,2]{1,0:T(1,128)S(1)}, s32[1,2]{1,0:T(1,128)}, u32[]{:S(2)}) copy-start(s32[1,2]{1,0:T(1,128)} %h_ref.1) | copy-start | bytes 28
  2.0 15.6 %collective-permute-start = (bf16[128,1664]{1,0:T(8,128)(2,1)S(1)}, bf16[128,1664]{1,0:T(8,128)(2,1)S(1)}, u32[]{:S(2)}, u32[]{:S(2)}) collective-permute-start(bf16[128,1664]{1,0:T(8,128)(2,1)S(1)} %get-tuple-element.49.refs_0_), channel_id=1, source_target_pairs={{0,1},{1,2},{2,3},{3,0},{4,5},{5,6},{6,7},{7,4},{8,9},{9,10},{10,1... | collective-permute-start | bytes 1277960 | tf_op jit(solution)/shard_map/ppermute | solution.py:346
  4.6 13.1 %collective-permute-start.2 = (bf16[128,1664]{1,0:T(8,128)(2,1)S(1)}, bf16[128,1664]{1,0:T(8,128)(2,1)S(1)}, u32[]{:S(2)}, u32[]{:S(2)}) collective-permute-start(bf16[128,1664]{1,0:T(8,128)(2,1)S(1)} %get-tuple-element.50.refs_1_), channel_id=1, source_target_pairs={{0,3},{1,0},{2,1},{3,2},{4,7},{5,4},{6,5},{7,6},{8,11},{9,8},{10,9... | collective-permute-start | bytes 1277960 | tf_op jit(solution)/shard_map/ppermute | solution.py:347
  6.8 5.6 %slice-start = ((s8[14155776]{0:T(1024)(128)(4,1)}), s8[1572864]{0:T(1024)(128)(4,1)S(1)}, s32[]{:S(2)}) async-start(s8[14155776]{0:T(1024)(128)(4,1)} %bitcast.6), calls=%async_computation | async-start | bytes 3145728
  8.5 4.7 %slice-start.3 = ((s8[14155776]{0:T(1024)(128)(4,1)}), s8[4194304]{0:T(1024)(128)(4,1)S(1)}, s32[]{:S(2)}) async-start(s8[14155776]{0:T(1024)(128)(4,1)} %bitcast.6), calls=%async_computation.3 | async-start | bytes 8388608
  8.6 4.7 %copy-start.2 = (f32[2,1536]{1,0:T(2,128)S(1)}, f32[2,1536]{1,0:T(2,128)}, u32[]{:S(2)}) copy-start(f32[2,1536]{1,0:T(2,128)} %refs_4_.7) | copy-start | bytes 36868
  9.6 15.7 %collective-permute-start.4 = (bf16[128,1664]{1,0:T(8,128)(2,1)S(1)}, bf16[128,1664]{1,0:T(8,128)(2,1)S(1)}, u32[]{:S(2)}, u32[]{:S(2)}) collective-permute-start(bf16[128,1664]{1,0:T(8,128)(2,1)S(1)} %get-tuple-element.50.refs_1_), channel_id=1, source_target_pairs={{0,1},{1,2},{2,3},{3,0},{4,5},{5,6},{6,7},{7,4},{8,9},{9,10},{10,1... | collective-permute-start | bytes 1277960 | tf_op jit(solution)/shard_map/ppermute | solution.py:346
  9.7 15.7 %collective-permute-start.5 = (bf16[128,1664]{1,0:T(8,128)(2,1)S(1)}, bf16[128,1664]{1,0:T(8,128)(2,1)S(1)}, u32[]{:S(2)}, u32[]{:S(2)}) collective-permute-start(bf16[128,1664]{1,0:T(8,128)(2,1)S(1)} %get-tuple-element.49.refs_0_), channel_id=1, source_target_pairs={{0,3},{1,0},{2,1},{3,2},{4,7},{5,4},{6,5},{7,6},{8,11},{9,8},{10,9... | collective-permute-start | bytes 1277960 | tf_op jit(solution)/shard_map/ppermute | solution.py:347
  17.6 16.9 %collective-permute-start.1 = (bf16[128,1664]{1,0:T(8,128)(2,1)S(1)}, bf16[128,1664]{1,0:T(8,128)(2,1)S(1)}, u32[]{:S(2)}, u32[]{:S(2)}) collective-permute-start(bf16[128,1664]{1,0:T(8,128)(2,1)S(1)} %collective-permute-done.refs_0_), channel_id=1, source_target_pairs={{0,1},{1,2},{2,3},{3,0},{4,5},{5,6},{6,7},{7,4},{8,9},{9,10},{10,1... | collective-permute-start | bytes 1277960 | tf_op jit(solution)/shard_map/ppermute | solution.py:346
  17.7 16.8 %collective-permute-start.3 = (bf16[128,1664]{1,0:T(8,128)(2,1)S(1)}, bf16[128,1664]{1,0:T(8,128)(2,1)S(1)}, u32[]{:S(2)}, u32[]{:S(2)}) collective-permute-start(bf16[128,1664]{1,0:T(8,128)(2,1)S(1)} %collective-permute-done.2.refs_1_), channel_id=1, source_target_pairs={{0,3},{1,0},{2,1},{3,2},{4,7},{5,4},{6,5},{7,6},{8,11},{9,8},{10,9... | collective-permute-start | bytes 1277960 | tf_op jit(solution)/shard_map/ppermute | solution.py:347
  28.5 9.4 %slice-start.4 = ((s8[4718592]{0:T(1024)(128)(4,1)}), s8[4194304]{0:T(1024)(128)(4,1)S(1)}, s32[]{:S(2)}) async-start(s8[4718592]{0:T(1024)(128)(4,1)} %bitcast.8), calls=%async_computation.4 | async-start | bytes 8388608
  33.6 4.3 %slice-start.5 = ((s8[4718592]{0:T(1024)(128)(4,1)}), s8[524288]{0:T(1024)(128)(4,1)S(1)}, s32[]{:S(2)}) async-start(s8[4718592]{0:T(1024)(128)(4,1)} %bitcast.8), calls=%async_computation.5 | async-start | bytes 1048576
  33.6 4.3 %copy-start.1 = (bf16[1,256,1536]{2,1,0:T(8,128)(2,1)S(1)}, bf16[1,256,1536]{2,1,0:T(8,128)(2,1)}, u32[]{:S(2)}) copy-start(bf16[1,256,1536]{2,1,0:T(8,128)(2,1)} %param.7) | copy-start | bytes 2359300
  41.5 2.7 %collective-permute-start.6 = (bf16[128,1536]{1,0:T(8,128)(2,1)S(1)}, bf16[128,1536]{1,0:T(8,128)(2,1)S(1)}, u32[]{:S(2)}, u32[]{:S(2)}) collective-permute-start(bf16[128,1536]{1,0:T(8,128)(2,1)S(1)} %get-tuple-element.68), channel_id=1, source_target_pairs={{0,4},{4,0},{8,12},{12,8},{16,20},{20,16},{24,28},{28,24},{32,36},... | collective-permute-start | bytes 1179656 | tf_op jit(solution)/shard_map/ppermute | solution.py:328
  44.7 5.3 %collective-permute-start.7 = (bf16[32,1536]{1,0:T(8,128)(2,1)S(1)}, bf16[32,1536]{1,0:T(8,128)(2,1)S(1)}, u32[]{:S(2)}, u32[]{:S(2)}) collective-permute-start(bf16[32,1536]{1,0:T(8,128)(2,1)S(1)} %get-tuple-element.70), channel_id=1, source_target_pairs={{0,8},{4,12},{8,16},{12,20},{16,24},{20,28},{24,0},{28,4},{32,40},... | collective-permute-start | bytes 294920 | tf_op jit(solution)/shard_map/ppermute | solution.py:330
  46.0 7.1 %collective-permute-start.8 = (bf16[32,1536]{1,0:T(8,128)(2,1)S(1)}, bf16[32,1536]{1,0:T(8,128)(2,1)S(1)}, u32[]{:S(2)}, u32[]{:S(2)}) collective-permute-start(bf16[32,1536]{1,0:T(8,128)(2,1)S(1)} %get-tuple-element.71), channel_id=1, source_target_pairs={{0,16},{4,20},{8,24},{12,28},{16,0},{20,4},{24,8},{28,12},{32,48},... | collective-permute-start | bytes 294920 | tf_op jit(solution)/shard_map/ppermute | solution.py:330
  48.5 4.7 %collective-permute-start.9 = (bf16[32,1536]{1,0:T(8,128)(2,1)S(1)}, bf16[32,1536]{1,0:T(8,128)(2,1)S(1)}, u32[]{:S(2)}, u32[]{:S(2)}) collective-permute-start(bf16[32,1536]{1,0:T(8,128)(2,1)S(1)} %get-tuple-element.72), channel_id=1, source_target_pairs={{0,24},{4,28},{8,0},{12,4},{16,8},{20,12},{24,16},{28,20},{32,56},... | collective-permute-start | bytes 294920 | tf_op jit(solution)/shard_map/ppermute | solution.py:330
  53.2 5.1 %collective-permute-start.10 = (bf16[32,1536]{1,0:T(8,128)(2,1)S(1)}, bf16[32,1536]{1,0:T(8,128)(2,1)S(1)}, u32[]{:S(2)}, u32[]{:S(2)}) collective-permute-start(bf16[32,1536]{1,0:T(8,128)(2,1)S(1)} %shard_map.82), channel_id=1, source_target_pairs={{0,32},{4,36},{8,40},{12,44},{16,48},{20,52},{24,56},{28,60},{32,6... | collective-permute-start | bytes 294920 | tf_op jit(solution)/shard_map/ppermute | solution.py:332
  54.5 6.1 %collective-permute-start.11 = (bf16[32,1536]{1,0:T(8,128)(2,1)S(1)}, bf16[32,1536]{1,0:T(8,128)(2,1)S(1)}, u32[]{:S(2)}, u32[]{:S(2)}) collective-permute-start(bf16[32,1536]{1,0:T(8,128)(2,1)S(1)} %shard_map.82), channel_id=1, source_target_pairs={{0,64},{4,68},{8,72},{12,76},{16,80},{20,84},{24,88},{28,92},{32,9... | collective-permute-start | bytes 294920 | tf_op jit(solution)/shard_map/ppermute | solution.py:332
  57.2 4.6 %collective-permute-start.12 = (bf16[32,1536]{1,0:T(8,128)(2,1)S(1)}, bf16[32,1536]{1,0:T(8,128)(2,1)S(1)}, u32[]{:S(2)}, u32[]{:S(2)}) collective-permute-start(bf16[32,1536]{1,0:T(8,128)(2,1)S(1)} %shard_map.82), channel_id=1, source_target_pairs={{0,96},{4,100},{8,104},{12,108},{16,112},{20,116},{24,120},{28,124... | collective-permute-start | bytes 294920 | tf_op jit(solution)/shard_map/ppermute | solution.py:332
  62.6 5.8 %collective-permute-start.13 = (bf16[32,1536]{1,0:T(8,128)(2,1)S(1)}, bf16[32,1536]{1,0:T(8,128)(2,1)S(1)}, u32[]{:S(2)}, u32[]{:S(2)}) collective-permute-start(bf16[32,1536]{1,0:T(8,128)(2,1)S(1)} %get-tuple-element.74), channel_id=1, source_target_pairs={{0,8},{4,12},{8,16},{12,20},{16,24},{20,28},{24,0},{28,4},{32,40},... | collective-permute-start | bytes 294920 | tf_op jit(solution)/shard_map/ppermute | solution.py:334
  63.1 5.3 %collective-permute-start.14 = (bf16[32,1536]{1,0:T(8,128)(2,1)S(1)}, bf16[32,1536]{1,0:T(8,128)(2,1)S(1)}, u32[]{:S(2)}, u32[]{:S(2)}) collective-permute-start(bf16[32,1536]{1,0:T(8,128)(2,1)S(1)} %get-tuple-element.75), channel_id=1, source_target_pairs={{0,16},{4,20},{8,24},{12,28},{16,0},{20,4},{24,8},{28,12},{32,48},... | collective-permute-start | bytes 294920 | tf_op jit(solution)/shard_map/ppermute | solution.py:334
  65.1 4.2 %collective-permute-start.15 = (bf16[32,1536]{1,0:T(8,128)(2,1)S(1)}, bf16[32,1536]{1,0:T(8,128)(2,1)S(1)}, u32[]{:S(2)}, u32[]{:S(2)}) collective-permute-start(bf16[32,1536]{1,0:T(8,128)(2,1)S(1)} %get-tuple-element.76), channel_id=1, source_target_pairs={{0,24},{4,28},{8,0},{12,4},{16,8},{20,12},{24,16},{28,20},{32,56},... | collective-permute-start | bytes 294920 | tf_op jit(solution)/shard_map/ppermute | solution.py:334
  70.1 5.0 %collective-permute-start.16 = (bf16[128,1536]{1,0:T(8,128)(2,1)S(1)}, bf16[128,1536]{1,0:T(8,128)(2,1)S(1)}, u32[]{:S(2)}, u32[]{:S(2)}) collective-permute-start(bf16[128,1536]{1,0:T(8,128)(2,1)S(1)} %get-tuple-element.78), channel_id=1, source_target_pairs={{0,4},{4,0},{8,12},{12,8},{16,20},{20,16},{24,28},{28,24},{32,36},... | collective-permute-start | bytes 1179656 | tf_op jit(solution)/shard_map/ppermute | solution.py:338
  (5 other events, 11.2 us)

commit v5 on v4

v5 whole, which is shorter than its diff:
```python
import functools
import math

import jax
import jax.numpy as jnp
from jax import lax
from jax.experimental import pallas as pl
from jax.experimental.pallas import tpu as pltpu
from jax.sharding import PartitionSpec as P

D = 1536
HEAD = 128
HEADS = D // HEAD
TILE = 512
TILES = D // TILE
MESSAGE_VMEM = 63 << 20
HINT = 1 << 33
WIDE = D + HEAD
VMEM = 16 << 20
epsilon = 1e-06
EXP_SCALE = HEAD ** (-0.5) * math.log2(math.e)
f32, bf16 = jnp.float32, jnp.bfloat16


def modulation_kernel(times, weight, first, second, shift, scale, gate, rates, bare_first, bare_second):
    rows, freq = 16, HEAD
    bare_first[...] = first[:, :D]
    bare_second[...] = second[:, :D]
    lane = lax.broadcasted_iota(jnp.int32, (rows, freq), 1)
    row = lax.broadcasted_iota(jnp.int32, (rows, 2 * freq), 0)
    t = jnp.full((rows, freq), times[0, 0], jnp.int32).astype(f32)
    angles = t * jnp.exp(-math.log(10000.0) * lane.astype(f32) / freq)
    embedded = jnp.concatenate([jnp.cos(angles), jnp.sin(angles)], axis=1)
    high = embedded.astype(bf16).astype(f32)
    middle = (embedded - high).astype(bf16).astype(f32)
    low = embedded - high - middle
    terms = jnp.where(row == 0, high, jnp.where(row == 1, middle, jnp.where(row == 2, low, 0.0))).astype(bf16)
    for g, out in enumerate((shift, scale, gate)):
        product = jnp.dot(terms, weight[:, g * D : (g + 1) * D], preferred_element_type=f32)
        out[...] = jnp.sum(product, axis=0, keepdims=True)
    half_width = HEAD // 2
    lane = lax.broadcasted_iota(jnp.int32, (1, HEAD), 1)
    rates[0:1, :] = jnp.exp(-math.log(10000.0) * (lane & (half_width - 1)).astype(f32) / half_width)
    rates[1:2, :] = jnp.where(lane < half_width, -1.0, 1.0)


def modulation(step_times, time_weight, first, second):
    half = first.shape[0]
    vm = pl.BlockSpec(memory_space=pltpu.VMEM)
    return pl.pallas_call(
        modulation_kernel,
        in_specs=[pl.BlockSpec(memory_space=pltpu.SMEM), vm, vm, vm],
        out_specs=[vm] * 6,
        out_shape=[pltpu.VMEM((1, D), f32)] * 3 + [pltpu.VMEM((2, HEAD), f32)] + [pltpu.VMEM((half, D), bf16)] * 2,
        cost_estimate=pl.CostEstimate(flops=HINT, bytes_accessed=0, transcendentals=0),
        compiler_params=pltpu.CompilerParams(vmem_limit_bytes=3 << 20),
    )(step_times, time_weight, first, second)


def message_kernel(x, positions_any, first, second, positions, sems):
    rows = first.shape[0]
    ids_load = pltpu.make_async_copy(positions_any, positions, sems.at[2])
    ids_load.start()
    copies = [
        pltpu.make_async_copy(x.at[pl.ds(j * rows, rows), :], out.at[:, pl.ds(0, D)], sems.at[j])
        for j, out in enumerate((first, second))
    ]
    for copy in copies:
        copy.start()
    lane = lax.broadcasted_iota(jnp.int32, (rows, HEAD), 1)
    row = lax.broadcasted_iota(jnp.int32, (rows, HEAD), 0)
    ids_load.wait()
    digits = []
    for j in range(2):
        spread = jnp.where(row == lane, positions[j : j + 1, :], 0).astype(f32)
        ids = jnp.sum(spread, axis=1, keepdims=True).astype(jnp.int32)
        digits.append((ids >> 5, ids & 31))
    for j, out in enumerate((first, second)):
        mine, others = digits[j], digits[1 - j]
        four = jnp.where(lane == 2, others[0], jnp.where(lane == 3, others[1], 0))
        four = jnp.where(lane == 0, mine[0], jnp.where(lane == 1, mine[1], four))
        out[:, D:] = four.astype(f32).astype(bf16)
    for copy in copies:
        copy.wait()


def with_positions(x, positions):
    half = x.shape[0] // 2
    anywhere = pl.BlockSpec(memory_space=pl.ANY)
    return pl.pallas_call(
        message_kernel,
        in_specs=[anywhere] * 2,
        out_specs=[pl.BlockSpec(memory_space=pltpu.VMEM)] * 2,
        out_shape=[pltpu.VMEM((half, WIDE), bf16)] * 2,
        scratch_shapes=[
            pltpu.VMEM((2, half), jnp.int32),
            pltpu.SemaphoreType.DMA((3,)),
        ],
        cost_estimate=pl.CostEstimate(flops=HINT, bytes_accessed=0, transcendentals=0),
        compiler_params=pltpu.CompilerParams(vmem_limit_bytes=MESSAGE_VMEM),
    )(x, positions.reshape(2, half))


def norm_rope(proj, gain, cos, sin, out_ref):
    rows = proj.shape[0]
    total = jnp.zeros((rows, HEAD), f32)
    for h in range(HEADS):
        p = proj[:, h * HEAD : (h + 1) * HEAD]
        total = total + p * p
    inv = lax.rsqrt(jnp.sum(total, axis=1, keepdims=True) * (1.0 / D) + epsilon)
    for h in range(HEADS):
        at = slice(h * HEAD, (h + 1) * HEAD)
        y = proj[:, at] * inv * gain[:, at]
        out_ref[:, at] = (y * cos + pltpu.roll(y, HEAD // 2, 1) * sin).astype(bf16)


def project_kernel(with_q, n_ids, *refs):
    x_refs, id_refs, (shift, scale, gains, rates, w) = refs[:2], refs[2 : 2 + n_ids], refs[2 + n_ids : 7 + n_ids]
    outs, (normed, proj) = refs[7 + n_ids : -2], refs[-2:]
    at, angles = 0, []
    for x_ref, ids in zip(x_refs, id_refs or x_refs):
        rows = x_ref.shape[0]
        x = x_ref[:, :D].astype(f32)
        inv = lax.rsqrt(jnp.sum(x * x, axis=1, keepdims=True) * (1.0 / D) + epsilon)
        normed[pl.ds(at, rows), :] = (x * inv * (1.0 + scale[...]) + shift[...]).astype(bf16)
        digits = ids[:, D:].astype(f32)
        angles.append((digits[:, n_ids : n_ids + 1] * 32.0 + digits[:, n_ids + 1 : n_ids + 2]) * rates[0:1, :])
        at += rows
    angles = jnp.concatenate(angles, axis=0)
    cos, sin = jnp.cos(angles), jnp.sin(angles) * rates[1:2, :]
    names = ["q", "k", "v"] if with_q else ["k", "v"]
    out_of = dict(zip(names, outs))
    first = {"q": 0, "k": TILES, "v": 2 * TILES}
    for g, name in enumerate(["k", "q", "v"] if with_q else ["k", "v"]):
        for t in range(TILES):
            at = slice(t * TILE, (t + 1) * TILE)
            col = (first[name] + t) * TILE
            acc = jnp.dot(normed[...], w[:, col : col + TILE], preferred_element_type=f32)
            if name == "v":
                out_of[name][:, at] = acc.astype(bf16)
            else:
                proj[g, :, at] = acc
        if name != "v":
            row = 1 if name == "k" else 0
            norm_rope(proj.at[g], gains[row : row + 1, :], cos, sin, out_of[name])


def project(xs, ids, shift, scale, gains, rates, w_qkv, with_q):
    rows = sum(x.shape[0] for x in xs)
    groups = 3 if with_q else 2
    vm = pl.BlockSpec(memory_space=pltpu.VMEM)
    return pl.pallas_call(
        functools.partial(project_kernel, with_q, len(ids)),
        in_specs=[vm] * (7 + len(ids)),
        out_specs=[vm] * groups,
        out_shape=[pltpu.VMEM((rows, D), bf16)] * groups,
        scratch_shapes=[pltpu.VMEM((rows, D), bf16), pltpu.VMEM((groups - 1, rows, D), f32)],
        cost_estimate=pl.CostEstimate(
            flops=2 * rows * D * D * groups, bytes_accessed=2 * D * D * groups, transcendentals=0
        ),
        compiler_params=pltpu.CompilerParams(vmem_limit_bytes=8 << 20),
    )(*xs, *ids, shift, scale, gains, rates, w_qkv)


def merge(new, total, acc, old, old_total, old_acc):
    m = jnp.maximum(new, old)
    fade_old, fade_new = jnp.exp2(old - m), jnp.exp2(new - m)
    return m, old_total * fade_old + total * fade_new, old_acc * fade_old + acc * fade_new


def attend_kernel(n_kv, q_ref, *refs):
    kv, before, (m_ref, l_ref, acc_ref) = refs[: 2 * n_kv], refs[2 * n_kv : -3], refs[-3:]
    rows = q_ref.shape[0]
    for h in range(HEADS):
        at = slice(h * HEAD, (h + 1) * HEAD)
        q = q_ref[:, at]
        scores = [
            lax.dot_general(q, kv[2 * j][:, at], (((1,), (1,)), ((), ())), preferred_element_type=f32)
            for j in range(n_kv)
        ]
        top = scores[0]
        for s in scores[1:]:
            top = jnp.maximum(top, s)
        m = jnp.max(top, axis=1, keepdims=True) * EXP_SCALE
        total = jnp.zeros((rows, 1), f32)
        acc = jnp.zeros((rows, HEAD), f32)
        for j in range(n_kv):
            p = jnp.exp2(scores[j] * EXP_SCALE - m)
            total = total + jnp.sum(p, axis=1, keepdims=True)
            acc = acc + jnp.dot(p.astype(bf16), kv[2 * j + 1][:, at], preferred_element_type=f32)
        m = jnp.broadcast_to(m, (rows, HEAD))
        total = jnp.broadcast_to(total, (rows, HEAD))
        if before:
            m, total, acc = merge(m, total, acc, before[0][h], before[1][h], before[2][:, at])
        m_ref[h] = m
        l_ref[h] = total
        acc_ref[:, at] = acc


def attend(q, kvs, before=()):
    rows = q.shape[0]
    keys = sum(k.shape[0] for k, _ in kvs)
    flat = [a for pair in kvs for a in pair]
    vm = pl.BlockSpec(memory_space=pltpu.VMEM)
    return pl.pallas_call(
        functools.partial(attend_kernel, len(kvs)),
        in_specs=[vm] * (1 + len(flat) + len(before)),
        out_specs=[vm] * 3,
        out_shape=[
            pltpu.VMEM((HEADS, rows, HEAD), f32),
            pltpu.VMEM((HEADS, rows, HEAD), f32),
            pltpu.VMEM((rows, D), f32),
        ],
        cost_estimate=pl.CostEstimate(
            flops=8 * rows * D * keys, bytes_accessed=4 * rows * D * 2, transcendentals=rows * keys * HEADS
        ),
        compiler_params=pltpu.CompilerParams(vmem_limit_bytes=12 << 20),
    )(q, *flat, *before)


def finish_kernel(theirs, times, place, q_ref, k_ref, v_ref, m_ref, l_ref, acc_ref, x_ref, gate_ref, w_ref, *refs):
    out_ref, attended = refs[0], refs[-1]
    half = out_ref.shape[0]
    which = 1 - place[0] if theirs else place[0]
    rows = pl.ds(pl.multiple_of(which * half, half), half)
    for h in range(HEADS):
        at = slice(h * HEAD, (h + 1) * HEAD)
        s = lax.dot_general(
            q_ref[rows, at], k_ref[:, at], (((1,), (1,)), ((), ())), preferred_element_type=f32
        )
        new = jnp.max(s, axis=1, keepdims=True) * EXP_SCALE
        p = jnp.exp2(s * EXP_SCALE - new)
        total = jnp.broadcast_to(jnp.sum(p, axis=1, keepdims=True), (half, HEAD))
        acc = jnp.dot(p.astype(bf16), v_ref[:, at], preferred_element_type=f32)
        new = jnp.broadcast_to(new, (half, HEAD))
        _, total, acc = merge(new, total, acc, m_ref[h, rows, :], l_ref[h, rows, :], acc_ref[rows, at])
        attended[:, at] = (acc / total).astype(bf16)
    size = jnp.full((1, TILE), times[0, 1] - times[0, 0], jnp.int32).astype(f32) / 1000.0
    for t in range(TILES):
        at = slice(t * TILE, (t + 1) * TILE)
        proj = jnp.dot(attended[...], w_ref[:, at], preferred_element_type=f32)
        inc = size * (x_ref[rows, at].astype(f32) + gate_ref[:, at] * proj)
        out_ref[:, at] = inc
        if theirs:
            refs[1][:, at] = inc.astype(bf16)


def finish(theirs, step_times, place, q, kv, state, x, gate, w_out):
    half = q.shape[0] // 2
    keys = kv[0].shape[0]
    vm = pl.BlockSpec(memory_space=pltpu.VMEM)
    outs = [pltpu.VMEM((half, D), f32)] + [pltpu.VMEM((half, D), bf16)] * theirs
    return pl.pallas_call(
        functools.partial(finish_kernel, theirs),
        in_specs=[pl.BlockSpec(memory_space=pltpu.SMEM)] * 2 + [vm] * 9,
        out_specs=[vm] * len(outs),
        out_shape=outs,
        scratch_shapes=[pltpu.VMEM((half, D), bf16)],
        cost_estimate=pl.CostEstimate(
            flops=8 * half * D * keys + 2 * half * D * D,
            bytes_accessed=2 * D * D,
            transcendentals=half * keys * HEADS,
        ),
        compiler_params=pltpu.CompilerParams(vmem_limit_bytes=12 << 20),
    )(step_times, place, q, *kv, *state, x, gate, w_out)


def split_kernel(place, mine, got, own, *pieces):
    xx = place[1]
    part = own.shape[0]
    for k, out in enumerate((own,) + pieces):
        at = pl.multiple_of(((xx + k) & 3) * part, part)
        both = mine[pl.ds(at, part), :] + got[pl.ds(at, part), :].astype(f32)
        out[...] = both.astype(out.dtype)


def row_kernel(own, one, two, three, out):
    out[...] = (own[...] + one[...].astype(f32) + two[...].astype(f32) + three[...].astype(f32)).astype(bf16)


def before_kernel(place, own, *refs):
    xs, ys, outs = refs[:3], refs[3:6], refs[6:]
    xx, yy = place[1], place[2]
    above = jnp.zeros(own.shape, f32)
    for k in (1, 2, 3):
        above = above + jnp.where(((yy - k) & 3) < yy, ys[k - 1][...].astype(f32), 0.0)
    src = [own[...]] + [r[...].astype(f32) for r in xs]
    for k, out in enumerate(outs):
        total = above
        for j in range(4):
            total = total + jnp.where(((xx - j) & 3) < ((xx + k) & 3), src[j], 0.0)
        out[...] = total.astype(out.dtype)


def given_kernel(place, mine, *refs):
    pieces, given = refs[:4], refs[4]
    c, xx = place[0], place[1]
    part = pieces[0].shape[0]
    for k in range(4):
        at = pl.ds(pl.multiple_of(((xx - k) & 3) * part, part), part)
        given[at, :] = (pieces[k][...].astype(f32) + jnp.where(c == 0, mine[at, :], 0.0)).astype(bf16)


def own_half_kernel(place, mine, got, *refs):
    pieces, (out, held, sem) = refs[:4], refs[4:]
    c, xx = place[0], place[1]
    part, half = pieces[0].shape[0], held.shape[0]
    for k in range(4):
        at = pl.ds(pl.multiple_of(((xx - k) & 3) * part, part), part)
        held[at, :] = pieces[k][...].astype(f32) + mine[at, :] + jnp.where(c == 0, 0.0, got[at, :].astype(f32))
    store = pltpu.make_async_copy(held, out.at[pl.ds(pl.multiple_of(c * half, half), half), :], sem)
    store.start()
    store.wait()


def other_half_kernel(place, theirs, other, begun, out, held, sem):
    half = held.shape[0]
    held[...] = other[...].astype(f32) + theirs[...]
    at = pl.multiple_of((1 - place[0]) * half, half)
    store = pltpu.make_async_copy(held, out.at[pl.ds(at, half), :], sem)
    store.start()
    store.wait()


def store_call(kernel, place, args, begun, rows):
    vm, anywhere = pl.BlockSpec(memory_space=pltpu.VMEM), pl.BlockSpec(memory_space=pl.ANY)
    return pl.pallas_call(
        kernel,
        in_specs=[pl.BlockSpec(memory_space=pltpu.SMEM)] + [vm] * len(args) + [anywhere] * len(begun),
        out_specs=anywhere,
        out_shape=jax.ShapeDtypeStruct((rows, D), f32),
        scratch_shapes=[pltpu.VMEM((rows // 2, D), f32), pltpu.SemaphoreType.DMA],
        input_output_aliases={1 + len(args): 0} if begun else {},
        cost_estimate=pl.CostEstimate(flops=0, bytes_accessed=6 * rows * D, transcendentals=0),
        compiler_params=pltpu.CompilerParams(vmem_limit_bytes=4 << 20),
    )(place, *args, *begun)


def small_call(kernel, place, args, outs):
    vm = pl.BlockSpec(memory_space=pltpu.VMEM)
    head = [] if place is None else [place]
    return pl.pallas_call(
        kernel,
        in_specs=[pl.BlockSpec(memory_space=pltpu.SMEM)] * len(head) + [vm] * len(args),
        out_specs=[vm] * len(outs),
        out_shape=outs,
        compiler_params=pltpu.CompilerParams(vmem_limit_bytes=3 << 20),
    )(*head, *args)


def scan_steps(place, mine, theirs, sent):
    half = mine.shape[0]
    part = half // 4
    pair = [(i, i ^ 1) for i in range(32)]
    ring = range(4)

    def along_x(k):
        return [((y * 4 + x) * 2 + c, (y * 4 + (x + k) % 4) * 2 + c) for y in ring for x in ring for c in (0, 1)]

    def along_y(k):
        return [((y * 4 + x) * 2 + c, ((y + k) % 4 * 4 + x) * 2 + c) for y in ring for x in ring for c in (0, 1)]

    narrow, wide = pltpu.VMEM((part, D), bf16), pltpu.VMEM((part, D), f32)
    got = lax.ppermute(sent, "step", pair)
    own, *pieces = small_call(split_kernel, place, (mine, got), [wide] + [narrow] * 3)
    xs = [lax.ppermute(piece, "step", along_x(k)) for k, piece in zip((1, 2, 3), pieces)]
    (row,) = small_call(row_kernel, None, (own, *xs), [narrow])
    ys = [lax.ppermute(row, "step", along_y(k)) for k in (1, 2, 3)]
    home, *away = small_call(before_kernel, place, (own, *xs, *ys), [wide] + [narrow] * 3)
    back = [lax.ppermute(piece, "step", along_x(k)) for k, piece in zip((1, 2, 3), away)]
    (given,) = small_call(given_kernel, place, (mine, home, *back), [pltpu.VMEM((half, D), bf16)])
    other = lax.ppermute(given, "step", pair)
    begun = store_call(own_half_kernel, place, (mine, got, home, *back), (), 2 * half)
    return store_call(other_half_kernel, place, (theirs, other), (begun,), 2 * half)


def on_device(states, step_times, positions, w_qkv, qk_gain, w_out, time_weight):
    n = lax.axis_size("seq")
    right = [(i, (i + 1) % n) for i in range(n)]
    left = [(i, (i - 1) % n) for i in range(n)]
    to_right = lambda v: lax.ppermute(v, "seq", right)
    to_left = lambda v: lax.ppermute(v, "seq", left)
    step = lax.axis_index("step")
    place = jnp.stack([step % 2, (step // 2) % 4, step // 8])

    x = states[0]
    first, second = with_positions(x, positions)
    r_first, l_second = to_right(first), to_left(second)
    modulated = modulation(step_times, time_weight, first, second)
    shift, scale, gate, rates, bare_first, bare_second, place = lax.optimization_barrier((*modulated, place))
    r_second, l_first = to_right(bare_second), to_left(bare_first)
    forward = to_right(r_first), to_left(l_second)

    given = (shift, scale, qk_gain, rates, w_qkv)
    q, k, v = project((first, second), (), *given, True)
    near = project((r_first, l_second), (), *given, False)
    next_near = project((r_second, l_first), (r_first, l_second), *given, False)
    far = project(forward, (), *given, False)
    state = attend(q, [next_near], attend(q, [(k, v), near]))
    late = (step_times, place, q, far, state, x, gate, w_out)
    theirs, sent = finish(True, *late)
    (mine,) = finish(False, *late)
    return scan_steps(place, mine, theirs, sent)[None]


def solution(mesh):
    placed = (P("step", "seq", None), P("step", None), P("seq"), P(), P(), P(), P())
    return jax.shard_map(
        on_device, mesh=mesh, in_specs=placed, out_specs=P("step", "seq", None), check_vma=False
    )
```

time: 77.1 us -> 75.3 us (0.977)
  waiting for transfers between devices: 15.5 us -> 10.7 us
  Pallas kernels: 27.9 us -> 31.9 us
  local copies, waits for them, and re-layouts: 4.53 us -> 2.7 us
  starting transfers between devices: 28.7 us -> 29.5 us
    pallas_call x6 -> x9, Pallas kernels: 17.7 us -> 23.1 us  [the longest x4 14 us: project(): pl.pallas_call(functools.partial(project_kernel, with_q, len(ids)), in_sp...]
    pallas_call x5 -> x4, Pallas kernels: 4.11 us -> 2.12 us  [small_call(): pl.pallas_call(kernel, in_specs=[pl.BlockSpec(memory_space=pltpu.SMEM)] *...]
    unnamed x24 -> x20, local copies, waits for them, and re-layouts: 4.53 us -> 2.7 us
    ppermute x1, waiting for transfers between devices: 1.35 us -> 0.01 us  [scan_steps(): other = lax.ppermute(given, 'step', pair)]
    ppermute x1, waiting for transfers between devices: 1.35 us -> 0.01 us  [scan_steps(): got = lax.ppermute(sent, 'step', pair)]
    ppermute x3, waiting for transfers between devices: 2.71 us -> 1.41 us  [on_device(): to_right = lambda v: lax.ppermute(v, 'seq', right)]
    ppermute x6, starting transfers between devices: 8.57 us -> 9.69 us  [scan_steps(): lax.ppermute(piece, 'step', along_x(k))]
    pallas_call x1 -> x2, Pallas kernels: 5.08 us -> 5.63 us  [attend(): pl.pallas_call(functools.partial(attend_kernel, len(kvs)), in_specs=[vm]...]
  transfers between devices with their start and end apart: 17 -> 17, of which waited for: 10 -> 7; matrix products, arithmetic and copies ran while one was open for 0% -> 0% of each run, Pallas kernels for 22% -> 28%
where the time goes in v5:
time: 75.3 us; the launch traced here: 75.2 us
  Pallas kernels  31.9 us (42%)
  starting transfers between devices  29.5 us (39%)
  waiting for transfers between devices  10.7 us (14%)
  local copies, waits for them, and re-layouts  2.7 us (4%)
    pallas_call x4, Pallas kernels, project(): pl.pallas_call(functools.partial(project_kernel, with_q, len(ids)), in_sp...  14 us
    ppermute x6, starting transfers between devices, scan_steps(): lax.ppermute(piece, 'step', along_x(k))  9.69 us
    ppermute x3, starting transfers between devices, on_device(): to_left = lambda v: lax.ppermute(v, 'seq', left)  7.52 us
    ppermute x6, waiting for transfers between devices, scan_steps(): lax.ppermute(piece, 'step', along_x(k))  6.37 us
    pallas_call x2, Pallas kernels, attend(): pl.pallas_call(functools.partial(attend_kernel, len(kvs)), in_specs=[vm]...  5.63 us
    ppermute x3, starting transfers between devices, scan_steps(): ys = [lax.ppermute(row, 'step', along_y(k)) for k in (1, 2, 3)]  5.06 us
    pallas_call x2, Pallas kernels, finish(): pl.pallas_call(functools.partial(finish_kernel, theirs), in_specs=[pl.Blo...  4.8 us
    ppermute x1, starting transfers between devices, scan_steps(): other = lax.ppermute(given, 'step', pair)  3.25 us
  transfers between devices with their start and end apart: 17, of which 7 were waited for; matrix products, arithmetic and copies ran while one was open for 0% of the time, Pallas kernels for 28%

profile of v5, /device:TPU:1, one launch (start us, length us, event | category | flops | bytes accessed | tf_op | source)
XLA Modules:
  0.0 75.2 jit_solution(6900211124080157381)
XLA Ops:
  1.2 2.5 %collective-permute-start = (bf16[128,1664]{1,0:T(8,128)(2,1)S(1)}, bf16[128,1664]{1,0:T(8,128)(2,1)S(1)}, u32[]{:S(2)}, u32[]{:S(2)}) collective-permute-start(bf16[128,1664]{1,0:T(8,128)(2,1)S(1)} %get-tuple-element.45.first.refs_0_), channel_id=1, source_target_pairs={{0,1},{1,2},{2,3},{3,0},{4,5},{5,6},{6,7},{7,4},{8,9},{9,10},{10,1... | collective-permute-start | bytes 1277960 | tf_op jit(solution)/shard_map/ppermute | solution.py:381
  3.7 2.2 %collective-permute-start.2 = (bf16[128,1664]{1,0:T(8,128)(2,1)S(1)}, bf16[128,1664]{1,0:T(8,128)(2,1)S(1)}, u32[]{:S(2)}, u32[]{:S(2)}) collective-permute-start(bf16[128,1664]{1,0:T(8,128)(2,1)S(1)} %get-tuple-element.46.second.refs_1_), channel_id=1, source_target_pairs={{0,3},{1,0},{2,1},{3,2},{4,7},{5,4},{6,5},{7,6},{8,11},{9,8},{10,9... | collective-permute-start | bytes 1277960 | tf_op jit(solution)/shard_map/ppermute | solution.py:382
  5.9 1.8 %copy-done.3 = bf16[256,4608]{1,0:T(8,128)(2,1)S(1)} copy-done((bf16[256,4608]{1,0:T(8,128)(2,1)S(1)}, bf16[256,4608]{1,0:T(8,128)(2,1)}, u32[]{:S(2)}) %copy-start.3) | copy-done | bytes 2359320
  8.8 2.7 %collective-permute-start.5 = (bf16[128,1536]{1,0:T(8,128)(2,1)S(1)}, bf16[128,1536]{1,0:T(8,128)(2,1)S(1)}, u32[]{:S(2)}, u32[]{:S(2)}) collective-permute-start(bf16[128,1536]{1,0:T(8,128)(2,1)S(1)} %get-tuple-element.61), channel_id=1, source_target_pairs={{0,3},{1,0},{2,1},{3,2},{4,7},{5,4},{6,5},{7,6},{8,11},{9,8},{10,9... | collective-permute-start | bytes 1179656 | tf_op jit(solution)/shard_map/ppermute | solution.py:382
  12.4 4.4 %shard_map.75 = (bf16[256,1536]{1,0:T(8,128)(2,1)S(1)}, bf16[256,1536]{1,0:T(8,128)(2,1)S(1)}, bf16[256,1536]{1,0:T(8,128)(2,1)S(1)}) custom-call(bf16[128,1664]{1,0:T(8,128)(2,1)S(1)} %get-tuple-element.45.first.refs_0_, bf16[128,1664]{1,0:T(8,128)(2,1)S(1)} %get-tuple-element.46.second.refs_1_, f32[1,1536]{1,0:T(1,128)S(1)} %get-tuple-element.54.refs_2_.refs_4_, ...), custom_call_target="tpu_custom_call" | custom-call | flops 3623878656 | bytes 14155776 | tf_op jit(solution)/shard_map/pallas_call | solution.py:152
  16.9 2.7 %collective-permute-start.3 = (bf16[128,1664]{1,0:T(8,128)(2,1)S(1)}, bf16[128,1664]{1,0:T(8,128)(2,1)S(1)}, u32[]{:S(2)}, u32[]{:S(2)}) collective-permute-start(bf16[128,1664]{1,0:T(8,128)(2,1)S(1)} %collective-permute-done.2.refs_3_.refs_1_), channel_id=1, source_target_pairs={{0,3},{1,0},{2,1},{3,2},{4,7},{5,4},{6,5},{7,6},{8,11},{9,8},{10,9... | collective-permute-start | bytes 1277960 | tf_op jit(solution)/shard_map/ppermute | solution.py:382
  19.5 3.1 %shard_map.78 = (bf16[256,1536]{1,0:T(8,128)(2,1)S(1)}, bf16[256,1536]{1,0:T(8,128)(2,1)S(1)}) custom-call(bf16[128,1664]{1,0:T(8,128)(2,1)S(1)} %collective-permute-done.refs_2_.refs_0_, bf16[128,1664]{1,0:T(8,128)(2,1)S(1)} %collective-permute-done.2.refs_3_.refs_1_, f32[1,1536]{1,0:T(1,128)S(1)} %get-tuple-element.54.refs_2_.refs_4_, ...), custom_call_target="tpu_custom_call" | custom-call | flops 2415919104 | bytes 9437184 | tf_op jit(solution)/shard_map/pallas_call | solution.py:152
  22.7 3.8 %shard_map.79 = (f32[12,256,128]{2,1,0:T(8,128)S(1)}, f32[12,256,128]{2,1,0:T(8,128)S(1)}, f32[256,1536]{1,0:T(8,128)S(1)}) custom-call(bf16[256,1536]{1,0:T(8,128)(2,1)S(1)} %get-tuple-element.57.q_ref, bf16[256,1536]{1,0:T(8,128)(2,1)S(1)} %get-tuple-element.64.refs_0_, bf16[256,1536]{1,0:T(8,128)(2,1)S(1)} %get-tuple-element.65.refs_1_, ...), custom_call_target="tpu_custom_call" | custom-call | flops 1610612736 | bytes 3145728 | tf_op jit(solution)/shard_map/pallas_call | solution.py:205
  26.5 3.2 %shard_map.77 = (bf16[256,1536]{1,0:T(8,128)(2,1)S(1)}, bf16[256,1536]{1,0:T(8,128)(2,1)S(1)}) custom-call(bf16[128,1536]{1,0:T(8,128)(2,1)S(1)} %collective-permute-done.4.refs_0_, bf16[128,1536]{1,0:T(8,128)(2,1)S(1)} %collective-permute-done.5.refs_1_, bf16[128,1664]{1,0:T(8,128)(2,1)S(1)} %collective-permute-done.refs_2_.refs_0_, ...), custom_call_target="tpu_custom_call" | custom-call | flops 2415919104 | bytes 9437184 | tf_op jit(solution)/shard_map/pallas_call | solution.py:152
  29.6 1.9 %shard_map.80 = (f32[12,256,128]{2,1,0:T(8,128)S(1)}, f32[12,256,128]{2,1,0:T(8,128)S(1)}, f32[256,1536]{1,0:T(8,128)S(1)}) custom-call(bf16[256,1536]{1,0:T(8,128)(2,1)S(1)} %get-tuple-element.57.q_ref, bf16[256,1536]{1,0:T(8,128)(2,1)S(1)} %get-tuple-element.62.refs_0_, bf16[256,1536]{1,0:T(8,128)(2,1)S(1)} %get-tuple-element.63.refs_1_, ...), custom_call_target="tpu_custom_call" | custom-call | flops 805306368 | bytes 3145728 | tf_op jit(solution)/shard_map/pallas_call | solution.py:205
  31.5 1.4 %collective-permute-done.1.refs_0_ = bf16[128,1664]{1,0:T(8,128)(2,1)S(1)} collective-permute-done((bf16[128,1664]{1,0:T(8,128)(2,1)S(1)}, bf16[128,1664]{1,0:T(8,128)(2,1)S(1)}, u32[]{:S(2)}, u32[]{:S(2)}) %collective-permute-start.1) | collective-permute-done | bytes 426016 | tf_op jit(solution)/shard_map/ppermute | solution.py:381
  32.9 3.4 %shard_map.76 = (bf16[256,1536]{1,0:T(8,128)(2,1)S(1)}, bf16[256,1536]{1,0:T(8,128)(2,1)S(1)}) custom-call(bf16[128,1664]{1,0:T(8,128)(2,1)S(1)} %collective-permute-done.1.refs_0_, bf16[128,1664]{1,0:T(8,128)(2,1)S(1)} %collective-permute-done.3.refs_1_, f32[1,1536]{1,0:T(1,128)S(1)} %get-tuple-element.54.refs_2_.refs_4_, ...), custom_call_target="tpu_custom_call" | custom-call | flops 2415919104 | bytes 9437184 | tf_op jit(solution)/shard_map/pallas_call | solution.py:152
  36.4 2.4 %shard_map.81 = (f32[128,1536]{1,0:T(8,128)S(1)}, bf16[128,1536]{1,0:T(8,128)(2,1)S(1)}) custom-call(s32[1,2]{1,0:T(1,128)S(1)} %copy-done.2, s32[3]{0:T(128)S(1)} %pad_add_fusion.place, bf16[256,1536]{1,0:T(8,128)(2,1)S(1)} %get-tuple-element.57.q_ref, bf16[256,1536]{1,0:T(8,128)(2,1)S(1)} %get-tuple-element.58.k_ref, ...), custom_call_target="tpu_custom_call" | custom-call | flops 1006632960 | bytes 4718592 | tf_op jit(solution)/shard_map/pallas_call | solution.py:253
  40.1 2.4 %shard_map.82.mine = f32[128,1536]{1,0:T(8,128)S(1)} custom-call(s32[1,2]{1,0:T(1,128)S(1)} %copy-done.2, s32[3]{0:T(128)S(1)} %pad_add_fusion.place, bf16[256,1536]{1,0:T(8,128)(2,1)S(1)} %get-tuple-element.57.q_ref, bf16[256,1536]{1,0:T(8,128)(2,1)S(1)} %get-tuple-element.58.k_ref, bf16[256,1536]{1,0:T(8,128)(2,1)S(1)} %get-tuple-element.59.v_ref, ...), custom_call_target="tpu_custom_call" | custom-call | flops 1006632960 | bytes 4718592 | tf_op jit(solution)/shard_map/pallas_call | solution.py:253
  44.4 2.4 %collective-permute-start.8 = (bf16[32,1536]{1,0:T(8,128)(2,1)S(1)}, bf16[32,1536]{1,0:T(8,128)(2,1)S(1)}, u32[]{:S(2)}, u32[]{:S(2)}) collective-permute-start(bf16[32,1536]{1,0:T(8,128)(2,1)S(1)} %get-tuple-element.79), channel_id=1, source_target_pairs={{0,16},{4,20},{8,24},{12,28},{16,0},{20,4},{24,8},{28,12},{32,48},... | collective-permute-start | bytes 294920 | tf_op jit(solution)/shard_map/ppermute | solution.py:366
  48.8 3.1 %collective-permute-done.8.two.refs_1_ = bf16[32,1536]{1,0:T(8,128)(2,1)S(1)} collective-permute-done((bf16[32,1536]{1,0:T(8,128)(2,1)S(1)}, bf16[32,1536]{1,0:T(8,128)(2,1)S(1)}, u32[]{:S(2)}, u32[]{:S(2)}) %collective-permute-start.8) | collective-permute-done | bytes 98336 | tf_op jit(solution)/shard_map/ppermute | solution.py:366
  53.3 2.6 %collective-permute-start.11 = (bf16[32,1536]{1,0:T(8,128)(2,1)S(1)}, bf16[32,1536]{1,0:T(8,128)(2,1)S(1)}, u32[]{:S(2)}, u32[]{:S(2)}) collective-permute-start(bf16[32,1536]{1,0:T(8,128)(2,1)S(1)} %shard_map.84), channel_id=1, source_target_pairs={{0,64},{4,68},{8,72},{12,76},{16,80},{20,84},{24,88},{28,92},{32,9... | collective-permute-start | bytes 294920 | tf_op jit(solution)/shard_map/ppermute | solution.py:368
  57.0 2.8 %collective-permute-done.11.refs_4_ = bf16[32,1536]{1,0:T(8,128)(2,1)S(1)} collective-permute-done((bf16[32,1536]{1,0:T(8,128)(2,1)S(1)}, bf16[32,1536]{1,0:T(8,128)(2,1)S(1)}, u32[]{:S(2)}, u32[]{:S(2)}) %collective-permute-start.11) | collective-permute-done | bytes 98336 | tf_op jit(solution)/shard_map/ppermute | solution.py:368
  60.7 1.4 %collective-permute-start.13 = (bf16[32,1536]{1,0:T(8,128)(2,1)S(1)}, bf16[32,1536]{1,0:T(8,128)(2,1)S(1)}, u32[]{:S(2)}, u32[]{:S(2)}) collective-permute-start(bf16[32,1536]{1,0:T(8,128)(2,1)S(1)} %get-tuple-element.82), channel_id=1, source_target_pairs={{0,8},{4,12},{8,16},{12,20},{16,24},{20,28},{24,0},{28,4},{32,40},... | collective-permute-start | bytes 294920 | tf_op jit(solution)/shard_map/ppermute | solution.py:370
  62.1 2.1 %collective-permute-start.14 = (bf16[32,1536]{1,0:T(8,128)(2,1)S(1)}, bf16[32,1536]{1,0:T(8,128)(2,1)S(1)}, u32[]{:S(2)}, u32[]{:S(2)}) collective-permute-start(bf16[32,1536]{1,0:T(8,128)(2,1)S(1)} %get-tuple-element.83), channel_id=1, source_target_pairs={{0,16},{4,20},{8,24},{12,28},{16,0},{20,4},{24,8},{28,12},{32,48},... | collective-permute-start | bytes 294920 | tf_op jit(solution)/shard_map/ppermute | solution.py:370
  65.5 1.8 %collective-permute-done.14.refs_2_ = bf16[32,1536]{1,0:T(8,128)(2,1)S(1)} collective-permute-done((bf16[32,1536]{1,0:T(8,128)(2,1)S(1)}, bf16[32,1536]{1,0:T(8,128)(2,1)S(1)}, u32[]{:S(2)}, u32[]{:S(2)}) %collective-permute-start.14) | collective-permute-done | bytes 98336 | tf_op jit(solution)/shard_map/ppermute | solution.py:370
  68.6 3.3 %collective-permute-start.16 = (bf16[128,1536]{1,0:T(8,128)(2,1)S(1)}, bf16[128,1536]{1,0:T(8,128)(2,1)S(1)}, u32[]{:S(2)}, u32[]{:S(2)}) collective-permute-start(bf16[128,1536]{1,0:T(8,128)(2,1)S(1)} %shard_map.86), channel_id=1, source_target_pairs={{0,4},{4,0},{8,12},{12,8},{16,20},{20,16},{24,28},{28,24},{32,36},... | collective-permute-start | bytes 1179656 | tf_op jit(solution)/shard_map/ppermute | solution.py:372
  71.9 1.6 %shard_map.87.begun = f32[256,1536]{1,0:T(8,128)} custom-call(s32[3]{0:T(128)S(1)} %pad_add_fusion.place, f32[128,1536]{1,0:T(8,128)S(1)} %shard_map.82.mine, bf16[128,1536]{1,0:T(8,128)(2,1)S(1)} %collective-permute-done.6.got, f32[32,1536]{1,0:T(8,128)S(1)} %get-tuple-element.81.refs_0_, bf16[32,1536]{1,0:T(8,128)(2,1)S(1)} %collective-permute-done.13.refs_1_, ...), custom_call_target="tpu_custom_call" | custom-call | bytes 2359296 | tf_op jit(solution)/shard_map/pallas_call | solution.py:327
  73.5 1.5 %shard_map.88 = f32[256,1536]{1,0:T(8,128)} custom-call(s32[3]{0:T(128)S(1)} %pad_add_fusion.place, f32[128,1536]{1,0:T(8,128)S(1)} %get-tuple-element.75.theirs, bf16[128,1536]{1,0:T(8,128)(2,1)S(1)} %collective-permute-done.16.other, f32[256,1536]{1,0:T(8,128)} %shard_map.87.begun), custom_call_target="tpu_custom_call", output_to_operand_aliasing={{}: (3, {})} | custom-call | bytes 2359296 | tf_op jit(solution)/shard_map/pallas_call | solution.py:327
  (49 shorter events, 14.4 us)
Async XLA Ops:
  0.0 5.9 %copy-start.2 = (s32[1,2]{1,0:T(1,128)S(1)}, s32[1,2]{1,0:T(1,128)}, u32[]{:S(2)}) copy-start(s32[1,2]{1,0:T(1,128)} %times.5) | copy-start | bytes 28
  1.2 15.6 %collective-permute-start = (bf16[128,1664]{1,0:T(8,128)(2,1)S(1)}, bf16[128,1664]{1,0:T(8,128)(2,1)S(1)}, u32[]{:S(2)}, u32[]{:S(2)}) collective-permute-start(bf16[128,1664]{1,0:T(8,128)(2,1)S(1)} %get-tuple-element.45.first.refs_0_), channel_id=1, source_target_pairs={{0,1},{1,2},{2,3},{3,0},{4,5},{5,6},{6,7},{7,4},{8,9},{9,10},{10,1... | collective-permute-start | bytes 1277960 | tf_op jit(solution)/shard_map/ppermute | solution.py:381
  3.7 13.1 %collective-permute-start.2 = (bf16[128,1664]{1,0:T(8,128)(2,1)S(1)}, bf16[128,1664]{1,0:T(8,128)(2,1)S(1)}, u32[]{:S(2)}, u32[]{:S(2)}) collective-permute-start(bf16[128,1664]{1,0:T(8,128)(2,1)S(1)} %get-tuple-element.46.second.refs_1_), channel_id=1, source_target_pairs={{0,3},{1,0},{2,1},{3,2},{4,7},{5,4},{6,5},{7,6},{8,11},{9,8},{10,9... | collective-permute-start | bytes 1277960 | tf_op jit(solution)/shard_map/ppermute | solution.py:382
  5.9 5.6 %slice-start = ((s8[14155776]{0:T(1024)(128)(4,1)}), s8[1572864]{0:T(1024)(128)(4,1)S(1)}, s32[]{:S(2)}) async-start(s8[14155776]{0:T(1024)(128)(4,1)} %bitcast.6), calls=%async_computation | async-start | bytes 3145728
  7.7 4.7 %slice-start.3 = ((s8[14155776]{0:T(1024)(128)(4,1)}), s8[4194304]{0:T(1024)(128)(4,1)S(1)}, s32[]{:S(2)}) async-start(s8[14155776]{0:T(1024)(128)(4,1)} %bitcast.6), calls=%async_computation.3 | async-start | bytes 8388608
  7.7 4.7 %copy-start.1 = (f32[2,1536]{1,0:T(2,128)S(1)}, f32[2,1536]{1,0:T(2,128)}, u32[]{:S(2)}) copy-start(f32[2,1536]{1,0:T(2,128)} %refs_4_.5) | copy-start | bytes 36868
  8.8 17.6 %collective-permute-start.4 = (bf16[128,1536]{1,0:T(8,128)(2,1)S(1)}, bf16[128,1536]{1,0:T(8,128)(2,1)S(1)}, u32[]{:S(2)}, u32[]{:S(2)}) collective-permute-start(bf16[128,1536]{1,0:T(8,128)(2,1)S(1)} %get-tuple-element.60), channel_id=1, source_target_pairs={{0,1},{1,2},{2,3},{3,0},{4,5},{5,6},{6,7},{7,4},{8,9},{9,10},{10,1... | collective-permute-start | bytes 1179656 | tf_op jit(solution)/shard_map/ppermute | solution.py:381
  8.8 17.6 %collective-permute-start.5 = (bf16[128,1536]{1,0:T(8,128)(2,1)S(1)}, bf16[128,1536]{1,0:T(8,128)(2,1)S(1)}, u32[]{:S(2)}, u32[]{:S(2)}) collective-permute-start(bf16[128,1536]{1,0:T(8,128)(2,1)S(1)} %get-tuple-element.61), channel_id=1, source_target_pairs={{0,3},{1,0},{2,1},{3,2},{4,7},{5,4},{6,5},{7,6},{8,11},{9,8},{10,9... | collective-permute-start | bytes 1179656 | tf_op jit(solution)/shard_map/ppermute | solution.py:382
  16.8 16.2 %collective-permute-start.1 = (bf16[128,1664]{1,0:T(8,128)(2,1)S(1)}, bf16[128,1664]{1,0:T(8,128)(2,1)S(1)}, u32[]{:S(2)}, u32[]{:S(2)}) collective-permute-start(bf16[128,1664]{1,0:T(8,128)(2,1)S(1)} %collective-permute-done.refs_2_.refs_0_), channel_id=1, source_target_pairs={{0,1},{1,2},{2,3},{3,0},{4,5},{5,6},{6,7},{7,4},{8,9},{9,10},{10,1... | collective-permute-start | bytes 1277960 | tf_op jit(solution)/shard_map/ppermute | solution.py:381
  16.9 16.1 %collective-permute-start.3 = (bf16[128,1664]{1,0:T(8,128)(2,1)S(1)}, bf16[128,1664]{1,0:T(8,128)(2,1)S(1)}, u32[]{:S(2)}, u32[]{:S(2)}) collective-permute-start(bf16[128,1664]{1,0:T(8,128)(2,1)S(1)} %collective-permute-done.2.refs_3_.refs_1_), channel_id=1, source_target_pairs={{0,3},{1,0},{2,1},{3,2},{4,7},{5,4},{6,5},{7,6},{8,11},{9,8},{10,9... | collective-permute-start | bytes 1277960 | tf_op jit(solution)/shard_map/ppermute | solution.py:382
  29.6 6.7 %slice-start.4 = ((s8[4718592]{0:T(1024)(128)(4,1)}), s8[4194304]{0:T(1024)(128)(4,1)S(1)}, s32[]{:S(2)}) async-start(s8[4718592]{0:T(1024)(128)(4,1)} %bitcast.8), calls=%async_computation.4 | async-start | bytes 8388608
  31.5 4.8 %slice-start.5 = ((s8[4718592]{0:T(1024)(128)(4,1)}), s8[524288]{0:T(1024)(128)(4,1)S(1)}, s32[]{:S(2)}) async-start(s8[4718592]{0:T(1024)(128)(4,1)} %bitcast.8), calls=%async_computation.5 | async-start | bytes 1048576
  31.5 4.8 %copy-start = (bf16[1,256,1536]{2,1,0:T(8,128)(2,1)S(1)}, bf16[1,256,1536]{2,1,0:T(8,128)(2,1)}, u32[]{:S(2)}) copy-start(bf16[1,256,1536]{2,1,0:T(8,128)(2,1)} %param.7) | copy-start | bytes 2359300
  38.8 3.7 %collective-permute-start.6 = (bf16[128,1536]{1,0:T(8,128)(2,1)S(1)}, bf16[128,1536]{1,0:T(8,128)(2,1)S(1)}, u32[]{:S(2)}, u32[]{:S(2)}) collective-permute-start(bf16[128,1536]{1,0:T(8,128)(2,1)S(1)} %get-tuple-element.76), channel_id=1, source_target_pairs={{0,4},{4,0},{8,12},{12,8},{16,20},{20,16},{24,28},{28,24},{32,36},... | collective-permute-start | bytes 1179656 | tf_op jit(solution)/shard_map/ppermute | solution.py:364
  43.1 5.7 %collective-permute-start.7 = (bf16[32,1536]{1,0:T(8,128)(2,1)S(1)}, bf16[32,1536]{1,0:T(8,128)(2,1)S(1)}, u32[]{:S(2)}, u32[]{:S(2)}) collective-permute-start(bf16[32,1536]{1,0:T(8,128)(2,1)S(1)} %get-tuple-element.78), channel_id=1, source_target_pairs={{0,8},{4,12},{8,16},{12,20},{16,24},{20,28},{24,0},{28,4},{32,40},... | collective-permute-start | bytes 294920 | tf_op jit(solution)/shard_map/ppermute | solution.py:366
  44.4 7.5 %collective-permute-start.8 = (bf16[32,1536]{1,0:T(8,128)(2,1)S(1)}, bf16[32,1536]{1,0:T(8,128)(2,1)S(1)}, u32[]{:S(2)}, u32[]{:S(2)}) collective-permute-start(bf16[32,1536]{1,0:T(8,128)(2,1)S(1)} %get-tuple-element.79), channel_id=1, source_target_pairs={{0,16},{4,20},{8,24},{12,28},{16,0},{20,4},{24,8},{28,12},{32,48},... | collective-permute-start | bytes 294920 | tf_op jit(solution)/shard_map/ppermute | solution.py:366
  46.8 5.1 %collective-permute-start.9 = (bf16[32,1536]{1,0:T(8,128)(2,1)S(1)}, bf16[32,1536]{1,0:T(8,128)(2,1)S(1)}, u32[]{:S(2)}, u32[]{:S(2)}) collective-permute-start(bf16[32,1536]{1,0:T(8,128)(2,1)S(1)} %get-tuple-element.80), channel_id=1, source_target_pairs={{0,24},{4,28},{8,0},{12,4},{16,8},{20,12},{24,16},{28,20},{32,56},... | collective-permute-start | bytes 294920 | tf_op jit(solution)/shard_map/ppermute | solution.py:366
  51.9 5.1 %collective-permute-start.10 = (bf16[32,1536]{1,0:T(8,128)(2,1)S(1)}, bf16[32,1536]{1,0:T(8,128)(2,1)S(1)}, u32[]{:S(2)}, u32[]{:S(2)}) collective-permute-start(bf16[32,1536]{1,0:T(8,128)(2,1)S(1)} %shard_map.84), channel_id=1, source_target_pairs={{0,32},{4,36},{8,40},{12,44},{16,48},{20,52},{24,56},{28,60},{32,6... | collective-permute-start | bytes 294920 | tf_op jit(solution)/shard_map/ppermute | solution.py:368
  53.3 6.5 %collective-permute-start.11 = (bf16[32,1536]{1,0:T(8,128)(2,1)S(1)}, bf16[32,1536]{1,0:T(8,128)(2,1)S(1)}, u32[]{:S(2)}, u32[]{:S(2)}) collective-permute-start(bf16[32,1536]{1,0:T(8,128)(2,1)S(1)} %shard_map.84), channel_id=1, source_target_pairs={{0,64},{4,68},{8,72},{12,76},{16,80},{20,84},{24,88},{28,92},{32,9... | collective-permute-start | bytes 294920 | tf_op jit(solution)/shard_map/ppermute | solution.py:368
  55.9 3.9 %collective-permute-start.12 = (bf16[32,1536]{1,0:T(8,128)(2,1)S(1)}, bf16[32,1536]{1,0:T(8,128)(2,1)S(1)}, u32[]{:S(2)}, u32[]{:S(2)}) collective-permute-start(bf16[32,1536]{1,0:T(8,128)(2,1)S(1)} %shard_map.84), channel_id=1, source_target_pairs={{0,96},{4,100},{8,104},{12,108},{16,112},{20,116},{24,120},{28,124... | collective-permute-start | bytes 294920 | tf_op jit(solution)/shard_map/ppermute | solution.py:368
  60.7 4.8 %collective-permute-start.13 = (bf16[32,1536]{1,0:T(8,128)(2,1)S(1)}, bf16[32,1536]{1,0:T(8,128)(2,1)S(1)}, u32[]{:S(2)}, u32[]{:S(2)}) collective-permute-start(bf16[32,1536]{1,0:T(8,128)(2,1)S(1)} %get-tuple-element.82), channel_id=1, source_target_pairs={{0,8},{4,12},{8,16},{12,20},{16,24},{20,28},{24,0},{28,4},{32,40},... | collective-permute-start | bytes 294920 | tf_op jit(solution)/shard_map/ppermute | solution.py:370
  62.1 5.2 %collective-permute-start.14 = (bf16[32,1536]{1,0:T(8,128)(2,1)S(1)}, bf16[32,1536]{1,0:T(8,128)(2,1)S(1)}, u32[]{:S(2)}, u32[]{:S(2)}) collective-permute-start(bf16[32,1536]{1,0:T(8,128)(2,1)S(1)} %get-tuple-element.83), channel_id=1, source_target_pairs={{0,16},{4,20},{8,24},{12,28},{16,0},{20,4},{24,8},{28,12},{32,48},... | collective-permute-start | bytes 294920 | tf_op jit(solution)/shard_map/ppermute | solution.py:370
  64.2 3.8 %collective-permute-start.15 = (bf16[32,1536]{1,0:T(8,128)(2,1)S(1)}, bf16[32,1536]{1,0:T(8,128)(2,1)S(1)}, u32[]{:S(2)}, u32[]{:S(2)}) collective-permute-start(bf16[32,1536]{1,0:T(8,128)(2,1)S(1)} %get-tuple-element.84), channel_id=1, source_target_pairs={{0,24},{4,28},{8,0},{12,4},{16,8},{20,12},{24,16},{28,20},{32,56},... | collective-permute-start | bytes 294920 | tf_op jit(solution)/shard_map/ppermute | solution.py:370
  68.6 4.8 %collective-permute-start.16 = (bf16[128,1536]{1,0:T(8,128)(2,1)S(1)}, bf16[128,1536]{1,0:T(8,128)(2,1)S(1)}, u32[]{:S(2)}, u32[]{:S(2)}) collective-permute-start(bf16[128,1536]{1,0:T(8,128)(2,1)S(1)} %shard_map.86), channel_id=1, source_target_pairs={{0,4},{4,0},{8,12},{12,8},{16,20},{20,16},{24,28},{28,24},{32,36},... | collective-permute-start | bytes 1179656 | tf_op jit(solution)/shard_map/ppermute | solution.py:372
  (3 other events, 9.4 us)

commit v6 on v5

--- a/solution.py
+++ b/solution.py
@@ -265,13 +265,20 @@
     )(step_times, place, q, *kv, *state, x, gate, w_out)
 
 
+def for_each_column(place, body):
+    for xx in range(4):
+        pl.when(place[1] == xx)(functools.partial(body, xx))
+
+
 def split_kernel(place, mine, got, own, *pieces):
-    xx = place[1]
     part = own.shape[0]
-    for k, out in enumerate((own,) + pieces):
-        at = pl.multiple_of(((xx + k) & 3) * part, part)
-        both = mine[pl.ds(at, part), :] + got[pl.ds(at, part), :].astype(f32)
-        out[...] = both.astype(out.dtype)
+
+    def split(xx):
+        for k, out in enumerate((own,) + pieces):
+            at = pl.ds((xx + k) % 4 * part, part)
+            out[...] = (mine[at, :] + got[at, :].astype(f32)).astype(out.dtype)
+
+    for_each_column(place, split)
 
 
 def row_kernel(own, one, two, three, out):
@@ -280,25 +287,35 @@
 
 def before_kernel(place, own, *refs):
     xs, ys, outs = refs[:3], refs[3:6], refs[6:]
-    xx, yy = place[1], place[2]
-    above = jnp.zeros(own.shape, f32)
+    yy = place[2]
+    outs[0][...] = jnp.zeros(own.shape, f32)
     for k in (1, 2, 3):
-        above = above + jnp.where(((yy - k) & 3) < yy, ys[k - 1][...].astype(f32), 0.0)
-    src = [own[...]] + [r[...].astype(f32) for r in xs]
-    for k, out in enumerate(outs):
-        total = above
-        for j in range(4):
-            total = total + jnp.where(((xx - j) & 3) < ((xx + k) & 3), src[j], 0.0)
-        out[...] = total.astype(out.dtype)
+
+        @pl.when(((yy - k) & 3) < yy)
+        def _(k=k):
+            outs[0][...] += ys[k - 1][...].astype(f32)
+
+    def prefix(xx):
+        total = outs[0][...]
+        for chip in range(4):
+            outs[(chip - xx) % 4][...] = total.astype(outs[(chip - xx) % 4].dtype)
+            if chip < 3:
+                j = (xx - chip) % 4
+                total = total + (own if j == 0 else xs[j - 1])[...].astype(f32)
+
+    for_each_column(place, prefix)
 
 
 def given_kernel(place, mine, *refs):
     pieces, given = refs[:4], refs[4]
-    c, xx = place[0], place[1]
     part = pieces[0].shape[0]
-    for k in range(4):
-        at = pl.ds(pl.multiple_of(((xx - k) & 3) * part, part), part)
-        given[at, :] = (pieces[k][...].astype(f32) + jnp.where(c == 0, mine[at, :], 0.0)).astype(bf16)
+
+    def join(xx):
+        for k in range(4):
+            at = pl.ds((xx - k) % 4 * part, part)
+            given[at, :] = (pieces[k][...].astype(f32) + jnp.where(place[0] == 0, mine[at, :], 0.0)).astype(bf16)
+
+    for_each_column(place, join)
 
 
 def own_half_kernel(place, mine, got, *refs):

time: 75.3 us -> 75.2 us (level)
  no operation moved by 1% of the time
where the time goes in v6:
time: 75.2 us; the launch traced here: 75 us
  Pallas kernels  31.7 us (42%)
  starting transfers between devices  29.5 us (39%)
  waiting for transfers between devices  10.7 us (14%)
  local copies, waits for them, and re-layouts  2.7 us (4%)
    pallas_call x4, Pallas kernels, project(): pl.pallas_call(functools.partial(project_kernel, with_q, len(ids)), in_sp...  14 us
    ppermute x6, starting transfers between devices, scan_steps(): lax.ppermute(piece, 'step', along_x(k))  9.69 us
    ppermute x3, starting transfers between devices, on_device(): to_left = lambda v: lax.ppermute(v, 'seq', left)  7.52 us
    ppermute x6, waiting for transfers between devices, scan_steps(): lax.ppermute(piece, 'step', along_x(k))  6.38 us
    pallas_call x2, Pallas kernels, attend(): pl.pallas_call(functools.partial(attend_kernel, len(kvs)), in_specs=[vm]...  5.63 us
    ppermute x3, starting transfers between devices, scan_steps(): ys = [lax.ppermute(row, 'step', along_y(k)) for k in (1, 2, 3)]  5.06 us
    pallas_call x2, Pallas kernels, finish(): pl.pallas_call(functools.partial(finish_kernel, theirs), in_specs=[pl.Blo...  4.8 us
    ppermute x1, starting transfers between devices, scan_steps(): other = lax.ppermute(given, 'step', pair)  3.25 us
  transfers between devices with their start and end apart: 17, of which 7 were waited for; matrix products, arithmetic and copies ran while one was open for 0% of the time, Pallas kernels for 28%

profile of v6, /device:TPU:1, one launch (start us, length us, event | category | flops | bytes accessed | tf_op | source)
XLA Modules:
  0.0 75.0 jit_solution(8057115070470146620)
XLA Ops:
  1.2 2.5 %collective-permute-start = (bf16[128,1664]{1,0:T(8,128)(2,1)S(1)}, bf16[128,1664]{1,0:T(8,128)(2,1)S(1)}, u32[]{:S(2)}, u32[]{:S(2)}) collective-permute-start(bf16[128,1664]{1,0:T(8,128)(2,1)S(1)} %get-tuple-element.45.first.refs_0_), channel_id=1, source_target_pairs={{0,1},{1,2},{2,3},{3,0},{4,5},{5,6},{6,7},{7,4},{8,9},{9,10},{10,1... | collective-permute-start | bytes 1277960 | tf_op jit(solution)/shard_map/ppermute | solution.py:398
  3.7 2.2 %collective-permute-start.2 = (bf16[128,1664]{1,0:T(8,128)(2,1)S(1)}, bf16[128,1664]{1,0:T(8,128)(2,1)S(1)}, u32[]{:S(2)}, u32[]{:S(2)}) collective-permute-start(bf16[128,1664]{1,0:T(8,128)(2,1)S(1)} %get-tuple-element.46.second.refs_1_), channel_id=1, source_target_pairs={{0,3},{1,0},{2,1},{3,2},{4,7},{5,4},{6,5},{7,6},{8,11},{9,8},{10,9... | collective-permute-start | bytes 1277960 | tf_op jit(solution)/shard_map/ppermute | solution.py:399
  5.9 1.8 %copy-done.3 = bf16[256,4608]{1,0:T(8,128)(2,1)S(1)} copy-done((bf16[256,4608]{1,0:T(8,128)(2,1)S(1)}, bf16[256,4608]{1,0:T(8,128)(2,1)}, u32[]{:S(2)}) %copy-start.3) | copy-done | bytes 2359320
  8.8 2.7 %collective-permute-start.5 = (bf16[128,1536]{1,0:T(8,128)(2,1)S(1)}, bf16[128,1536]{1,0:T(8,128)(2,1)S(1)}, u32[]{:S(2)}, u32[]{:S(2)}) collective-permute-start(bf16[128,1536]{1,0:T(8,128)(2,1)S(1)} %get-tuple-element.61), channel_id=1, source_target_pairs={{0,3},{1,0},{2,1},{3,2},{4,7},{5,4},{6,5},{7,6},{8,11},{9,8},{10,9... | collective-permute-start | bytes 1179656 | tf_op jit(solution)/shard_map/ppermute | solution.py:399
  12.4 4.4 %shard_map.75 = (bf16[256,1536]{1,0:T(8,128)(2,1)S(1)}, bf16[256,1536]{1,0:T(8,128)(2,1)S(1)}, bf16[256,1536]{1,0:T(8,128)(2,1)S(1)}) custom-call(bf16[128,1664]{1,0:T(8,128)(2,1)S(1)} %get-tuple-element.45.first.refs_0_, bf16[128,1664]{1,0:T(8,128)(2,1)S(1)} %get-tuple-element.46.second.refs_1_, f32[1,1536]{1,0:T(1,128)S(1)} %get-tuple-element.54.refs_2_.refs_4_, ...), custom_call_target="tpu_custom_call" | custom-call | flops 3623878656 | bytes 14155776 | tf_op jit(solution)/shard_map/pallas_call | solution.py:152
  16.9 2.7 %collective-permute-start.3 = (bf16[128,1664]{1,0:T(8,128)(2,1)S(1)}, bf16[128,1664]{1,0:T(8,128)(2,1)S(1)}, u32[]{:S(2)}, u32[]{:S(2)}) collective-permute-start(bf16[128,1664]{1,0:T(8,128)(2,1)S(1)} %collective-permute-done.2.refs_3_.refs_1_), channel_id=1, source_target_pairs={{0,3},{1,0},{2,1},{3,2},{4,7},{5,4},{6,5},{7,6},{8,11},{9,8},{10,9... | collective-permute-start | bytes 1277960 | tf_op jit(solution)/shard_map/ppermute | solution.py:399
  19.5 3.1 %shard_map.78 = (bf16[256,1536]{1,0:T(8,128)(2,1)S(1)}, bf16[256,1536]{1,0:T(8,128)(2,1)S(1)}) custom-call(bf16[128,1664]{1,0:T(8,128)(2,1)S(1)} %collective-permute-done.refs_2_.refs_0_, bf16[128,1664]{1,0:T(8,128)(2,1)S(1)} %collective-permute-done.2.refs_3_.refs_1_, f32[1,1536]{1,0:T(1,128)S(1)} %get-tuple-element.54.refs_2_.refs_4_, ...), custom_call_target="tpu_custom_call" | custom-call | flops 2415919104 | bytes 9437184 | tf_op jit(solution)/shard_map/pallas_call | solution.py:152
  22.7 3.8 %shard_map.79 = (f32[12,256,128]{2,1,0:T(8,128)S(1)}, f32[12,256,128]{2,1,0:T(8,128)S(1)}, f32[256,1536]{1,0:T(8,128)S(1)}) custom-call(bf16[256,1536]{1,0:T(8,128)(2,1)S(1)} %get-tuple-element.57.q_ref, bf16[256,1536]{1,0:T(8,128)(2,1)S(1)} %get-tuple-element.64.refs_0_, bf16[256,1536]{1,0:T(8,128)(2,1)S(1)} %get-tuple-element.65.refs_1_, ...), custom_call_target="tpu_custom_call" | custom-call | flops 1610612736 | bytes 3145728 | tf_op jit(solution)/shard_map/pallas_call | solution.py:205
  26.5 3.2 %shard_map.77 = (bf16[256,1536]{1,0:T(8,128)(2,1)S(1)}, bf16[256,1536]{1,0:T(8,128)(2,1)S(1)}) custom-call(bf16[128,1536]{1,0:T(8,128)(2,1)S(1)} %collective-permute-done.4.refs_0_, bf16[128,1536]{1,0:T(8,128)(2,1)S(1)} %collective-permute-done.5.refs_1_, bf16[128,1664]{1,0:T(8,128)(2,1)S(1)} %collective-permute-done.refs_2_.refs_0_, ...), custom_call_target="tpu_custom_call" | custom-call | flops 2415919104 | bytes 9437184 | tf_op jit(solution)/shard_map/pallas_call | solution.py:152
  29.6 1.9 %shard_map.80 = (f32[12,256,128]{2,1,0:T(8,128)S(1)}, f32[12,256,128]{2,1,0:T(8,128)S(1)}, f32[256,1536]{1,0:T(8,128)S(1)}) custom-call(bf16[256,1536]{1,0:T(8,128)(2,1)S(1)} %get-tuple-element.57.q_ref, bf16[256,1536]{1,0:T(8,128)(2,1)S(1)} %get-tuple-element.62.refs_0_, bf16[256,1536]{1,0:T(8,128)(2,1)S(1)} %get-tuple-element.63.refs_1_, ...), custom_call_target="tpu_custom_call" | custom-call | flops 805306368 | bytes 3145728 | tf_op jit(solution)/shard_map/pallas_call | solution.py:205
  31.5 1.4 %collective-permute-done.1.refs_0_ = bf16[128,1664]{1,0:T(8,128)(2,1)S(1)} collective-permute-done((bf16[128,1664]{1,0:T(8,128)(2,1)S(1)}, bf16[128,1664]{1,0:T(8,128)(2,1)S(1)}, u32[]{:S(2)}, u32[]{:S(2)}) %collective-permute-start.1) | collective-permute-done | bytes 426016 | tf_op jit(solution)/shard_map/ppermute | solution.py:398
  32.9 3.4 %shard_map.76 = (bf16[256,1536]{1,0:T(8,128)(2,1)S(1)}, bf16[256,1536]{1,0:T(8,128)(2,1)S(1)}) custom-call(bf16[128,1664]{1,0:T(8,128)(2,1)S(1)} %collective-permute-done.1.refs_0_, bf16[128,1664]{1,0:T(8,128)(2,1)S(1)} %collective-permute-done.3.refs_1_, f32[1,1536]{1,0:T(1,128)S(1)} %get-tuple-element.54.refs_2_.refs_4_, ...), custom_call_target="tpu_custom_call" | custom-call | flops 2415919104 | bytes 9437184 | tf_op jit(solution)/shard_map/pallas_call | solution.py:152
  36.4 2.4 %shard_map.81 = (f32[128,1536]{1,0:T(8,128)S(1)}, bf16[128,1536]{1,0:T(8,128)(2,1)S(1)}) custom-call(s32[1,2]{1,0:T(1,128)S(1)} %copy-done.2, s32[3]{0:T(128)S(1)} %pad_add_fusion.place, bf16[256,1536]{1,0:T(8,128)(2,1)S(1)} %get-tuple-element.57.q_ref, bf16[256,1536]{1,0:T(8,128)(2,1)S(1)} %get-tuple-element.58.k_ref, ...), custom_call_target="tpu_custom_call" | custom-call | flops 1006632960 | bytes 4718592 | tf_op jit(solution)/shard_map/pallas_call | solution.py:253
  40.1 2.4 %shard_map.82.mine = f32[128,1536]{1,0:T(8,128)S(1)} custom-call(s32[1,2]{1,0:T(1,128)S(1)} %copy-done.2, s32[3]{0:T(128)S(1)} %pad_add_fusion.place, bf16[256,1536]{1,0:T(8,128)(2,1)S(1)} %get-tuple-element.57.q_ref, bf16[256,1536]{1,0:T(8,128)(2,1)S(1)} %get-tuple-element.58.k_ref, bf16[256,1536]{1,0:T(8,128)(2,1)S(1)} %get-tuple-element.59.v_ref, ...), custom_call_target="tpu_custom_call" | custom-call | flops 1006632960 | bytes 4718592 | tf_op jit(solution)/shard_map/pallas_call | solution.py:253
  44.4 2.4 %collective-permute-start.8 = (bf16[32,1536]{1,0:T(8,128)(2,1)S(1)}, bf16[32,1536]{1,0:T(8,128)(2,1)S(1)}, u32[]{:S(2)}, u32[]{:S(2)}) collective-permute-start(bf16[32,1536]{1,0:T(8,128)(2,1)S(1)} %get-tuple-element.79), channel_id=1, source_target_pairs={{0,16},{4,20},{8,24},{12,28},{16,0},{20,4},{24,8},{28,12},{32,48},... | collective-permute-start | bytes 294920 | tf_op jit(solution)/shard_map/ppermute | solution.py:383
  48.8 3.1 %collective-permute-done.8.two.refs_1_ = bf16[32,1536]{1,0:T(8,128)(2,1)S(1)} collective-permute-done((bf16[32,1536]{1,0:T(8,128)(2,1)S(1)}, bf16[32,1536]{1,0:T(8,128)(2,1)S(1)}, u32[]{:S(2)}, u32[]{:S(2)}) %collective-permute-start.8) | collective-permute-done | bytes 98336 | tf_op jit(solution)/shard_map/ppermute | solution.py:383
  53.3 2.6 %collective-permute-start.11 = (bf16[32,1536]{1,0:T(8,128)(2,1)S(1)}, bf16[32,1536]{1,0:T(8,128)(2,1)S(1)}, u32[]{:S(2)}, u32[]{:S(2)}) collective-permute-start(bf16[32,1536]{1,0:T(8,128)(2,1)S(1)} %shard_map.84), channel_id=1, source_target_pairs={{0,64},{4,68},{8,72},{12,76},{16,80},{20,84},{24,88},{28,92},{32,9... | collective-permute-start | bytes 294920 | tf_op jit(solution)/shard_map/ppermute | solution.py:385
  57.0 2.8 %collective-permute-done.11.refs_4_ = bf16[32,1536]{1,0:T(8,128)(2,1)S(1)} collective-permute-done((bf16[32,1536]{1,0:T(8,128)(2,1)S(1)}, bf16[32,1536]{1,0:T(8,128)(2,1)S(1)}, u32[]{:S(2)}, u32[]{:S(2)}) %collective-permute-start.11) | collective-permute-done | bytes 98336 | tf_op jit(solution)/shard_map/ppermute | solution.py:385
  60.5 1.4 %collective-permute-start.13 = (bf16[32,1536]{1,0:T(8,128)(2,1)S(1)}, bf16[32,1536]{1,0:T(8,128)(2,1)S(1)}, u32[]{:S(2)}, u32[]{:S(2)}) collective-permute-start(bf16[32,1536]{1,0:T(8,128)(2,1)S(1)} %get-tuple-element.82), channel_id=1, source_target_pairs={{0,8},{4,12},{8,16},{12,20},{16,24},{20,28},{24,0},{28,4},{32,40},... | collective-permute-start | bytes 294920 | tf_op jit(solution)/shard_map/ppermute | solution.py:387
  62.0 2.1 %collective-permute-start.14 = (bf16[32,1536]{1,0:T(8,128)(2,1)S(1)}, bf16[32,1536]{1,0:T(8,128)(2,1)S(1)}, u32[]{:S(2)}, u32[]{:S(2)}) collective-permute-start(bf16[32,1536]{1,0:T(8,128)(2,1)S(1)} %get-tuple-element.83), channel_id=1, source_target_pairs={{0,16},{4,20},{8,24},{12,28},{16,0},{20,4},{24,8},{28,12},{32,48},... | collective-permute-start | bytes 294920 | tf_op jit(solution)/shard_map/ppermute | solution.py:387
  65.4 1.8 %collective-permute-done.14.refs_2_ = bf16[32,1536]{1,0:T(8,128)(2,1)S(1)} collective-permute-done((bf16[32,1536]{1,0:T(8,128)(2,1)S(1)}, bf16[32,1536]{1,0:T(8,128)(2,1)S(1)}, u32[]{:S(2)}, u32[]{:S(2)}) %collective-permute-start.14) | collective-permute-done | bytes 98336 | tf_op jit(solution)/shard_map/ppermute | solution.py:387
  68.5 3.2 %collective-permute-start.16 = (bf16[128,1536]{1,0:T(8,128)(2,1)S(1)}, bf16[128,1536]{1,0:T(8,128)(2,1)S(1)}, u32[]{:S(2)}, u32[]{:S(2)}) collective-permute-start(bf16[128,1536]{1,0:T(8,128)(2,1)S(1)} %shard_map.86), channel_id=1, source_target_pairs={{0,4},{4,0},{8,12},{12,8},{16,20},{20,16},{24,28},{28,24},{32,36},... | collective-permute-start | bytes 1179656 | tf_op jit(solution)/shard_map/ppermute | solution.py:389
  71.8 1.6 %shard_map.87.begun = f32[256,1536]{1,0:T(8,128)} custom-call(s32[3]{0:T(128)S(1)} %pad_add_fusion.place, f32[128,1536]{1,0:T(8,128)S(1)} %shard_map.82.mine, bf16[128,1536]{1,0:T(8,128)(2,1)S(1)} %collective-permute-done.6.got, f32[32,1536]{1,0:T(8,128)S(1)} %get-tuple-element.81.refs_0_, bf16[32,1536]{1,0:T(8,128)(2,1)S(1)} %collective-permute-done.13.refs_1_, ...), custom_call_target="tpu_custom_call" | custom-call | bytes 2359296 | tf_op jit(solution)/shard_map/pallas_call | solution.py:344
  73.3 1.5 %shard_map.88 = f32[256,1536]{1,0:T(8,128)} custom-call(s32[3]{0:T(128)S(1)} %pad_add_fusion.place, f32[128,1536]{1,0:T(8,128)S(1)} %get-tuple-element.75.theirs, bf16[128,1536]{1,0:T(8,128)(2,1)S(1)} %collective-permute-done.16.other, f32[256,1536]{1,0:T(8,128)} %shard_map.87.begun), custom_call_target="tpu_custom_call", output_to_operand_aliasing={{}: (3, {})} | custom-call | bytes 2359296 | tf_op jit(solution)/shard_map/pallas_call | solution.py:344
  (49 shorter events, 14.3 us)
Async XLA Ops:
  0.0 5.9 %copy-start.2 = (s32[1,2]{1,0:T(1,128)S(1)}, s32[1,2]{1,0:T(1,128)}, u32[]{:S(2)}) copy-start(s32[1,2]{1,0:T(1,128)} %times.5) | copy-start | bytes 28
  1.2 15.6 %collective-permute-start = (bf16[128,1664]{1,0:T(8,128)(2,1)S(1)}, bf16[128,1664]{1,0:T(8,128)(2,1)S(1)}, u32[]{:S(2)}, u32[]{:S(2)}) collective-permute-start(bf16[128,1664]{1,0:T(8,128)(2,1)S(1)} %get-tuple-element.45.first.refs_0_), channel_id=1, source_target_pairs={{0,1},{1,2},{2,3},{3,0},{4,5},{5,6},{6,7},{7,4},{8,9},{9,10},{10,1... | collective-permute-start | bytes 1277960 | tf_op jit(solution)/shard_map/ppermute | solution.py:398
  3.7 13.1 %collective-permute-start.2 = (bf16[128,1664]{1,0:T(8,128)(2,1)S(1)}, bf16[128,1664]{1,0:T(8,128)(2,1)S(1)}, u32[]{:S(2)}, u32[]{:S(2)}) collective-permute-start(bf16[128,1664]{1,0:T(8,128)(2,1)S(1)} %get-tuple-element.46.second.refs_1_), channel_id=1, source_target_pairs={{0,3},{1,0},{2,1},{3,2},{4,7},{5,4},{6,5},{7,6},{8,11},{9,8},{10,9... | collective-permute-start | bytes 1277960 | tf_op jit(solution)/shard_map/ppermute | solution.py:399
  5.9 5.6 %slice-start = ((s8[14155776]{0:T(1024)(128)(4,1)}), s8[1572864]{0:T(1024)(128)(4,1)S(1)}, s32[]{:S(2)}) async-start(s8[14155776]{0:T(1024)(128)(4,1)} %bitcast.6), calls=%async_computation | async-start | bytes 3145728
  7.7 4.7 %slice-start.3 = ((s8[14155776]{0:T(1024)(128)(4,1)}), s8[4194304]{0:T(1024)(128)(4,1)S(1)}, s32[]{:S(2)}) async-start(s8[14155776]{0:T(1024)(128)(4,1)} %bitcast.6), calls=%async_computation.3 | async-start | bytes 8388608
  7.7 4.7 %copy-start.1 = (f32[2,1536]{1,0:T(2,128)S(1)}, f32[2,1536]{1,0:T(2,128)}, u32[]{:S(2)}) copy-start(f32[2,1536]{1,0:T(2,128)} %refs_4_.5) | copy-start | bytes 36868
  8.8 17.6 %collective-permute-start.4 = (bf16[128,1536]{1,0:T(8,128)(2,1)S(1)}, bf16[128,1536]{1,0:T(8,128)(2,1)S(1)}, u32[]{:S(2)}, u32[]{:S(2)}) collective-permute-start(bf16[128,1536]{1,0:T(8,128)(2,1)S(1)} %get-tuple-element.60), channel_id=1, source_target_pairs={{0,1},{1,2},{2,3},{3,0},{4,5},{5,6},{6,7},{7,4},{8,9},{9,10},{10,1... | collective-permute-start | bytes 1179656 | tf_op jit(solution)/shard_map/ppermute | solution.py:398
  8.8 17.6 %collective-permute-start.5 = (bf16[128,1536]{1,0:T(8,128)(2,1)S(1)}, bf16[128,1536]{1,0:T(8,128)(2,1)S(1)}, u32[]{:S(2)}, u32[]{:S(2)}) collective-permute-start(bf16[128,1536]{1,0:T(8,128)(2,1)S(1)} %get-tuple-element.61), channel_id=1, source_target_pairs={{0,3},{1,0},{2,1},{3,2},{4,7},{5,4},{6,5},{7,6},{8,11},{9,8},{10,9... | collective-permute-start | bytes 1179656 | tf_op jit(solution)/shard_map/ppermute | solution.py:399
  16.8 16.2 %collective-permute-start.1 = (bf16[128,1664]{1,0:T(8,128)(2,1)S(1)}, bf16[128,1664]{1,0:T(8,128)(2,1)S(1)}, u32[]{:S(2)}, u32[]{:S(2)}) collective-permute-start(bf16[128,1664]{1,0:T(8,128)(2,1)S(1)} %collective-permute-done.refs_2_.refs_0_), channel_id=1, source_target_pairs={{0,1},{1,2},{2,3},{3,0},{4,5},{5,6},{6,7},{7,4},{8,9},{9,10},{10,1... | collective-permute-start | bytes 1277960 | tf_op jit(solution)/shard_map/ppermute | solution.py:398
  16.9 16.1 %collective-permute-start.3 = (bf16[128,1664]{1,0:T(8,128)(2,1)S(1)}, bf16[128,1664]{1,0:T(8,128)(2,1)S(1)}, u32[]{:S(2)}, u32[]{:S(2)}) collective-permute-start(bf16[128,1664]{1,0:T(8,128)(2,1)S(1)} %collective-permute-done.2.refs_3_.refs_1_), channel_id=1, source_target_pairs={{0,3},{1,0},{2,1},{3,2},{4,7},{5,4},{6,5},{7,6},{8,11},{9,8},{10,9... | collective-permute-start | bytes 1277960 | tf_op jit(solution)/shard_map/ppermute | solution.py:399
  29.6 6.7 %slice-start.4 = ((s8[4718592]{0:T(1024)(128)(4,1)}), s8[4194304]{0:T(1024)(128)(4,1)S(1)}, s32[]{:S(2)}) async-start(s8[4718592]{0:T(1024)(128)(4,1)} %bitcast.8), calls=%async_computation.4 | async-start | bytes 8388608
  31.5 4.8 %slice-start.5 = ((s8[4718592]{0:T(1024)(128)(4,1)}), s8[524288]{0:T(1024)(128)(4,1)S(1)}, s32[]{:S(2)}) async-start(s8[4718592]{0:T(1024)(128)(4,1)} %bitcast.8), calls=%async_computation.5 | async-start | bytes 1048576
  31.5 4.8 %copy-start = (bf16[1,256,1536]{2,1,0:T(8,128)(2,1)S(1)}, bf16[1,256,1536]{2,1,0:T(8,128)(2,1)}, u32[]{:S(2)}) copy-start(bf16[1,256,1536]{2,1,0:T(8,128)(2,1)} %param.7) | copy-start | bytes 2359300
  38.8 3.7 %collective-permute-start.6 = (bf16[128,1536]{1,0:T(8,128)(2,1)S(1)}, bf16[128,1536]{1,0:T(8,128)(2,1)S(1)}, u32[]{:S(2)}, u32[]{:S(2)}) collective-permute-start(bf16[128,1536]{1,0:T(8,128)(2,1)S(1)} %get-tuple-element.76), channel_id=1, source_target_pairs={{0,4},{4,0},{8,12},{12,8},{16,20},{20,16},{24,28},{28,24},{32,36},... | collective-permute-start | bytes 1179656 | tf_op jit(solution)/shard_map/ppermute | solution.py:381
  43.1 5.7 %collective-permute-start.7 = (bf16[32,1536]{1,0:T(8,128)(2,1)S(1)}, bf16[32,1536]{1,0:T(8,128)(2,1)S(1)}, u32[]{:S(2)}, u32[]{:S(2)}) collective-permute-start(bf16[32,1536]{1,0:T(8,128)(2,1)S(1)} %get-tuple-element.78), channel_id=1, source_target_pairs={{0,8},{4,12},{8,16},{12,20},{16,24},{20,28},{24,0},{28,4},{32,40},... | collective-permute-start | bytes 294920 | tf_op jit(solution)/shard_map/ppermute | solution.py:383
  44.4 7.5 %collective-permute-start.8 = (bf16[32,1536]{1,0:T(8,128)(2,1)S(1)}, bf16[32,1536]{1,0:T(8,128)(2,1)S(1)}, u32[]{:S(2)}, u32[]{:S(2)}) collective-permute-start(bf16[32,1536]{1,0:T(8,128)(2,1)S(1)} %get-tuple-element.79), channel_id=1, source_target_pairs={{0,16},{4,20},{8,24},{12,28},{16,0},{20,4},{24,8},{28,12},{32,48},... | collective-permute-start | bytes 294920 | tf_op jit(solution)/shard_map/ppermute | solution.py:383
  46.9 5.1 %collective-permute-start.9 = (bf16[32,1536]{1,0:T(8,128)(2,1)S(1)}, bf16[32,1536]{1,0:T(8,128)(2,1)S(1)}, u32[]{:S(2)}, u32[]{:S(2)}) collective-permute-start(bf16[32,1536]{1,0:T(8,128)(2,1)S(1)} %get-tuple-element.80), channel_id=1, source_target_pairs={{0,24},{4,28},{8,0},{12,4},{16,8},{20,12},{24,16},{28,20},{32,56},... | collective-permute-start | bytes 294920 | tf_op jit(solution)/shard_map/ppermute | solution.py:383
  52.0 5.1 %collective-permute-start.10 = (bf16[32,1536]{1,0:T(8,128)(2,1)S(1)}, bf16[32,1536]{1,0:T(8,128)(2,1)S(1)}, u32[]{:S(2)}, u32[]{:S(2)}) collective-permute-start(bf16[32,1536]{1,0:T(8,128)(2,1)S(1)} %shard_map.84), channel_id=1, source_target_pairs={{0,32},{4,36},{8,40},{12,44},{16,48},{20,52},{24,56},{28,60},{32,6... | collective-permute-start | bytes 294920 | tf_op jit(solution)/shard_map/ppermute | solution.py:385
  53.3 6.5 %collective-permute-start.11 = (bf16[32,1536]{1,0:T(8,128)(2,1)S(1)}, bf16[32,1536]{1,0:T(8,128)(2,1)S(1)}, u32[]{:S(2)}, u32[]{:S(2)}) collective-permute-start(bf16[32,1536]{1,0:T(8,128)(2,1)S(1)} %shard_map.84), channel_id=1, source_target_pairs={{0,64},{4,68},{8,72},{12,76},{16,80},{20,84},{24,88},{28,92},{32,9... | collective-permute-start | bytes 294920 | tf_op jit(solution)/shard_map/ppermute | solution.py:385
  56.0 3.9 %collective-permute-start.12 = (bf16[32,1536]{1,0:T(8,128)(2,1)S(1)}, bf16[32,1536]{1,0:T(8,128)(2,1)S(1)}, u32[]{:S(2)}, u32[]{:S(2)}) collective-permute-start(bf16[32,1536]{1,0:T(8,128)(2,1)S(1)} %shard_map.84), channel_id=1, source_target_pairs={{0,96},{4,100},{8,104},{12,108},{16,112},{20,116},{24,120},{28,124... | collective-permute-start | bytes 294920 | tf_op jit(solution)/shard_map/ppermute | solution.py:385
  60.5 4.8 %collective-permute-start.13 = (bf16[32,1536]{1,0:T(8,128)(2,1)S(1)}, bf16[32,1536]{1,0:T(8,128)(2,1)S(1)}, u32[]{:S(2)}, u32[]{:S(2)}) collective-permute-start(bf16[32,1536]{1,0:T(8,128)(2,1)S(1)} %get-tuple-element.82), channel_id=1, source_target_pairs={{0,8},{4,12},{8,16},{12,20},{16,24},{20,28},{24,0},{28,4},{32,40},... | collective-permute-start | bytes 294920 | tf_op jit(solution)/shard_map/ppermute | solution.py:387
  62.0 5.2 %collective-permute-start.14 = (bf16[32,1536]{1,0:T(8,128)(2,1)S(1)}, bf16[32,1536]{1,0:T(8,128)(2,1)S(1)}, u32[]{:S(2)}, u32[]{:S(2)}) collective-permute-start(bf16[32,1536]{1,0:T(8,128)(2,1)S(1)} %get-tuple-element.83), channel_id=1, source_target_pairs={{0,16},{4,20},{8,24},{12,28},{16,0},{20,4},{24,8},{28,12},{32,48},... | collective-permute-start | bytes 294920 | tf_op jit(solution)/shard_map/ppermute | solution.py:387
  64.1 3.8 %collective-permute-start.15 = (bf16[32,1536]{1,0:T(8,128)(2,1)S(1)}, bf16[32,1536]{1,0:T(8,128)(2,1)S(1)}, u32[]{:S(2)}, u32[]{:S(2)}) collective-permute-start(bf16[32,1536]{1,0:T(8,128)(2,1)S(1)} %get-tuple-element.84), channel_id=1, source_target_pairs={{0,24},{4,28},{8,0},{12,4},{16,8},{20,12},{24,16},{28,20},{32,56},... | collective-permute-start | bytes 294920 | tf_op jit(solution)/shard_map/ppermute | solution.py:387
  68.5 4.8 %collective-permute-start.16 = (bf16[128,1536]{1,0:T(8,128)(2,1)S(1)}, bf16[128,1536]{1,0:T(8,128)(2,1)S(1)}, u32[]{:S(2)}, u32[]{:S(2)}) collective-permute-start(bf16[128,1536]{1,0:T(8,128)(2,1)S(1)} %shard_map.86), channel_id=1, source_target_pairs={{0,4},{4,0},{8,12},{12,8},{16,20},{20,16},{24,28},{28,24},{32,36},... | collective-permute-start | bytes 1179656 | tf_op jit(solution)/shard_map/ppermute | solution.py:389
  (3 other events, 9.4 us)

commit v7 on v6

--- a/solution.py
+++ b/solution.py
@@ -265,12 +265,18 @@
     )(step_times, place, q, *kv, *state, x, gate, w_out)
 
 
+def here():
+    step = lax.axis_index("step")
+    return step & 1, (step >> 1) & 3, step >> 3
+
+
 def for_each_column(place, body):
     for xx in range(4):
         pl.when(place[1] == xx)(functools.partial(body, xx))
 
 
-def split_kernel(place, mine, got, own, *pieces):
+def split_kernel(mine, got, own, *pieces):
+    place = here()
     part = own.shape[0]
 
     def split(xx):
@@ -285,7 +291,8 @@
     out[...] = (own[...] + one[...].astype(f32) + two[...].astype(f32) + three[...].astype(f32)).astype(bf16)
 
 
-def before_kernel(place, own, *refs):
+def before_kernel(own, *refs):
+    place = here()
     xs, ys, outs = refs[:3], refs[3:6], refs[6:]
     yy = place[2]
     outs[0][...] = jnp.zeros(own.shape, f32)
@@ -306,7 +313,8 @@
     for_each_column(place, prefix)
 
 
-def given_kernel(place, mine, *refs):
+def given_kernel(mine, *refs):
+    place = here()
     pieces, given = refs[:4], refs[4]
     part = pieces[0].shape[0]
 
@@ -318,7 +326,8 @@
     for_each_column(place, join)
 
 
-def own_half_kernel(place, mine, got, *refs):
+def own_half_kernel(mine, got, *refs):
+    place = here()
     pieces, (out, held, sem) = refs[:4], refs[4:]
     c, xx = place[0], place[1]
     part, half = pieces[0].shape[0], held.shape[0]
@@ -330,7 +339,8 @@
     store.wait()
 
 
-def other_half_kernel(place, theirs, other, begun, out, held, sem):
+def other_half_kernel(theirs, other, begun, out, held, sem):
+    place = here()
     half = held.shape[0]
     held[...] = other[...].astype(f32) + theirs[...]
     at = pl.multiple_of((1 - place[0]) * half, half)
@@ -339,33 +349,32 @@
     store.wait()
 
 
-def store_call(kernel, place, args, begun, rows):
+def store_call(kernel, args, begun, rows):
     vm, anywhere = pl.BlockSpec(memory_space=pltpu.VMEM), pl.BlockSpec(memory_space=pl.ANY)
     return pl.pallas_call(
         kernel,
-        in_specs=[pl.BlockSpec(memory_space=pltpu.SMEM)] + [vm] * len(args) + [anywhere] * len(begun),
+        in_specs=[vm] * len(args) + [anywhere] * len(begun),
         out_specs=anywhere,
         out_shape=jax.ShapeDtypeStruct((rows, D), f32),
         scratch_shapes=[pltpu.VMEM((rows // 2, D), f32), pltpu.SemaphoreType.DMA],
-        input_output_aliases={1 + len(args): 0} if begun else {},
+        input_output_aliases={len(args): 0} if begun else {},
         cost_estimate=pl.CostEstimate(flops=0, bytes_accessed=6 * rows * D, transcendentals=0),
         compiler_params=pltpu.CompilerParams(vmem_limit_bytes=4 << 20),
-    )(place, *args, *begun)
-
-
-def small_call(kernel, place, args, outs):
+    )(*args, *begun)
+
+
+def small_call(kernel, args, outs):
     vm = pl.BlockSpec(memory_space=pltpu.VMEM)
-    head = [] if place is None else [place]
     return pl.pallas_call(
         kernel,
-        in_specs=[pl.BlockSpec(memory_space=pltpu.SMEM)] * len(head) + [vm] * len(args),
+        in_specs=[vm] * len(args),
         out_specs=[vm] * len(outs),
         out_shape=outs,
         compiler_params=pltpu.CompilerParams(vmem_limit_bytes=3 << 20),
-    )(*head, *args)
-
-
-def scan_steps(place, mine, theirs, sent):
+    )(*args)
+
+
+def scan_steps(mine, theirs, sent):
     half = mine.shape[0]
     part = half // 4
     pair = [(i, i ^ 1) for i in range(32)]
@@ -379,16 +388,16 @@
 
     narrow, wide = pltpu.VMEM((part, D), bf16), pltpu.VMEM((part, D), f32)
     got = lax.ppermute(sent, "step", pair)
-    own, *pieces = small_call(split_kernel, place, (mine, got), [wide] + [narrow] * 3)
+    own, *pieces = small_call(split_kernel, (mine, got), [wide] + [narrow] * 3)
     xs = [lax.ppermute(piece, "step", along_x(k)) for k, piece in zip((1, 2, 3), pieces)]
-    (row,) = small_call(row_kernel, None, (own, *xs), [narrow])
+    (row,) = small_call(row_kernel, (own, *xs), [narrow])
     ys = [lax.ppermute(row, "step", along_y(k)) for k in (1, 2, 3)]
-    home, *away = small_call(before_kernel, place, (own, *xs, *ys), [wide] + [narrow] * 3)
+    home, *away = small_call(before_kernel, (own, *xs, *ys), [wide] + [narrow] * 3)
     back = [lax.ppermute(piece, "step", along_x(k)) for k, piece in zip((1, 2, 3), away)]
-    (given,) = small_call(given_kernel, place, (mine, home, *back), [pltpu.VMEM((half, D), bf16)])
+    (given,) = small_call(given_kernel, (mine, home, *back), [pltpu.VMEM((half, D), bf16)])
     other = lax.ppermute(given, "step", pair)
-    begun = store_call(own_half_kernel, place, (mine, got, home, *back), (), 2 * half)
-    return store_call(other_half_kernel, place, (theirs, other), (begun,), 2 * half)
+    begun = store_call(own_half_kernel, (mine, got, home, *back), (), 2 * half)
+    return store_call(other_half_kernel, (theirs, other), (begun,), 2 * half)
 
 
 def on_device(states, step_times, positions, w_qkv, qk_gain, w_out, time_weight):
@@ -417,7 +426,7 @@
     late = (step_times, place, q, far, state, x, gate, w_out)
     theirs, sent = finish(True, *late)
     (mine,) = finish(False, *late)
-    return scan_steps(place, mine, theirs, sent)[None]
+    return scan_steps(mine, theirs, sent)[None]
 
 
 def solution(mesh):

time: 75.2 us -> 72.7 us (0.967)
  Pallas kernels: 31.7 us -> 28.9 us
    pallas_call x6, Pallas kernels: 5.07 us -> 2.29 us  [the longest x2 1.96 us: store_call(): pl.pallas_call(kernel, in_specs=[vm] * len(args) + [anywhere] * len(begun...]
  transfers between devices with their start and end apart: 17 -> 17, of which waited for: 7 -> 8; matrix products, arithmetic and copies ran while one was open for 0% -> 0% of each run, Pallas kernels for 28% -> 29%
where the time goes in v7:
time: 72.7 us; the launch traced here: 72.6 us
  starting transfers between devices  29.4 us (40%)
  Pallas kernels  28.9 us (40%)
  waiting for transfers between devices  11 us (15%)
  local copies, waits for them, and re-layouts  2.7 us (4%)
    pallas_call x4, Pallas kernels, project(): pl.pallas_call(functools.partial(project_kernel, with_q, len(ids)), in_sp...  14 us
    ppermute x6, starting transfers between devices, scan_steps(): lax.ppermute(piece, 'step', along_x(k))  9.7 us
    ppermute x3, starting transfers between devices, on_device(): to_left = lambda v: lax.ppermute(v, 'seq', left)  7.52 us
    ppermute x6, waiting for transfers between devices, scan_steps(): lax.ppermute(piece, 'step', along_x(k))  6.38 us
    pallas_call x2, Pallas kernels, attend(): pl.pallas_call(functools.partial(attend_kernel, len(kvs)), in_specs=[vm]...  5.63 us
    ppermute x3, starting transfers between devices, scan_steps(): ys = [lax.ppermute(row, 'step', along_y(k)) for k in (1, 2, 3)]  5.06 us
    pallas_call x2, Pallas kernels, finish(): pl.pallas_call(functools.partial(finish_kernel, theirs), in_specs=[pl.Blo...  4.8 us
    ppermute x1, starting transfers between devices, scan_steps(): other = lax.ppermute(given, 'step', pair)  3.24 us
  transfers between devices with their start and end apart: 17, of which 8 were waited for; matrix products, arithmetic and copies ran while one was open for 0% of the time, Pallas kernels for 29%

profile of v7, /device:TPU:1, one launch (start us, length us, event | category | flops | bytes accessed | tf_op | source)
XLA Modules:
  0.0 72.6 jit_solution(16229849508850037428)
XLA Ops:
  1.2 2.5 %collective-permute-start = (bf16[128,1664]{1,0:T(8,128)(2,1)S(1)}, bf16[128,1664]{1,0:T(8,128)(2,1)S(1)}, u32[]{:S(2)}, u32[]{:S(2)}) collective-permute-start(bf16[128,1664]{1,0:T(8,128)(2,1)S(1)} %get-tuple-element.45.first.refs_0_), channel_id=1, source_target_pairs={{0,1},{1,2},{2,3},{3,0},{4,5},{5,6},{6,7},{7,4},{8,9},{9,10},{10,1... | collective-permute-start | bytes 1277960 | tf_op jit(solution)/shard_map/ppermute | solution.py:407
  3.7 2.2 %collective-permute-start.2 = (bf16[128,1664]{1,0:T(8,128)(2,1)S(1)}, bf16[128,1664]{1,0:T(8,128)(2,1)S(1)}, u32[]{:S(2)}, u32[]{:S(2)}) collective-permute-start(bf16[128,1664]{1,0:T(8,128)(2,1)S(1)} %get-tuple-element.46.second.refs_1_), channel_id=1, source_target_pairs={{0,3},{1,0},{2,1},{3,2},{4,7},{5,4},{6,5},{7,6},{8,11},{9,8},{10,9... | collective-permute-start | bytes 1277960 | tf_op jit(solution)/shard_map/ppermute | solution.py:408
  5.9 1.8 %copy-done.3 = bf16[256,4608]{1,0:T(8,128)(2,1)S(1)} copy-done((bf16[256,4608]{1,0:T(8,128)(2,1)S(1)}, bf16[256,4608]{1,0:T(8,128)(2,1)}, u32[]{:S(2)}) %copy-start.3) | copy-done | bytes 2359320
  8.8 2.7 %collective-permute-start.5 = (bf16[128,1536]{1,0:T(8,128)(2,1)S(1)}, bf16[128,1536]{1,0:T(8,128)(2,1)S(1)}, u32[]{:S(2)}, u32[]{:S(2)}) collective-permute-start(bf16[128,1536]{1,0:T(8,128)(2,1)S(1)} %get-tuple-element.61), channel_id=1, source_target_pairs={{0,3},{1,0},{2,1},{3,2},{4,7},{5,4},{6,5},{7,6},{8,11},{9,8},{10,9... | collective-permute-start | bytes 1179656 | tf_op jit(solution)/shard_map/ppermute | solution.py:408
  12.4 4.4 %shard_map.75 = (bf16[256,1536]{1,0:T(8,128)(2,1)S(1)}, bf16[256,1536]{1,0:T(8,128)(2,1)S(1)}, bf16[256,1536]{1,0:T(8,128)(2,1)S(1)}) custom-call(bf16[128,1664]{1,0:T(8,128)(2,1)S(1)} %get-tuple-element.45.first.refs_0_, bf16[128,1664]{1,0:T(8,128)(2,1)S(1)} %get-tuple-element.46.second.refs_1_, f32[1,1536]{1,0:T(1,128)S(1)} %get-tuple-element.54.refs_2_.refs_4_, ...), custom_call_target="tpu_custom_call" | custom-call | flops 3623878656 | bytes 14155776 | tf_op jit(solution)/shard_map/pallas_call | solution.py:152
  16.9 2.7 %collective-permute-start.3 = (bf16[128,1664]{1,0:T(8,128)(2,1)S(1)}, bf16[128,1664]{1,0:T(8,128)(2,1)S(1)}, u32[]{:S(2)}, u32[]{:S(2)}) collective-permute-start(bf16[128,1664]{1,0:T(8,128)(2,1)S(1)} %collective-permute-done.2.refs_3_.refs_1_), channel_id=1, source_target_pairs={{0,3},{1,0},{2,1},{3,2},{4,7},{5,4},{6,5},{7,6},{8,11},{9,8},{10,9... | collective-permute-start | bytes 1277960 | tf_op jit(solution)/shard_map/ppermute | solution.py:408
  19.5 3.1 %shard_map.78 = (bf16[256,1536]{1,0:T(8,128)(2,1)S(1)}, bf16[256,1536]{1,0:T(8,128)(2,1)S(1)}) custom-call(bf16[128,1664]{1,0:T(8,128)(2,1)S(1)} %collective-permute-done.refs_2_.refs_0_, bf16[128,1664]{1,0:T(8,128)(2,1)S(1)} %collective-permute-done.2.refs_3_.refs_1_, f32[1,1536]{1,0:T(1,128)S(1)} %get-tuple-element.54.refs_2_.refs_4_, ...), custom_call_target="tpu_custom_call" | custom-call | flops 2415919104 | bytes 9437184 | tf_op jit(solution)/shard_map/pallas_call | solution.py:152
  22.7 3.8 %shard_map.79 = (f32[12,256,128]{2,1,0:T(8,128)S(1)}, f32[12,256,128]{2,1,0:T(8,128)S(1)}, f32[256,1536]{1,0:T(8,128)S(1)}) custom-call(bf16[256,1536]{1,0:T(8,128)(2,1)S(1)} %get-tuple-element.57.q_ref, bf16[256,1536]{1,0:T(8,128)(2,1)S(1)} %get-tuple-element.64.refs_0_, bf16[256,1536]{1,0:T(8,128)(2,1)S(1)} %get-tuple-element.65.refs_1_, ...), custom_call_target="tpu_custom_call" | custom-call | flops 1610612736 | bytes 3145728 | tf_op jit(solution)/shard_map/pallas_call | solution.py:205
  26.5 3.1 %shard_map.77 = (bf16[256,1536]{1,0:T(8,128)(2,1)S(1)}, bf16[256,1536]{1,0:T(8,128)(2,1)S(1)}) custom-call(bf16[128,1536]{1,0:T(8,128)(2,1)S(1)} %collective-permute-done.4.refs_0_, bf16[128,1536]{1,0:T(8,128)(2,1)S(1)} %collective-permute-done.5.refs_1_, bf16[128,1664]{1,0:T(8,128)(2,1)S(1)} %collective-permute-done.refs_2_.refs_0_, ...), custom_call_target="tpu_custom_call" | custom-call | flops 2415919104 | bytes 9437184 | tf_op jit(solution)/shard_map/pallas_call | solution.py:152
  29.6 1.9 %shard_map.80 = (f32[12,256,128]{2,1,0:T(8,128)S(1)}, f32[12,256,128]{2,1,0:T(8,128)S(1)}, f32[256,1536]{1,0:T(8,128)S(1)}) custom-call(bf16[256,1536]{1,0:T(8,128)(2,1)S(1)} %get-tuple-element.57.q_ref, bf16[256,1536]{1,0:T(8,128)(2,1)S(1)} %get-tuple-element.62.refs_0_, bf16[256,1536]{1,0:T(8,128)(2,1)S(1)} %get-tuple-element.63.refs_1_, ...), custom_call_target="tpu_custom_call" | custom-call | flops 805306368 | bytes 3145728 | tf_op jit(solution)/shard_map/pallas_call | solution.py:205
  31.5 1.4 %collective-permute-done.1.refs_0_ = bf16[128,1664]{1,0:T(8,128)(2,1)S(1)} collective-permute-done((bf16[128,1664]{1,0:T(8,128)(2,1)S(1)}, bf16[128,1664]{1,0:T(8,128)(2,1)S(1)}, u32[]{:S(2)}, u32[]{:S(2)}) %collective-permute-start.1) | collective-permute-done | bytes 426016 | tf_op jit(solution)/shard_map/ppermute | solution.py:407
  32.9 3.4 %shard_map.76 = (bf16[256,1536]{1,0:T(8,128)(2,1)S(1)}, bf16[256,1536]{1,0:T(8,128)(2,1)S(1)}) custom-call(bf16[128,1664]{1,0:T(8,128)(2,1)S(1)} %collective-permute-done.1.refs_0_, bf16[128,1664]{1,0:T(8,128)(2,1)S(1)} %collective-permute-done.3.refs_1_, f32[1,1536]{1,0:T(1,128)S(1)} %get-tuple-element.54.refs_2_.refs_4_, ...), custom_call_target="tpu_custom_call" | custom-call | flops 2415919104 | bytes 9437184 | tf_op jit(solution)/shard_map/pallas_call | solution.py:152
  36.4 2.4 %shard_map.81 = (f32[128,1536]{1,0:T(8,128)S(1)}, bf16[128,1536]{1,0:T(8,128)(2,1)S(1)}) custom-call(s32[1,2]{1,0:T(1,128)S(1)} %copy-done.2, s32[3]{0:T(128)S(1)} %pad_add_fusion.place, bf16[256,1536]{1,0:T(8,128)(2,1)S(1)} %get-tuple-element.57.q_ref, bf16[256,1536]{1,0:T(8,128)(2,1)S(1)} %get-tuple-element.58.k_ref, ...), custom_call_target="tpu_custom_call" | custom-call | flops 1006632960 | bytes 4718592 | tf_op jit(solution)/shard_map/pallas_call | solution.py:253
  38.8 1.3 %collective-permute-start.6 = (bf16[128,1536]{1,0:T(8,128)(2,1)S(1)}, bf16[128,1536]{1,0:T(8,128)(2,1)S(1)}, u32[]{:S(2)}, u32[]{:S(2)}) collective-permute-start(bf16[128,1536]{1,0:T(8,128)(2,1)S(1)} %get-tuple-element.76), channel_id=1, source_target_pairs={{0,4},{4,0},{8,12},{12,8},{16,20},{20,16},{24,28},{28,24},{32,36},... | collective-permute-start | bytes 1179656 | tf_op jit(solution)/shard_map/ppermute | solution.py:390
  40.1 2.4 %shard_map.82.mine = f32[128,1536]{1,0:T(8,128)S(1)} custom-call(s32[1,2]{1,0:T(1,128)S(1)} %copy-done.2, s32[3]{0:T(128)S(1)} %pad_add_fusion.place, bf16[256,1536]{1,0:T(8,128)(2,1)S(1)} %get-tuple-element.57.q_ref, bf16[256,1536]{1,0:T(8,128)(2,1)S(1)} %get-tuple-element.58.k_ref, bf16[256,1536]{1,0:T(8,128)(2,1)S(1)} %get-tuple-element.59.v_ref, ...), custom_call_target="tpu_custom_call" | custom-call | flops 1006632960 | bytes 4718592 | tf_op jit(solution)/shard_map/pallas_call | solution.py:253
  43.9 2.4 %collective-permute-start.8 = (bf16[32,1536]{1,0:T(8,128)(2,1)S(1)}, bf16[32,1536]{1,0:T(8,128)(2,1)S(1)}, u32[]{:S(2)}, u32[]{:S(2)}) collective-permute-start(bf16[32,1536]{1,0:T(8,128)(2,1)S(1)} %get-tuple-element.79), channel_id=1, source_target_pairs={{0,16},{4,20},{8,24},{12,28},{16,0},{20,4},{24,8},{28,12},{32,48},... | collective-permute-start | bytes 294920 | tf_op jit(solution)/shard_map/ppermute | solution.py:392
  48.3 3.1 %collective-permute-done.8.two.refs_1_ = bf16[32,1536]{1,0:T(8,128)(2,1)S(1)} collective-permute-done((bf16[32,1536]{1,0:T(8,128)(2,1)S(1)}, bf16[32,1536]{1,0:T(8,128)(2,1)S(1)}, u32[]{:S(2)}, u32[]{:S(2)}) %collective-permute-start.8) | collective-permute-done | bytes 98336 | tf_op jit(solution)/shard_map/ppermute | solution.py:392
  51.4 1.4 %collective-permute-start.10 = (bf16[32,1536]{1,0:T(8,128)(2,1)S(1)}, bf16[32,1536]{1,0:T(8,128)(2,1)S(1)}, u32[]{:S(2)}, u32[]{:S(2)}) collective-permute-start(bf16[32,1536]{1,0:T(8,128)(2,1)S(1)} %shard_map.84), channel_id=1, source_target_pairs={{0,32},{4,36},{8,40},{12,44},{16,48},{20,52},{24,56},{28,60},{32,6... | collective-permute-start | bytes 294920 | tf_op jit(solution)/shard_map/ppermute | solution.py:394
  52.8 2.6 %collective-permute-start.11 = (bf16[32,1536]{1,0:T(8,128)(2,1)S(1)}, bf16[32,1536]{1,0:T(8,128)(2,1)S(1)}, u32[]{:S(2)}, u32[]{:S(2)}) collective-permute-start(bf16[32,1536]{1,0:T(8,128)(2,1)S(1)} %shard_map.84), channel_id=1, source_target_pairs={{0,64},{4,68},{8,72},{12,76},{16,80},{20,84},{24,88},{28,92},{32,9... | collective-permute-start | bytes 294920 | tf_op jit(solution)/shard_map/ppermute | solution.py:394
  56.5 2.8 %collective-permute-done.11.refs_4_ = bf16[32,1536]{1,0:T(8,128)(2,1)S(1)} collective-permute-done((bf16[32,1536]{1,0:T(8,128)(2,1)S(1)}, bf16[32,1536]{1,0:T(8,128)(2,1)S(1)}, u32[]{:S(2)}, u32[]{:S(2)}) %collective-permute-start.11) | collective-permute-done | bytes 98336 | tf_op jit(solution)/shard_map/ppermute | solution.py:394
  59.4 1.4 %collective-permute-start.13 = (bf16[32,1536]{1,0:T(8,128)(2,1)S(1)}, bf16[32,1536]{1,0:T(8,128)(2,1)S(1)}, u32[]{:S(2)}, u32[]{:S(2)}) collective-permute-start(bf16[32,1536]{1,0:T(8,128)(2,1)S(1)} %get-tuple-element.82), channel_id=1, source_target_pairs={{0,8},{4,12},{8,16},{12,20},{16,24},{20,28},{24,0},{28,4},{32,40},... | collective-permute-start | bytes 294920 | tf_op jit(solution)/shard_map/ppermute | solution.py:396
  60.9 2.1 %collective-permute-start.14 = (bf16[32,1536]{1,0:T(8,128)(2,1)S(1)}, bf16[32,1536]{1,0:T(8,128)(2,1)S(1)}, u32[]{:S(2)}, u32[]{:S(2)}) collective-permute-start(bf16[32,1536]{1,0:T(8,128)(2,1)S(1)} %get-tuple-element.83), channel_id=1, source_target_pairs={{0,16},{4,20},{8,24},{12,28},{16,0},{20,4},{24,8},{28,12},{32,48},... | collective-permute-start | bytes 294920 | tf_op jit(solution)/shard_map/ppermute | solution.py:396
  64.3 1.8 %collective-permute-done.14.refs_2_ = bf16[32,1536]{1,0:T(8,128)(2,1)S(1)} collective-permute-done((bf16[32,1536]{1,0:T(8,128)(2,1)S(1)}, bf16[32,1536]{1,0:T(8,128)(2,1)S(1)}, u32[]{:S(2)}, u32[]{:S(2)}) %collective-permute-start.14) | collective-permute-done | bytes 98336 | tf_op jit(solution)/shard_map/ppermute | solution.py:396
  66.9 3.2 %collective-permute-start.16 = (bf16[128,1536]{1,0:T(8,128)(2,1)S(1)}, bf16[128,1536]{1,0:T(8,128)(2,1)S(1)}, u32[]{:S(2)}, u32[]{:S(2)}) collective-permute-start(bf16[128,1536]{1,0:T(8,128)(2,1)S(1)} %shard_map.86), channel_id=1, source_target_pairs={{0,4},{4,0},{8,12},{12,8},{16,20},{20,16},{24,28},{28,24},{32,36},... | collective-permute-start | bytes 1179656 | tf_op jit(solution)/shard_map/ppermute | solution.py:398
  (49 shorter events, 12.2 us)
Async XLA Ops:
  0.0 5.9 %copy-start.2 = (s32[1,2]{1,0:T(1,128)S(1)}, s32[1,2]{1,0:T(1,128)}, u32[]{:S(2)}) copy-start(s32[1,2]{1,0:T(1,128)} %times.5) | copy-start | bytes 28
  1.2 15.6 %collective-permute-start = (bf16[128,1664]{1,0:T(8,128)(2,1)S(1)}, bf16[128,1664]{1,0:T(8,128)(2,1)S(1)}, u32[]{:S(2)}, u32[]{:S(2)}) collective-permute-start(bf16[128,1664]{1,0:T(8,128)(2,1)S(1)} %get-tuple-element.45.first.refs_0_), channel_id=1, source_target_pairs={{0,1},{1,2},{2,3},{3,0},{4,5},{5,6},{6,7},{7,4},{8,9},{9,10},{10,1... | collective-permute-start | bytes 1277960 | tf_op jit(solution)/shard_map/ppermute | solution.py:407
  3.7 13.1 %collective-permute-start.2 = (bf16[128,1664]{1,0:T(8,128)(2,1)S(1)}, bf16[128,1664]{1,0:T(8,128)(2,1)S(1)}, u32[]{:S(2)}, u32[]{:S(2)}) collective-permute-start(bf16[128,1664]{1,0:T(8,128)(2,1)S(1)} %get-tuple-element.46.second.refs_1_), channel_id=1, source_target_pairs={{0,3},{1,0},{2,1},{3,2},{4,7},{5,4},{6,5},{7,6},{8,11},{9,8},{10,9... | collective-permute-start | bytes 1277960 | tf_op jit(solution)/shard_map/ppermute | solution.py:408
  5.9 5.6 %slice-start = ((s8[14155776]{0:T(1024)(128)(4,1)}), s8[1572864]{0:T(1024)(128)(4,1)S(1)}, s32[]{:S(2)}) async-start(s8[14155776]{0:T(1024)(128)(4,1)} %bitcast.6), calls=%async_computation | async-start | bytes 3145728
  7.7 4.7 %slice-start.3 = ((s8[14155776]{0:T(1024)(128)(4,1)}), s8[4194304]{0:T(1024)(128)(4,1)S(1)}, s32[]{:S(2)}) async-start(s8[14155776]{0:T(1024)(128)(4,1)} %bitcast.6), calls=%async_computation.3 | async-start | bytes 8388608
  7.7 4.7 %copy-start.1 = (f32[2,1536]{1,0:T(2,128)S(1)}, f32[2,1536]{1,0:T(2,128)}, u32[]{:S(2)}) copy-start(f32[2,1536]{1,0:T(2,128)} %refs_4_.5) | copy-start | bytes 36868
  8.8 17.6 %collective-permute-start.4 = (bf16[128,1536]{1,0:T(8,128)(2,1)S(1)}, bf16[128,1536]{1,0:T(8,128)(2,1)S(1)}, u32[]{:S(2)}, u32[]{:S(2)}) collective-permute-start(bf16[128,1536]{1,0:T(8,128)(2,1)S(1)} %get-tuple-element.60), channel_id=1, source_target_pairs={{0,1},{1,2},{2,3},{3,0},{4,5},{5,6},{6,7},{7,4},{8,9},{9,10},{10,1... | collective-permute-start | bytes 1179656 | tf_op jit(solution)/shard_map/ppermute | solution.py:407
  8.8 17.6 %collective-permute-start.5 = (bf16[128,1536]{1,0:T(8,128)(2,1)S(1)}, bf16[128,1536]{1,0:T(8,128)(2,1)S(1)}, u32[]{:S(2)}, u32[]{:S(2)}) collective-permute-start(bf16[128,1536]{1,0:T(8,128)(2,1)S(1)} %get-tuple-element.61), channel_id=1, source_target_pairs={{0,3},{1,0},{2,1},{3,2},{4,7},{5,4},{6,5},{7,6},{8,11},{9,8},{10,9... | collective-permute-start | bytes 1179656 | tf_op jit(solution)/shard_map/ppermute | solution.py:408
  16.8 16.2 %collective-permute-start.1 = (bf16[128,1664]{1,0:T(8,128)(2,1)S(1)}, bf16[128,1664]{1,0:T(8,128)(2,1)S(1)}, u32[]{:S(2)}, u32[]{:S(2)}) collective-permute-start(bf16[128,1664]{1,0:T(8,128)(2,1)S(1)} %collective-permute-done.refs_2_.refs_0_), channel_id=1, source_target_pairs={{0,1},{1,2},{2,3},{3,0},{4,5},{5,6},{6,7},{7,4},{8,9},{9,10},{10,1... | collective-permute-start | bytes 1277960 | tf_op jit(solution)/shard_map/ppermute | solution.py:407
  16.9 16.1 %collective-permute-start.3 = (bf16[128,1664]{1,0:T(8,128)(2,1)S(1)}, bf16[128,1664]{1,0:T(8,128)(2,1)S(1)}, u32[]{:S(2)}, u32[]{:S(2)}) collective-permute-start(bf16[128,1664]{1,0:T(8,128)(2,1)S(1)} %collective-permute-done.2.refs_3_.refs_1_), channel_id=1, source_target_pairs={{0,3},{1,0},{2,1},{3,2},{4,7},{5,4},{6,5},{7,6},{8,11},{9,8},{10,9... | collective-permute-start | bytes 1277960 | tf_op jit(solution)/shard_map/ppermute | solution.py:408
  29.6 6.7 %slice-start.4 = ((s8[4718592]{0:T(1024)(128)(4,1)}), s8[4194304]{0:T(1024)(128)(4,1)S(1)}, s32[]{:S(2)}) async-start(s8[4718592]{0:T(1024)(128)(4,1)} %bitcast.8), calls=%async_computation.4 | async-start | bytes 8388608
  31.5 4.8 %slice-start.5 = ((s8[4718592]{0:T(1024)(128)(4,1)}), s8[524288]{0:T(1024)(128)(4,1)S(1)}, s32[]{:S(2)}) async-start(s8[4718592]{0:T(1024)(128)(4,1)} %bitcast.8), calls=%async_computation.5 | async-start | bytes 1048576
  31.5 4.8 %copy-start = (bf16[1,256,1536]{2,1,0:T(8,128)(2,1)S(1)}, bf16[1,256,1536]{2,1,0:T(8,128)(2,1)}, u32[]{:S(2)}) copy-start(bf16[1,256,1536]{2,1,0:T(8,128)(2,1)} %param.7) | copy-start | bytes 2359300
  38.8 3.7 %collective-permute-start.6 = (bf16[128,1536]{1,0:T(8,128)(2,1)S(1)}, bf16[128,1536]{1,0:T(8,128)(2,1)S(1)}, u32[]{:S(2)}, u32[]{:S(2)}) collective-permute-start(bf16[128,1536]{1,0:T(8,128)(2,1)S(1)} %get-tuple-element.76), channel_id=1, source_target_pairs={{0,4},{4,0},{8,12},{12,8},{16,20},{20,16},{24,28},{28,24},{32,36},... | collective-permute-start | bytes 1179656 | tf_op jit(solution)/shard_map/ppermute | solution.py:390
  42.6 5.7 %collective-permute-start.7 = (bf16[32,1536]{1,0:T(8,128)(2,1)S(1)}, bf16[32,1536]{1,0:T(8,128)(2,1)S(1)}, u32[]{:S(2)}, u32[]{:S(2)}) collective-permute-start(bf16[32,1536]{1,0:T(8,128)(2,1)S(1)} %get-tuple-element.78), channel_id=1, source_target_pairs={{0,8},{4,12},{8,16},{12,20},{16,24},{20,28},{24,0},{28,4},{32,40},... | collective-permute-start | bytes 294920 | tf_op jit(solution)/shard_map/ppermute | solution.py:392
  43.9 7.5 %collective-permute-start.8 = (bf16[32,1536]{1,0:T(8,128)(2,1)S(1)}, bf16[32,1536]{1,0:T(8,128)(2,1)S(1)}, u32[]{:S(2)}, u32[]{:S(2)}) collective-permute-start(bf16[32,1536]{1,0:T(8,128)(2,1)S(1)} %get-tuple-element.79), channel_id=1, source_target_pairs={{0,16},{4,20},{8,24},{12,28},{16,0},{20,4},{24,8},{28,12},{32,48},... | collective-permute-start | bytes 294920 | tf_op jit(solution)/shard_map/ppermute | solution.py:392
  46.3 5.1 %collective-permute-start.9 = (bf16[32,1536]{1,0:T(8,128)(2,1)S(1)}, bf16[32,1536]{1,0:T(8,128)(2,1)S(1)}, u32[]{:S(2)}, u32[]{:S(2)}) collective-permute-start(bf16[32,1536]{1,0:T(8,128)(2,1)S(1)} %get-tuple-element.80), channel_id=1, source_target_pairs={{0,24},{4,28},{8,0},{12,4},{16,8},{20,12},{24,16},{28,20},{32,56},... | collective-permute-start | bytes 294920 | tf_op jit(solution)/shard_map/ppermute | solution.py:392
  51.4 5.1 %collective-permute-start.10 = (bf16[32,1536]{1,0:T(8,128)(2,1)S(1)}, bf16[32,1536]{1,0:T(8,128)(2,1)S(1)}, u32[]{:S(2)}, u32[]{:S(2)}) collective-permute-start(bf16[32,1536]{1,0:T(8,128)(2,1)S(1)} %shard_map.84), channel_id=1, source_target_pairs={{0,32},{4,36},{8,40},{12,44},{16,48},{20,52},{24,56},{28,60},{32,6... | collective-permute-start | bytes 294920 | tf_op jit(solution)/shard_map/ppermute | solution.py:394
  52.8 6.5 %collective-permute-start.11 = (bf16[32,1536]{1,0:T(8,128)(2,1)S(1)}, bf16[32,1536]{1,0:T(8,128)(2,1)S(1)}, u32[]{:S(2)}, u32[]{:S(2)}) collective-permute-start(bf16[32,1536]{1,0:T(8,128)(2,1)S(1)} %shard_map.84), channel_id=1, source_target_pairs={{0,64},{4,68},{8,72},{12,76},{16,80},{20,84},{24,88},{28,92},{32,9... | collective-permute-start | bytes 294920 | tf_op jit(solution)/shard_map/ppermute | solution.py:394
  55.4 3.9 %collective-permute-start.12 = (bf16[32,1536]{1,0:T(8,128)(2,1)S(1)}, bf16[32,1536]{1,0:T(8,128)(2,1)S(1)}, u32[]{:S(2)}, u32[]{:S(2)}) collective-permute-start(bf16[32,1536]{1,0:T(8,128)(2,1)S(1)} %shard_map.84), channel_id=1, source_target_pairs={{0,96},{4,100},{8,104},{12,108},{16,112},{20,116},{24,120},{28,124... | collective-permute-start | bytes 294920 | tf_op jit(solution)/shard_map/ppermute | solution.py:394
  59.4 4.8 %collective-permute-start.13 = (bf16[32,1536]{1,0:T(8,128)(2,1)S(1)}, bf16[32,1536]{1,0:T(8,128)(2,1)S(1)}, u32[]{:S(2)}, u32[]{:S(2)}) collective-permute-start(bf16[32,1536]{1,0:T(8,128)(2,1)S(1)} %get-tuple-element.82), channel_id=1, source_target_pairs={{0,8},{4,12},{8,16},{12,20},{16,24},{20,28},{24,0},{28,4},{32,40},... | collective-permute-start | bytes 294920 | tf_op jit(solution)/shard_map/ppermute | solution.py:396
  60.9 5.2 %collective-permute-start.14 = (bf16[32,1536]{1,0:T(8,128)(2,1)S(1)}, bf16[32,1536]{1,0:T(8,128)(2,1)S(1)}, u32[]{:S(2)}, u32[]{:S(2)}) collective-permute-start(bf16[32,1536]{1,0:T(8,128)(2,1)S(1)} %get-tuple-element.83), channel_id=1, source_target_pairs={{0,16},{4,20},{8,24},{12,28},{16,0},{20,4},{24,8},{28,12},{32,48},... | collective-permute-start | bytes 294920 | tf_op jit(solution)/shard_map/ppermute | solution.py:396
  63.0 3.8 %collective-permute-start.15 = (bf16[32,1536]{1,0:T(8,128)(2,1)S(1)}, bf16[32,1536]{1,0:T(8,128)(2,1)S(1)}, u32[]{:S(2)}, u32[]{:S(2)}) collective-permute-start(bf16[32,1536]{1,0:T(8,128)(2,1)S(1)} %get-tuple-element.84), channel_id=1, source_target_pairs={{0,24},{4,28},{8,0},{12,4},{16,8},{20,12},{24,16},{28,20},{32,56},... | collective-permute-start | bytes 294920 | tf_op jit(solution)/shard_map/ppermute | solution.py:396
  66.9 4.6 %collective-permute-start.16 = (bf16[128,1536]{1,0:T(8,128)(2,1)S(1)}, bf16[128,1536]{1,0:T(8,128)(2,1)S(1)}, u32[]{:S(2)}, u32[]{:S(2)}) collective-permute-start(bf16[128,1536]{1,0:T(8,128)(2,1)S(1)} %shard_map.86), channel_id=1, source_target_pairs={{0,4},{4,0},{8,12},{12,8},{16,20},{20,16},{24,28},{28,24},{32,36},... | collective-permute-start | bytes 1179656 | tf_op jit(solution)/shard_map/ppermute | solution.py:398
  (3 other events, 9.4 us)

commit v8 on v7

--- a/solution.py
+++ b/solution.py
@@ -42,6 +42,7 @@
     lane = lax.broadcasted_iota(jnp.int32, (1, HEAD), 1)
     rates[0:1, :] = jnp.exp(-math.log(10000.0) * (lane & (half_width - 1)).astype(f32) / half_width)
     rates[1:2, :] = jnp.where(lane < half_width, -1.0, 1.0)
+    rates[2:3, :] = jnp.full((1, HEAD), times[0, 1] - times[0, 0], jnp.int32).astype(f32) / 1000.0
 
 
 def modulation(step_times, time_weight, first, second):
@@ -51,7 +52,7 @@
         modulation_kernel,
         in_specs=[pl.BlockSpec(memory_space=pltpu.SMEM), vm, vm, vm],
         out_specs=[vm] * 6,
-        out_shape=[pltpu.VMEM((1, D), f32)] * 3 + [pltpu.VMEM((2, HEAD), f32)] + [pltpu.VMEM((half, D), bf16)] * 2,
+        out_shape=[pltpu.VMEM((1, D), f32)] * 3 + [pltpu.VMEM((3, HEAD), f32)] + [pltpu.VMEM((half, D), bf16)] * 2,
         cost_estimate=pl.CostEstimate(flops=HINT, bytes_accessed=0, transcendentals=0),
         compiler_params=pltpu.CompilerParams(vmem_limit_bytes=3 << 20),
     )(step_times, time_weight, first, second)
@@ -218,10 +219,10 @@
     )(q, *flat, *before)
 
 
-def finish_kernel(theirs, times, place, q_ref, k_ref, v_ref, m_ref, l_ref, acc_ref, x_ref, gate_ref, w_ref, *refs):
+def finish_kernel(theirs, rates, q_ref, k_ref, v_ref, m_ref, l_ref, acc_ref, x_ref, gate_ref, w_ref, *refs):
     out_ref, attended = refs[0], refs[-1]
     half = out_ref.shape[0]
-    which = 1 - place[0] if theirs else place[0]
+    which = 1 - here()[0] if theirs else here()[0]
     rows = pl.ds(pl.multiple_of(which * half, half), half)
     for h in range(HEADS):
         at = slice(h * HEAD, (h + 1) * HEAD)
@@ -235,7 +236,7 @@
         new = jnp.broadcast_to(new, (half, HEAD))
         _, total, acc = merge(new, total, acc, m_ref[h, rows, :], l_ref[h, rows, :], acc_ref[rows, at])
         attended[:, at] = (acc / total).astype(bf16)
-    size = jnp.full((1, TILE), times[0, 1] - times[0, 0], jnp.int32).astype(f32) / 1000.0
+    size = jnp.concatenate([rates[2:3, :]] * (TILE // HEAD), axis=1)
     for t in range(TILES):
         at = slice(t * TILE, (t + 1) * TILE)
         proj = jnp.dot(attended[...], w_ref[:, at], preferred_element_type=f32)
@@ -245,14 +246,14 @@
             refs[1][:, at] = inc.astype(bf16)
 
 
-def finish(theirs, step_times, place, q, kv, state, x, gate, w_out):
+def finish(theirs, rates, q, kv, state, x, gate, w_out):
     half = q.shape[0] // 2
     keys = kv[0].shape[0]
     vm = pl.BlockSpec(memory_space=pltpu.VMEM)
     outs = [pltpu.VMEM((half, D), f32)] + [pltpu.VMEM((half, D), bf16)] * theirs
     return pl.pallas_call(
         functools.partial(finish_kernel, theirs),
-        in_specs=[pl.BlockSpec(memory_space=pltpu.SMEM)] * 2 + [vm] * 9,
+        in_specs=[vm] * 10,
         out_specs=[vm] * len(outs),
         out_shape=outs,
         scratch_shapes=[pltpu.VMEM((half, D), bf16)],
@@ -262,7 +263,7 @@
             transcendentals=half * keys * HEADS,
         ),
         compiler_params=pltpu.CompilerParams(vmem_limit_bytes=12 << 20),
-    )(step_times, place, q, *kv, *state, x, gate, w_out)
+    )(rates, q, *kv, *state, x, gate, w_out)
 
 
 def here():
@@ -406,14 +407,11 @@
     left = [(i, (i - 1) % n) for i in range(n)]
     to_right = lambda v: lax.ppermute(v, "seq", right)
     to_left = lambda v: lax.ppermute(v, "seq", left)
-    step = lax.axis_index("step")
-    place = jnp.stack([step % 2, (step // 2) % 4, step // 8])
-
     x = states[0]
     first, second = with_positions(x, positions)
     r_first, l_second = to_right(first), to_left(second)
     modulated = modulation(step_times, time_weight, first, second)
-    shift, scale, gate, rates, bare_first, bare_second, place = lax.optimization_barrier((*modulated, place))
+    shift, scale, gate, rates, bare_first, bare_second = modulated
     r_second, l_first = to_right(bare_second), to_left(bare_first)
     forward = to_right(r_first), to_left(l_second)
 
@@ -423,7 +421,7 @@
     next_near = project((r_second, l_first), (r_first, l_second), *given, False)
     far = project(forward, (), *given, False)
     state = attend(q, [next_near], attend(q, [(k, v), near]))
-    late = (step_times, place, q, far, state, x, gate, w_out)
+    late = (rates, q, far, state, x, gate, w_out)
     theirs, sent = finish(True, *late)
     (mine,) = finish(False, *late)
     return scan_steps(mine, theirs, sent)[None]

time: 72.7 us -> 71.7 us (0.986)
  Pallas kernels: 28.9 us -> 27.9 us
    pallas_call x2, Pallas kernels: 4.8 us -> 3.71 us  [finish(): pl.pallas_call(functools.partial(finish_kernel, theirs), in_specs=[vm] *...]
  transfers between devices with their start and end apart: 17 -> 17, of which waited for: 8 -> 8; matrix products, arithmetic and copies ran while one was open for 0% -> 0% of each run, Pallas kernels for 29% -> 28%
where the time goes in v8:
time: 71.7 us; the launch traced here: 71.5 us
  starting transfers between devices  29.6 us (41%)
  Pallas kernels  27.9 us (39%)
  waiting for transfers between devices  11.1 us (15%)
  local copies, waits for them, and re-layouts  2.48 us (3%)
    pallas_call x4, Pallas kernels, project(): pl.pallas_call(functools.partial(project_kernel, with_q, len(ids)), in_sp...  14 us
    ppermute x6, starting transfers between devices, scan_steps(): lax.ppermute(piece, 'step', along_x(k))  9.7 us
    ppermute x3, starting transfers between devices, on_device(): to_left = lambda v: lax.ppermute(v, 'seq', left)  7.56 us
    ppermute x6, waiting for transfers between devices, scan_steps(): lax.ppermute(piece, 'step', along_x(k))  6.38 us
    pallas_call x2, Pallas kernels, attend(): pl.pallas_call(functools.partial(attend_kernel, len(kvs)), in_specs=[vm]...  5.67 us
    ppermute x3, starting transfers between devices, scan_steps(): ys = [lax.ppermute(row, 'step', along_y(k)) for k in (1, 2, 3)]  5.06 us
    pallas_call x2, Pallas kernels, finish(): pl.pallas_call(functools.partial(finish_kernel, theirs), in_specs=[vm] *...  3.71 us
    ppermute x1, starting transfers between devices, scan_steps(): other = lax.ppermute(given, 'step', pair)  3.26 us
  transfers between devices with their start and end apart: 17, of which 8 were waited for; matrix products, arithmetic and copies ran while one was open for 0% of the time, Pallas kernels for 28%

profile of v8, /device:TPU:1, one launch (start us, length us, event | category | flops | bytes accessed | tf_op | source)
XLA Modules:
  0.0 71.5 jit_solution(15653528470411948553)
XLA Ops:
  1.2 2.5 %collective-permute-start = (bf16[128,1664]{1,0:T(8,128)(2,1)S(1)}, bf16[128,1664]{1,0:T(8,128)(2,1)S(1)}, u32[]{:S(2)}, u32[]{:S(2)}) collective-permute-start(bf16[128,1664]{1,0:T(8,128)(2,1)S(1)} %get-tuple-element.38.first.refs_0_), channel_id=1, source_target_pairs={{0,1},{1,2},{2,3},{3,0},{4,5},{5,6},{6,7},{7,4},{8,9},{9,10},{10,1... | collective-permute-start | bytes 1277960 | tf_op jit(solution)/shard_map/ppermute | solution.py:408
  3.7 2.2 %collective-permute-start.2 = (bf16[128,1664]{1,0:T(8,128)(2,1)S(1)}, bf16[128,1664]{1,0:T(8,128)(2,1)S(1)}, u32[]{:S(2)}, u32[]{:S(2)}) collective-permute-start(bf16[128,1664]{1,0:T(8,128)(2,1)S(1)} %get-tuple-element.39.second.refs_1_), channel_id=1, source_target_pairs={{0,3},{1,0},{2,1},{3,2},{4,7},{5,4},{6,5},{7,6},{8,11},{9,8},{10,9... | collective-permute-start | bytes 1277960 | tf_op jit(solution)/shard_map/ppermute | solution.py:409
  6.0 2.4 %copy-done.2 = bf16[256,4608]{1,0:T(8,128)(2,1)S(1)} copy-done((bf16[256,4608]{1,0:T(8,128)(2,1)S(1)}, bf16[256,4608]{1,0:T(8,128)(2,1)}, u32[]{:S(2)}) %copy-start.2) | copy-done | bytes 2359320
  9.5 2.7 %collective-permute-start.5 = (bf16[128,1536]{1,0:T(8,128)(2,1)S(1)}, bf16[128,1536]{1,0:T(8,128)(2,1)S(1)}, u32[]{:S(2)}, u32[]{:S(2)}) collective-permute-start(bf16[128,1536]{1,0:T(8,128)(2,1)S(1)} %get-tuple-element.47), channel_id=1, source_target_pairs={{0,3},{1,0},{2,1},{3,2},{4,7},{5,4},{6,5},{7,6},{8,11},{9,8},{10,9... | collective-permute-start | bytes 1179656 | tf_op jit(solution)/shard_map/ppermute | solution.py:409
  12.2 4.4 %shard_map.75 = (bf16[256,1536]{1,0:T(8,128)(2,1)S(1)}, bf16[256,1536]{1,0:T(8,128)(2,1)S(1)}, bf16[256,1536]{1,0:T(8,128)(2,1)S(1)}) custom-call(bf16[128,1664]{1,0:T(8,128)(2,1)S(1)} %get-tuple-element.38.first.refs_0_, bf16[128,1664]{1,0:T(8,128)(2,1)S(1)} %get-tuple-element.39.second.refs_1_, f32[1,1536]{1,0:T(1,128)S(1)} %get-tuple-element.41.refs_2_.refs_4_, ...), custom_call_target="tpu_custom_call" | custom-call | flops 3623878656 | bytes 14155776 | tf_op jit(solution)/shard_map/pallas_call | solution.py:153
  16.7 2.7 %collective-permute-start.3 = (bf16[128,1664]{1,0:T(8,128)(2,1)S(1)}, bf16[128,1664]{1,0:T(8,128)(2,1)S(1)}, u32[]{:S(2)}, u32[]{:S(2)}) collective-permute-start(bf16[128,1664]{1,0:T(8,128)(2,1)S(1)} %collective-permute-done.2.refs_3_.refs_1_), channel_id=1, source_target_pairs={{0,3},{1,0},{2,1},{3,2},{4,7},{5,4},{6,5},{7,6},{8,11},{9,8},{10,9... | collective-permute-start | bytes 1277960 | tf_op jit(solution)/shard_map/ppermute | solution.py:409
  19.3 3.1 %shard_map.78 = (bf16[256,1536]{1,0:T(8,128)(2,1)S(1)}, bf16[256,1536]{1,0:T(8,128)(2,1)S(1)}) custom-call(bf16[128,1664]{1,0:T(8,128)(2,1)S(1)} %collective-permute-done.refs_2_.refs_0_, bf16[128,1664]{1,0:T(8,128)(2,1)S(1)} %collective-permute-done.2.refs_3_.refs_1_, f32[1,1536]{1,0:T(1,128)S(1)} %get-tuple-element.41.refs_2_.refs_4_, ...), custom_call_target="tpu_custom_call" | custom-call | flops 2415919104 | bytes 9437184 | tf_op jit(solution)/shard_map/pallas_call | solution.py:153
  22.5 3.8 %shard_map.79 = (f32[12,256,128]{2,1,0:T(8,128)S(1)}, f32[12,256,128]{2,1,0:T(8,128)S(1)}, f32[256,1536]{1,0:T(8,128)S(1)}) custom-call(bf16[256,1536]{1,0:T(8,128)(2,1)S(1)} %get-tuple-element.43.q_ref, bf16[256,1536]{1,0:T(8,128)(2,1)S(1)} %get-tuple-element.50.refs_0_, bf16[256,1536]{1,0:T(8,128)(2,1)S(1)} %get-tuple-element.51.refs_1_, ...), custom_call_target="tpu_custom_call" | custom-call | flops 1610612736 | bytes 3145728 | tf_op jit(solution)/shard_map/pallas_call | solution.py:206
  26.3 3.1 %shard_map.77 = (bf16[256,1536]{1,0:T(8,128)(2,1)S(1)}, bf16[256,1536]{1,0:T(8,128)(2,1)S(1)}) custom-call(bf16[128,1536]{1,0:T(8,128)(2,1)S(1)} %collective-permute-done.4.refs_0_, bf16[128,1536]{1,0:T(8,128)(2,1)S(1)} %collective-permute-done.5.refs_1_, bf16[128,1664]{1,0:T(8,128)(2,1)S(1)} %collective-permute-done.refs_2_.refs_0_, ...), custom_call_target="tpu_custom_call" | custom-call | flops 2415919104 | bytes 9437184 | tf_op jit(solution)/shard_map/pallas_call | solution.py:153
  29.5 1.9 %shard_map.80 = (f32[12,256,128]{2,1,0:T(8,128)S(1)}, f32[12,256,128]{2,1,0:T(8,128)S(1)}, f32[256,1536]{1,0:T(8,128)S(1)}) custom-call(bf16[256,1536]{1,0:T(8,128)(2,1)S(1)} %get-tuple-element.43.q_ref, bf16[256,1536]{1,0:T(8,128)(2,1)S(1)} %get-tuple-element.48.refs_0_, bf16[256,1536]{1,0:T(8,128)(2,1)S(1)} %get-tuple-element.49.refs_1_, ...), custom_call_target="tpu_custom_call" | custom-call | flops 805306368 | bytes 3145728 | tf_op jit(solution)/shard_map/pallas_call | solution.py:206
  31.4 1.5 %collective-permute-done.1.refs_0_ = bf16[128,1664]{1,0:T(8,128)(2,1)S(1)} collective-permute-done((bf16[128,1664]{1,0:T(8,128)(2,1)S(1)}, bf16[128,1664]{1,0:T(8,128)(2,1)S(1)}, u32[]{:S(2)}, u32[]{:S(2)}) %collective-permute-start.1) | collective-permute-done | bytes 426016 | tf_op jit(solution)/shard_map/ppermute | solution.py:408
  32.9 3.4 %shard_map.76 = (bf16[256,1536]{1,0:T(8,128)(2,1)S(1)}, bf16[256,1536]{1,0:T(8,128)(2,1)S(1)}) custom-call(bf16[128,1664]{1,0:T(8,128)(2,1)S(1)} %collective-permute-done.1.refs_0_, bf16[128,1664]{1,0:T(8,128)(2,1)S(1)} %collective-permute-done.3.refs_1_, f32[1,1536]{1,0:T(1,128)S(1)} %get-tuple-element.41.refs_2_.refs_4_, ...), custom_call_target="tpu_custom_call" | custom-call | flops 2415919104 | bytes 9437184 | tf_op jit(solution)/shard_map/pallas_call | solution.py:153
  36.4 1.9 %shard_map.81 = (f32[128,1536]{1,0:T(8,128)S(1)}, bf16[128,1536]{1,0:T(8,128)(2,1)S(1)}) custom-call(f32[3,128]{1,0:T(4,128)S(1)} %get-tuple-element.40.refs_5_.refs_7_.rates, bf16[256,1536]{1,0:T(8,128)(2,1)S(1)} %get-tuple-element.43.q_ref, bf16[256,1536]{1,0:T(8,128)(2,1)S(1)} %get-tuple-element.44.k_ref, bf16[256,1536]{1,0:T(8,128)(2,1)S(1)} %get-tuple-element.45.v_ref, ...), custom_call_target="tpu_custom_call" | custom-call | flops 1006632960 | bytes 4718592 | tf_op jit(solution)/shard_map/pallas_call | solution.py:254
  38.2 1.3 %collective-permute-start.6 = (bf16[128,1536]{1,0:T(8,128)(2,1)S(1)}, bf16[128,1536]{1,0:T(8,128)(2,1)S(1)}, u32[]{:S(2)}, u32[]{:S(2)}) collective-permute-start(bf16[128,1536]{1,0:T(8,128)(2,1)S(1)} %get-tuple-element.62), channel_id=1, source_target_pairs={{0,4},{4,0},{8,12},{12,8},{16,20},{20,16},{24,28},{28,24},{32,36},... | collective-permute-start | bytes 1179656 | tf_op jit(solution)/shard_map/ppermute | solution.py:391
  39.5 1.8 %shard_map.82.mine = f32[128,1536]{1,0:T(8,128)S(1)} custom-call(f32[3,128]{1,0:T(4,128)S(1)} %get-tuple-element.40.refs_5_.refs_7_.rates, bf16[256,1536]{1,0:T(8,128)(2,1)S(1)} %get-tuple-element.43.q_ref, bf16[256,1536]{1,0:T(8,128)(2,1)S(1)} %get-tuple-element.44.k_ref, bf16[256,1536]{1,0:T(8,128)(2,1)S(1)} %get-tuple-element.45.v_ref, ...), custom_call_target="tpu_custom_call" | custom-call | flops 1006632960 | bytes 4718592 | tf_op jit(solution)/shard_map/pallas_call | solution.py:254
  42.8 2.4 %collective-permute-start.8 = (bf16[32,1536]{1,0:T(8,128)(2,1)S(1)}, bf16[32,1536]{1,0:T(8,128)(2,1)S(1)}, u32[]{:S(2)}, u32[]{:S(2)}) collective-permute-start(bf16[32,1536]{1,0:T(8,128)(2,1)S(1)} %get-tuple-element.65), channel_id=1, source_target_pairs={{0,16},{4,20},{8,24},{12,28},{16,0},{20,4},{24,8},{28,12},{32,48},... | collective-permute-start | bytes 294920 | tf_op jit(solution)/shard_map/ppermute | solution.py:393
  47.2 3.1 %collective-permute-done.8.two.refs_1_ = bf16[32,1536]{1,0:T(8,128)(2,1)S(1)} collective-permute-done((bf16[32,1536]{1,0:T(8,128)(2,1)S(1)}, bf16[32,1536]{1,0:T(8,128)(2,1)S(1)}, u32[]{:S(2)}, u32[]{:S(2)}) %collective-permute-start.8) | collective-permute-done | bytes 98336 | tf_op jit(solution)/shard_map/ppermute | solution.py:393
  50.3 1.4 %collective-permute-start.10 = (bf16[32,1536]{1,0:T(8,128)(2,1)S(1)}, bf16[32,1536]{1,0:T(8,128)(2,1)S(1)}, u32[]{:S(2)}, u32[]{:S(2)}) collective-permute-start(bf16[32,1536]{1,0:T(8,128)(2,1)S(1)} %shard_map.84), channel_id=1, source_target_pairs={{0,32},{4,36},{8,40},{12,44},{16,48},{20,52},{24,56},{28,60},{32,6... | collective-permute-start | bytes 294920 | tf_op jit(solution)/shard_map/ppermute | solution.py:395
  51.7 2.6 %collective-permute-start.11 = (bf16[32,1536]{1,0:T(8,128)(2,1)S(1)}, bf16[32,1536]{1,0:T(8,128)(2,1)S(1)}, u32[]{:S(2)}, u32[]{:S(2)}) collective-permute-start(bf16[32,1536]{1,0:T(8,128)(2,1)S(1)} %shard_map.84), channel_id=1, source_target_pairs={{0,64},{4,68},{8,72},{12,76},{16,80},{20,84},{24,88},{28,92},{32,9... | collective-permute-start | bytes 294920 | tf_op jit(solution)/shard_map/ppermute | solution.py:395
  55.4 2.8 %collective-permute-done.11.refs_4_ = bf16[32,1536]{1,0:T(8,128)(2,1)S(1)} collective-permute-done((bf16[32,1536]{1,0:T(8,128)(2,1)S(1)}, bf16[32,1536]{1,0:T(8,128)(2,1)S(1)}, u32[]{:S(2)}, u32[]{:S(2)}) %collective-permute-start.11) | collective-permute-done | bytes 98336 | tf_op jit(solution)/shard_map/ppermute | solution.py:395
  58.4 1.4 %collective-permute-start.13 = (bf16[32,1536]{1,0:T(8,128)(2,1)S(1)}, bf16[32,1536]{1,0:T(8,128)(2,1)S(1)}, u32[]{:S(2)}, u32[]{:S(2)}) collective-permute-start(bf16[32,1536]{1,0:T(8,128)(2,1)S(1)} %get-tuple-element.68), channel_id=1, source_target_pairs={{0,8},{4,12},{8,16},{12,20},{16,24},{20,28},{24,0},{28,4},{32,40},... | collective-permute-start | bytes 294920 | tf_op jit(solution)/shard_map/ppermute | solution.py:397
  59.8 2.1 %collective-permute-start.14 = (bf16[32,1536]{1,0:T(8,128)(2,1)S(1)}, bf16[32,1536]{1,0:T(8,128)(2,1)S(1)}, u32[]{:S(2)}, u32[]{:S(2)}) collective-permute-start(bf16[32,1536]{1,0:T(8,128)(2,1)S(1)} %get-tuple-element.69), channel_id=1, source_target_pairs={{0,16},{4,20},{8,24},{12,28},{16,0},{20,4},{24,8},{28,12},{32,48},... | collective-permute-start | bytes 294920 | tf_op jit(solution)/shard_map/ppermute | solution.py:397
  63.2 1.8 %collective-permute-done.14.refs_2_ = bf16[32,1536]{1,0:T(8,128)(2,1)S(1)} collective-permute-done((bf16[32,1536]{1,0:T(8,128)(2,1)S(1)}, bf16[32,1536]{1,0:T(8,128)(2,1)S(1)}, u32[]{:S(2)}, u32[]{:S(2)}) %collective-permute-start.14) | collective-permute-done | bytes 98336 | tf_op jit(solution)/shard_map/ppermute | solution.py:397
  65.8 3.3 %collective-permute-start.16 = (bf16[128,1536]{1,0:T(8,128)(2,1)S(1)}, bf16[128,1536]{1,0:T(8,128)(2,1)S(1)}, u32[]{:S(2)}, u32[]{:S(2)}) collective-permute-start(bf16[128,1536]{1,0:T(8,128)(2,1)S(1)} %shard_map.86), channel_id=1, source_target_pairs={{0,4},{4,0},{8,12},{12,8},{16,20},{20,16},{24,28},{28,24},{32,36},... | collective-permute-start | bytes 1179656 | tf_op jit(solution)/shard_map/ppermute | solution.py:399
  (48 shorter events, 11.4 us)
Async XLA Ops:
  0.0 6.0 %copy-start.3 = (s32[1,2]{1,0:T(1,128)S(1)}, s32[1,2]{1,0:T(1,128)}, u32[]{:S(2)}) copy-start(s32[1,2]{1,0:T(1,128)} %times.1) | copy-start | bytes 28
  1.2 15.4 %collective-permute-start = (bf16[128,1664]{1,0:T(8,128)(2,1)S(1)}, bf16[128,1664]{1,0:T(8,128)(2,1)S(1)}, u32[]{:S(2)}, u32[]{:S(2)}) collective-permute-start(bf16[128,1664]{1,0:T(8,128)(2,1)S(1)} %get-tuple-element.38.first.refs_0_), channel_id=1, source_target_pairs={{0,1},{1,2},{2,3},{3,0},{4,5},{5,6},{6,7},{7,4},{8,9},{9,10},{10,1... | collective-permute-start | bytes 1277960 | tf_op jit(solution)/shard_map/ppermute | solution.py:408
  3.7 8.5 %slice-start = ((s8[14155776]{0:T(1024)(128)(4,1)}), s8[4194304]{0:T(1024)(128)(4,1)S(1)}, s32[]{:S(2)}) async-start(s8[14155776]{0:T(1024)(128)(4,1)} %bitcast.3), calls=%async_computation | async-start | bytes 8388608
  3.7 8.5 %slice-start.1 = ((s8[14155776]{0:T(1024)(128)(4,1)}), s8[4194304]{0:T(1024)(128)(4,1)S(1)}, s32[]{:S(2)}) async-start(s8[14155776]{0:T(1024)(128)(4,1)} %bitcast.3), calls=%async_computation.1 | async-start | bytes 8388608
  3.7 8.5 %slice-start.2 = ((s8[14155776]{0:T(1024)(128)(4,1)}), s8[4194304]{0:T(1024)(128)(4,1)S(1)}, s32[]{:S(2)}) async-start(s8[14155776]{0:T(1024)(128)(4,1)} %bitcast.3), calls=%async_computation.2 | async-start | bytes 8388608
  3.7 8.5 %slice-start.3 = ((s8[14155776]{0:T(1024)(128)(4,1)}), s8[1572864]{0:T(1024)(128)(4,1)S(1)}, s32[]{:S(2)}) async-start(s8[14155776]{0:T(1024)(128)(4,1)} %bitcast.3), calls=%async_computation.3 | async-start | bytes 3145728
  3.7 8.5 %copy-start.1 = (f32[2,1536]{1,0:T(2,128)S(1)}, f32[2,1536]{1,0:T(2,128)}, u32[]{:S(2)}) copy-start(f32[2,1536]{1,0:T(2,128)} %refs_4_.5) | copy-start | bytes 36868
  3.7 12.9 %collective-permute-start.2 = (bf16[128,1664]{1,0:T(8,128)(2,1)S(1)}, bf16[128,1664]{1,0:T(8,128)(2,1)S(1)}, u32[]{:S(2)}, u32[]{:S(2)}) collective-permute-start(bf16[128,1664]{1,0:T(8,128)(2,1)S(1)} %get-tuple-element.39.second.refs_1_), channel_id=1, source_target_pairs={{0,3},{1,0},{2,1},{3,2},{4,7},{5,4},{6,5},{7,6},{8,11},{9,8},{10,9... | collective-permute-start | bytes 1277960 | tf_op jit(solution)/shard_map/ppermute | solution.py:409
  9.4 16.9 %collective-permute-start.4 = (bf16[128,1536]{1,0:T(8,128)(2,1)S(1)}, bf16[128,1536]{1,0:T(8,128)(2,1)S(1)}, u32[]{:S(2)}, u32[]{:S(2)}) collective-permute-start(bf16[128,1536]{1,0:T(8,128)(2,1)S(1)} %get-tuple-element.46), channel_id=1, source_target_pairs={{0,1},{1,2},{2,3},{3,0},{4,5},{5,6},{6,7},{7,4},{8,9},{9,10},{10,1... | collective-permute-start | bytes 1179656 | tf_op jit(solution)/shard_map/ppermute | solution.py:408
  9.5 16.8 %collective-permute-start.5 = (bf16[128,1536]{1,0:T(8,128)(2,1)S(1)}, bf16[128,1536]{1,0:T(8,128)(2,1)S(1)}, u32[]{:S(2)}, u32[]{:S(2)}) collective-permute-start(bf16[128,1536]{1,0:T(8,128)(2,1)S(1)} %get-tuple-element.47), channel_id=1, source_target_pairs={{0,3},{1,0},{2,1},{3,2},{4,7},{5,4},{6,5},{7,6},{8,11},{9,8},{10,9... | collective-permute-start | bytes 1179656 | tf_op jit(solution)/shard_map/ppermute | solution.py:409
  16.6 16.3 %collective-permute-start.1 = (bf16[128,1664]{1,0:T(8,128)(2,1)S(1)}, bf16[128,1664]{1,0:T(8,128)(2,1)S(1)}, u32[]{:S(2)}, u32[]{:S(2)}) collective-permute-start(bf16[128,1664]{1,0:T(8,128)(2,1)S(1)} %collective-permute-done.refs_2_.refs_0_), channel_id=1, source_target_pairs={{0,1},{1,2},{2,3},{3,0},{4,5},{5,6},{6,7},{7,4},{8,9},{9,10},{10,1... | collective-permute-start | bytes 1277960 | tf_op jit(solution)/shard_map/ppermute | solution.py:408
  16.7 16.2 %collective-permute-start.3 = (bf16[128,1664]{1,0:T(8,128)(2,1)S(1)}, bf16[128,1664]{1,0:T(8,128)(2,1)S(1)}, u32[]{:S(2)}, u32[]{:S(2)}) collective-permute-start(bf16[128,1664]{1,0:T(8,128)(2,1)S(1)} %collective-permute-done.2.refs_3_.refs_1_), channel_id=1, source_target_pairs={{0,3},{1,0},{2,1},{3,2},{4,7},{5,4},{6,5},{7,6},{8,11},{9,8},{10,9... | collective-permute-start | bytes 1277960 | tf_op jit(solution)/shard_map/ppermute | solution.py:409
  29.5 6.8 %slice-start.4 = ((s8[4718592]{0:T(1024)(128)(4,1)}), s8[4194304]{0:T(1024)(128)(4,1)S(1)}, s32[]{:S(2)}) async-start(s8[4718592]{0:T(1024)(128)(4,1)} %bitcast.5), calls=%async_computation.4 | async-start | bytes 8388608
  38.2 3.2 %collective-permute-start.6 = (bf16[128,1536]{1,0:T(8,128)(2,1)S(1)}, bf16[128,1536]{1,0:T(8,128)(2,1)S(1)}, u32[]{:S(2)}, u32[]{:S(2)}) collective-permute-start(bf16[128,1536]{1,0:T(8,128)(2,1)S(1)} %get-tuple-element.62), channel_id=1, source_target_pairs={{0,4},{4,0},{8,12},{12,8},{16,20},{20,16},{24,28},{28,24},{32,36},... | collective-permute-start | bytes 1179656 | tf_op jit(solution)/shard_map/ppermute | solution.py:391
  41.5 5.7 %collective-permute-start.7 = (bf16[32,1536]{1,0:T(8,128)(2,1)S(1)}, bf16[32,1536]{1,0:T(8,128)(2,1)S(1)}, u32[]{:S(2)}, u32[]{:S(2)}) collective-permute-start(bf16[32,1536]{1,0:T(8,128)(2,1)S(1)} %get-tuple-element.64), channel_id=1, source_target_pairs={{0,8},{4,12},{8,16},{12,20},{16,24},{20,28},{24,0},{28,4},{32,40},... | collective-permute-start | bytes 294920 | tf_op jit(solution)/shard_map/ppermute | solution.py:393
  42.8 7.5 %collective-permute-start.8 = (bf16[32,1536]{1,0:T(8,128)(2,1)S(1)}, bf16[32,1536]{1,0:T(8,128)(2,1)S(1)}, u32[]{:S(2)}, u32[]{:S(2)}) collective-permute-start(bf16[32,1536]{1,0:T(8,128)(2,1)S(1)} %get-tuple-element.65), channel_id=1, source_target_pairs={{0,16},{4,20},{8,24},{12,28},{16,0},{20,4},{24,8},{28,12},{32,48},... | collective-permute-start | bytes 294920 | tf_op jit(solution)/shard_map/ppermute | solution.py:393
  45.2 5.1 %collective-permute-start.9 = (bf16[32,1536]{1,0:T(8,128)(2,1)S(1)}, bf16[32,1536]{1,0:T(8,128)(2,1)S(1)}, u32[]{:S(2)}, u32[]{:S(2)}) collective-permute-start(bf16[32,1536]{1,0:T(8,128)(2,1)S(1)} %get-tuple-element.66), channel_id=1, source_target_pairs={{0,24},{4,28},{8,0},{12,4},{16,8},{20,12},{24,16},{28,20},{32,56},... | collective-permute-start | bytes 294920 | tf_op jit(solution)/shard_map/ppermute | solution.py:393
  50.3 5.1 %collective-permute-start.10 = (bf16[32,1536]{1,0:T(8,128)(2,1)S(1)}, bf16[32,1536]{1,0:T(8,128)(2,1)S(1)}, u32[]{:S(2)}, u32[]{:S(2)}) collective-permute-start(bf16[32,1536]{1,0:T(8,128)(2,1)S(1)} %shard_map.84), channel_id=1, source_target_pairs={{0,32},{4,36},{8,40},{12,44},{16,48},{20,52},{24,56},{28,60},{32,6... | collective-permute-start | bytes 294920 | tf_op jit(solution)/shard_map/ppermute | solution.py:395
  51.7 6.5 %collective-permute-start.11 = (bf16[32,1536]{1,0:T(8,128)(2,1)S(1)}, bf16[32,1536]{1,0:T(8,128)(2,1)S(1)}, u32[]{:S(2)}, u32[]{:S(2)}) collective-permute-start(bf16[32,1536]{1,0:T(8,128)(2,1)S(1)} %shard_map.84), channel_id=1, source_target_pairs={{0,64},{4,68},{8,72},{12,76},{16,80},{20,84},{24,88},{28,92},{32,9... | collective-permute-start | bytes 294920 | tf_op jit(solution)/shard_map/ppermute | solution.py:395
  54.3 3.9 %collective-permute-start.12 = (bf16[32,1536]{1,0:T(8,128)(2,1)S(1)}, bf16[32,1536]{1,0:T(8,128)(2,1)S(1)}, u32[]{:S(2)}, u32[]{:S(2)}) collective-permute-start(bf16[32,1536]{1,0:T(8,128)(2,1)S(1)} %shard_map.84), channel_id=1, source_target_pairs={{0,96},{4,100},{8,104},{12,108},{16,112},{20,116},{24,120},{28,124... | collective-permute-start | bytes 294920 | tf_op jit(solution)/shard_map/ppermute | solution.py:395
  58.4 4.8 %collective-permute-start.13 = (bf16[32,1536]{1,0:T(8,128)(2,1)S(1)}, bf16[32,1536]{1,0:T(8,128)(2,1)S(1)}, u32[]{:S(2)}, u32[]{:S(2)}) collective-permute-start(bf16[32,1536]{1,0:T(8,128)(2,1)S(1)} %get-tuple-element.68), channel_id=1, source_target_pairs={{0,8},{4,12},{8,16},{12,20},{16,24},{20,28},{24,0},{28,4},{32,40},... | collective-permute-start | bytes 294920 | tf_op jit(solution)/shard_map/ppermute | solution.py:397
  59.8 5.2 %collective-permute-start.14 = (bf16[32,1536]{1,0:T(8,128)(2,1)S(1)}, bf16[32,1536]{1,0:T(8,128)(2,1)S(1)}, u32[]{:S(2)}, u32[]{:S(2)}) collective-permute-start(bf16[32,1536]{1,0:T(8,128)(2,1)S(1)} %get-tuple-element.69), channel_id=1, source_target_pairs={{0,16},{4,20},{8,24},{12,28},{16,0},{20,4},{24,8},{28,12},{32,48},... | collective-permute-start | bytes 294920 | tf_op jit(solution)/shard_map/ppermute | solution.py:397
  61.9 3.8 %collective-permute-start.15 = (bf16[32,1536]{1,0:T(8,128)(2,1)S(1)}, bf16[32,1536]{1,0:T(8,128)(2,1)S(1)}, u32[]{:S(2)}, u32[]{:S(2)}) collective-permute-start(bf16[32,1536]{1,0:T(8,128)(2,1)S(1)} %get-tuple-element.70), channel_id=1, source_target_pairs={{0,24},{4,28},{8,0},{12,4},{16,8},{20,12},{24,16},{28,20},{32,56},... | collective-permute-start | bytes 294920 | tf_op jit(solution)/shard_map/ppermute | solution.py:397
  65.8 4.6 %collective-permute-start.16 = (bf16[128,1536]{1,0:T(8,128)(2,1)S(1)}, bf16[128,1536]{1,0:T(8,128)(2,1)S(1)}, u32[]{:S(2)}, u32[]{:S(2)}) collective-permute-start(bf16[128,1536]{1,0:T(8,128)(2,1)S(1)} %shard_map.86), channel_id=1, source_target_pairs={{0,4},{4,0},{8,12},{12,8},{16,20},{20,16},{24,28},{28,24},{32,36},... | collective-permute-start | bytes 1179656 | tf_op jit(solution)/shard_map/ppermute | solution.py:399
  (3 other events, 12.4 us)
